TPU v7x, 32 devices: a whole 2x2x4 slice. The times are simulated.
32 devices in a mesh: dp: 8 (over z, core), expert: 4 (over y, x).
Axes of the slice: x: 2, y: 2, z: 4, core: 2. Of those that a mesh axis runs over, the one named last changes fastest.
Arguments:
- grad_out: bfloat16 [4096, 2048], P(('dp', 'expert')), may hold values from -6 to 6
- expert_ids: int32 [4096, 8], P(('dp', 'expert')), may hold values from 0 to 15, all different within a row; in each aligned block of 128 rows (0 to 127, 128 to 255, ...) at most 96 rows name the same one
- gate_weights: bfloat16 [4096, 8], P(('dp', 'expert')), may hold values from 0.019897461 to 0.5
- saved_hidden: bfloat16 [4, 3072, 768], P('expert', 'dp'), may hold values from -0.29882812 to 0.29882812
- down_weight: bfloat16 [4, 768, 2048], P('expert'), may hold values from -0.21875 to 0.21875
Outputs:
- hidden_grad: bfloat16 [4, 3072, 768], P('expert', 'dp')
- gate_grad: float32 [4096, 8], P(('dp', 'expert'))
- weight_grad: float32 [4, 2048, 768], P('expert', 'dp')
Inputs may be any that keep to these rules, and one draw needn't show every extreme that they name: `expert_ids`: each row names 8 different experts; in the rows of one device (aligned blocks of 128 rows) no expert is named by more than 96 rows.
All inputs are finite; a program needn't handle non-finite values.
Results may differ from a plain program's by a relative error of at most 0.0029.
Values may be sent and summed in bfloat16 or wider, within the bound.
No kernel may reach another device: no remote copies, remote signals or barrier semaphores. Data moves between devices by JAX's collectives and lax.ppermute only.
A program may use at most 64 MiB of HBM per device.

v0:
```python
import jax
import jax.numpy as jnp
from jax import lax
from jax.sharding import PartitionSpec as P

TOP = 8
EXP_DEV = 4


def per_device(grad_out, expert_ids, gate_weights, saved_hidden, down_weight):
    peer_count = lax.axis_size("expert")
    tok_rows = grad_out.shape[0]
    capacity = saved_hidden.shape[1] // peer_count
    slot_total = peer_count * capacity
    flat_ids = expert_ids.reshape(-1)
    flight = flat_ids % EXP_DEV == 0
    target = flat_ids // EXP_DEV
    onehot = (
        (target[:, None] == jnp.arange(peer_count, dtype=jnp.int32)[None, :]) & flight[:, None]
    ).astype(jnp.int32)
    slot_rank = jnp.cumsum(onehot, axis=0) - 1
    slot_index = jnp.sum(slot_rank * onehot, axis=1)
    slot_place = jnp.where(flight, target * capacity + slot_index, slot_total)
    slot_match = slot_place[None, :] == jnp.arange(slot_total, dtype=jnp.int32)[:, None]
    gates_flat = gate_weights.astype(jnp.float32).reshape(-1)
    send_gates = jnp.sum(jnp.where(slot_match, gates_flat[None, :], 0.0), axis=1).astype(
        jnp.bfloat16
    )
    token_match = jnp.any(slot_match.reshape(slot_total, tok_rows, TOP), axis=2).astype(
        jnp.bfloat16
    )
    send_rows = jnp.dot(token_match, grad_out, preferred_element_type=jnp.float32).astype(
        jnp.bfloat16
    )
    rows_in, gates_in = (
        lax.all_to_all(
            send_rows.reshape(peer_count, capacity, -1),
            "expert",
            split_axis=0,
            concat_axis=0,
            tiled=True,
        ),
        lax.all_to_all(
            send_gates.reshape(peer_count, capacity),
            "expert",
            split_axis=0,
            concat_axis=0,
            tiled=True,
        ),
    )
    slot_rows = rows_in.reshape(slot_total, -1)
    slot_gates = gates_in.reshape(slot_total).astype(jnp.float32)
    hidden = saved_hidden[0]
    weight = down_weight[0]
    update = lax.dot_general(
        slot_rows, weight, (((1,), (1,)), ((), ())), preferred_element_type=jnp.float32
    )
    grad_hidden = (slot_gates[:, None] * update).astype(jnp.bfloat16)
    pair_grad = jnp.sum(hidden.astype(jnp.float32) * update, axis=1)
    returned = lax.all_to_all(
        pair_grad.reshape(peer_count, capacity), "expert", split_axis=0, concat_axis=0, tiled=True
    )
    gate_flat = jnp.sum(jnp.where(slot_match, returned.reshape(slot_total)[:, None], 0.0), axis=0)
    gate_grad = gate_flat.reshape(tok_rows, TOP)
    scaled = (slot_gates[:, None] * hidden.astype(jnp.float32)).astype(jnp.bfloat16)
    grad_term = lax.dot_general(
        slot_rows, scaled, (((0,), (0,)), ((), ())), preferred_element_type=jnp.float32
    )
    weight_shard = lax.psum_scatter(grad_term, "dp", scatter_dimension=0, tiled=True)
    return (grad_hidden[None], gate_grad, weight_shard[None])


def solution(mesh):
    placed = (
        P(("dp", "expert"), None),
        P(("dp", "expert"), None),
        P(("dp", "expert"), None),
        P("expert", "dp", None),
        P("expert", None, None),
    )
    return jax.shard_map(
        per_device,
        mesh=mesh,
        in_specs=placed,
        out_specs=(P("expert", "dp", None), P(("dp", "expert"), None), P("expert", "dp", None)),
        check_vma=False,
    )
```

profile of v0, /device:TPU:0, one launch (start us, length us, event | category | flops | bytes accessed | tf_op | source)
XLA Modules:
  0.0 139.6 jit_solution(1043433313644562587)
XLA Ops:
  7.2 0.9 copy.26
  8.1 0.1 reshape.205
  8.2 0.1 reshape.206
  8.4 1.1 reduce-window.6
  9.5 0.2 slice_reduce_fusion
  9.7 0.2 reduce-window.9
  10.3 0.6 fusion.2
  10.8 1.6 %convolution_convert_fusion = bf16[384,2048]{1,0:T(8,128)(2,1)S(1)} fusion(pred[384,128]{1,0:T(8,128)(4,1)S(1)} %fusion.2, bf16[128,2048]{1,0:T(8,128)(2,1)} %param.5), kind=kOutput, calls=%fused_computation.2 | convolution fusion | flops 202113024 | bytes 2146304 | tf_op jit(solution)/shard_map/dot_general | solution.py:32
  12.5 24.9 %all_to_all.20 = bf16[4,96,2048]{2,1,0:T(8,128)(2,1)S(1)} all-to-all(bf16[4,96,2048]{2,1,0:T(8,128)(2,1)S(1)} %bitcast.40), channel_id=1, replica_groups=mesh['dp'=8,'expert'=4] {'expert'}, dimensions={0} | all-to-all | bytes 3145728 | tf_op jit(solution)/shard_map/all_to_all | solution.py:36
  37.3 2.6 %fusion.4 = (f32[384]{0:T(512)S(1)}, f32[384,768]{1,0:T(8,128)}) fusion(bf16[1,384,768]{2,1,0:T(8,128)(2,1)S(1)} %copy-done.2, bf16[384,2048]{1,0:T(8,128)(2,1)S(1)} %bitcast.38, bf16[1,768,2048]{2,1,0:T(8,128)(2,1)S(1)} %copy-done), kind=kOutput, calls=%fused_computation.11 | convolution fusion | flops 1208843904 | bytes 6489600 | tf_op jit(solution)/shard_map/dot_general | solution.py:55
  40.0 0.7 all_to_all.15
  40.6 3.2 %all-to-all-start.2 = ((f32[4,1,96]{2,1,0:T(1,128)}), f32[4,1,96]{2,1,0:T(1,128)S(1)}, u32[]{:S(2)}, u32[]{:S(2)}) async-start(f32[4,1,96]{2,1,0:T(1,128)} %all_to_all.15), calls=%async_computation.2 | async-start | bytes 4096 | tf_op jit(solution)/shard_map/all_to_all | solution.py:60
  43.9 0.1 copy.28
  44.0 0.1 reshape.211
  44.1 4.3 %all-to-all-done.2 = f32[4,1,96]{2,1,0:T(1,128)S(1)} async-done(((f32[4,1,96]{2,1,0:T(1,128)}), f32[4,1,96]{2,1,0:T(1,128)S(1)}, u32[]{:S(2)}, u32[]{:S(2)}) %all-to-all-start.2) | async-done | bytes 1568 | tf_op jit(solution)/shard_map/all_to_all | solution.py:60
  48.4 0.5 broadcast.216
  48.9 0.7 reduce.9
  49.7 0.4 select_reduce_fusion
  50.1 0.1 convert_element_type.67
  50.2 7.0 %all_to_all.21 = bf16[4,1,96]{2,1,0:T(2,128)(2,1)S(1)} all-to-all(bf16[4,1,96]{2,1,0:T(2,128)(2,1)S(1)} %convert_element_type.67), channel_id=1, replica_groups=mesh['dp'=8,'expert'=4] {'expert'}, dimensions={0} | all-to-all | bytes 1536 | tf_op jit(solution)/shard_map/all_to_all | solution.py:43
  57.3 6.1 %fusion.8 = f32[2048,768]{1,0:T(8,128)} fusion(bf16[384,2048]{1,0:T(8,128)(2,1)} %bitcast.39, bf16[1,384,768]{2,1,0:T(8,128)(2,1)} %param.8, f32[384]{0:T(512)S(1)} %reshape.212), kind=kOutput, calls=%fused_computation.16 | convolution fusion | flops 1208844288 | bytes 8455680 | tf_op jit(solution)/shard_map/dot_general | solution.py:66
  63.5 0.7 copy.35
  64.2 2.2 %fusion.6 = bf16[1,384,768]{2,1,0:T(8,128)(2,1)} fusion(f32[384,768]{1,0:T(8,128)} %get-tuple-element.15, f32[384]{0:T(512)S(1)} %reshape.212), kind=kLoop, calls=%fused_computation.14 | loop fusion | flops 589824 | bytes 1771008 | tf_op jit(solution)/shard_map/broadcast_in_dim | solution.py:70
  66.4 66.4 %reduce-scatter.2.cloned.1.call-done = f32[256,768]{1,0:T(8,128)} async-done(((f32[2048,768]{1,0:T(8,128)}), f32[256,768]{1,0:T(8,128)}) %reduce-scatter.2.cloned.1.call-update) | async-done | bytes 786448 | tf_op jit(solution)/shard_map/reduce_scatter | solution.py:69
  (25 shorter events, 0.7 us)
Async XLA Ops:
  7.2 30.2 %copy-start = (bf16[1,768,2048]{2,1,0:T(8,128)(2,1)S(1)}, bf16[1,768,2048]{2,1,0:T(8,128)(2,1)}, u32[]{:S(2)}) copy-start(bf16[1,768,2048]{2,1,0:T(8,128)(2,1)} %param.9) | copy-start | bytes 9437188
  12.4 24.9 %copy-start.2 = (bf16[1,384,768]{2,1,0:T(8,128)(2,1)S(1)}, bf16[1,384,768]{2,1,0:T(8,128)(2,1)}, u32[]{:S(2)}) copy-start(bf16[1,384,768]{2,1,0:T(8,128)(2,1)} %param.8) | copy-start | bytes 1769476
  37.3 2.7 %copy-start.1 = (bf16[4,96,2048]{2,1,0:T(8,128)(2,1)}, bf16[4,96,2048]{2,1,0:T(8,128)(2,1)S(1)}, u32[]{:S(2)}) copy-start(bf16[4,96,2048]{2,1,0:T(8,128)(2,1)S(1)} %all_to_all.20) | copy-start | bytes 4718596
  37.3 6.6 %copy-start.3 = (bf16[128,8]{0,1:T(8,128)(2,1)S(1)}, bf16[128,8]{0,1:T(8,128)(2,1)}, u32[]{:S(2)}) copy-start(bf16[128,8]{0,1:T(8,128)(2,1)} %param.7) | copy-start | bytes 6148
  40.6 7.8 %all-to-all-start.2 = ((f32[4,1,96]{2,1,0:T(1,128)}), f32[4,1,96]{2,1,0:T(1,128)S(1)}, u32[]{:S(2)}, u32[]{:S(2)}) async-start(f32[4,1,96]{2,1,0:T(1,128)} %all_to_all.15), calls=%async_computation.2 | async-start | bytes 4096 | tf_op jit(solution)/shard_map/all_to_all | solution.py:60
  43.9 88.9 %reduce-scatter.2.cloned.1.call-start = ((), (), s32[]{:S(2)}) async-start(), calls=%async_computation.4 | async-start | bytes 7077888 | tf_op jit(solution)/shard_map/reduce_scatter | solution.py:69
Sparse Core Ops, SparseCore 0:
  63.5 69.1 reduce-scatter.1
where the time goes:
time: 140 us
  waiting for transfers between devices  70.6 us (50%)
  blocking collectives  31.8 us (23%)
  between operations  14.2 us (10%)
  matrix products  10.3 us (7%)
  other arithmetic  5.49 us (4%)
  local copies, waits for them, and re-layouts  3.86 us (3%)
  starting transfers between devices  3.26 us (2%)
    reduce_scatter x1, waiting for transfers between devices, per_device(): lax.psum_scatter(grad_term, 'dp', scatter_dimension=0, tiled=True)  66.4 us
    all_to_all x1, blocking collectives, per_device(): lax.all_to_all(send_rows.reshape(peer_count, capacity, -1), 'expert', spl...  24.9 us
    all_to_all x1, blocking collectives, per_device(): lax.all_to_all(send_gates.reshape(peer_count, capacity), 'expert', split_...  6.98 us
    dot_general x1, matrix products, per_device(): lax.dot_general(slot_rows, scaled, (((0,), (0,)), ((), ())), preferred_el...  6.1 us
    all_to_all x1, waiting for transfers between devices, per_device(): lax.all_to_all(pair_grad.reshape(peer_count, capacity), 'expert', split_a...  4.26 us
    all_to_all x1, starting transfers between devices, per_device(): lax.all_to_all(pair_grad.reshape(peer_count, capacity), 'expert', split_a...  3.22 us
  transfers between devices with their start and end apart: 2, of which 2 were waited for; matrix products, arithmetic and copies ran while one was open for 2% of the time, Pallas kernels for 0%

commit v1 on v0

v1 whole, which is shorter than its diff:
```python
import functools

import jax
import jax.numpy as jnp
from jax import lax
from jax.experimental import pallas as pl
from jax.experimental.pallas import tpu as pltpu
from jax.sharding import PartitionSpec as P

TOP = 8
EXP_DEV = 4
F32 = jnp.float32
BF16 = jnp.bfloat16
GATE_LANES = 128


def per_device_general(grad_out, expert_ids, gate_weights, saved_hidden, down_weight):
    peer_count = lax.axis_size("expert")
    tok_rows = grad_out.shape[0]
    capacity = saved_hidden.shape[1] // peer_count
    slot_total = peer_count * capacity
    flat_ids = expert_ids.reshape(-1)
    flight = flat_ids % EXP_DEV == 0
    target = flat_ids // EXP_DEV
    onehot = (
        (target[:, None] == jnp.arange(peer_count, dtype=jnp.int32)[None, :]) & flight[:, None]
    ).astype(jnp.int32)
    slot_rank = jnp.cumsum(onehot, axis=0) - 1
    slot_index = jnp.sum(slot_rank * onehot, axis=1)
    slot_place = jnp.where(flight, target * capacity + slot_index, slot_total)
    slot_match = slot_place[None, :] == jnp.arange(slot_total, dtype=jnp.int32)[:, None]
    gates_flat = gate_weights.astype(F32).reshape(-1)
    send_gates = jnp.sum(jnp.where(slot_match, gates_flat[None, :], 0.0), axis=1).astype(BF16)
    token_match = jnp.any(slot_match.reshape(slot_total, tok_rows, TOP), axis=2).astype(BF16)
    send_rows = jnp.dot(token_match, grad_out, preferred_element_type=F32).astype(BF16)
    exchange = functools.partial(
        lax.all_to_all, axis_name="expert", split_axis=0, concat_axis=0, tiled=True
    )
    rows_in = exchange(send_rows.reshape(peer_count, capacity, -1))
    gates_in = exchange(send_gates.reshape(peer_count, capacity))
    slot_rows = rows_in.reshape(slot_total, -1)
    slot_gates = gates_in.reshape(slot_total).astype(F32)
    hidden = saved_hidden[0]
    weight = down_weight[0]
    update = lax.dot_general(
        slot_rows, weight, (((1,), (1,)), ((), ())), preferred_element_type=F32
    )
    grad_hidden = (slot_gates[:, None] * update).astype(BF16)
    pair_grad = jnp.sum(hidden.astype(F32) * update, axis=1)
    returned = exchange(pair_grad.reshape(peer_count, capacity))
    gate_flat = jnp.sum(jnp.where(slot_match, returned.reshape(slot_total)[:, None], 0.0), axis=0)
    gate_grad = gate_flat.reshape(tok_rows, TOP)
    scaled = (slot_gates[:, None] * hidden.astype(F32)).astype(BF16)
    grad_term = lax.dot_general(
        slot_rows, scaled, (((0,), (0,)), ((), ())), preferred_element_type=F32
    )
    weight_shard = lax.psum_scatter(grad_term, "dp", scatter_dimension=0, tiled=True)
    return (grad_hidden[None], gate_grad, weight_shard[None])


def coordinates():
    group = lax.axis_index("dp")
    return group // 2, group % 2, lax.axis_index("expert")


def dot(a, b, dims):
    return lax.dot_general(a, b, (dims, ((), ())), preferred_element_type=F32)


def swap_kernel(block, ids_ref, gates_ref, grad_ref, send_ref, marks_ref):
    _, core, _ = coordinates()
    tokens = grad_ref.shape[0]
    ids = ids_ref[...]
    gates = gates_ref[...].astype(F32)
    experts = ids.shape[0] // 2
    marks_ref[...] = jnp.full(marks_ref.shape, -1.0, BF16)
    rows = []
    for j in range(experts):
        hit = ids == j * EXP_DEV
        value = jnp.sum(jnp.where(hit, gates, 0.0), axis=0, keepdims=True)
        live = jnp.sum(jnp.where(hit, 1.0, 0.0), axis=0, keepdims=True)
        rows.append(jnp.where(live > 0.0, value, -1.0))
    rows.append(jnp.full((marks_ref.shape[0] - experts, tokens), -1.0, F32))
    marks = jnp.concatenate(rows, axis=0).astype(BF16)
    marks_ref[...] = marks
    for i in range(send_ref.shape[1] // block):
        start = pl.multiple_of((2 * i + 1 - core) * block, block)
        send_ref[:tokens, i * block : (i + 1) * block] = grad_ref[:, pl.ds(start, block)]
    send_ref[tokens:, :] = jnp.zeros((16, send_ref.shape[1]), BF16)
    send_ref[tokens:, :tokens] = marks


def gather_kernel(block, capacity, grad_ref, marks_ref, other_ref, *outs):
    _first, matches_ref = outs[:-2], outs[-2]
    scratch = outs[-1]
    chip, core, peer = coordinates()
    tokens = grad_ref.shape[0]
    chunk = chip ^ 3
    before = (
        lax.broadcasted_iota(jnp.int32, (tokens, tokens), 0)
        < lax.broadcasted_iota(jnp.int32, (tokens, tokens), 1)
    ).astype(F32).astype(BF16)
    slot = lax.broadcasted_iota(jnp.int32, (capacity, tokens), 0).astype(F32)
    own = grad_ref[:, pl.ds(pl.multiple_of((2 * chunk + core) * block, block), block)]
    other = other_ref[:tokens, pl.ds(pl.multiple_of(chunk * block, block), block)]
    for g in range(2):
        marks = (marks_ref[...] if g == 0 else other_ref[tokens:, :tokens]).astype(F32)
        live = jnp.where(marks >= 0.0, 1.0, 0.0)
        rank = dot(live.astype(BF16), before, ((1,), (0,)))
        scratch[2 * g] = marks
        scratch[2 * g + 1] = jnp.where(marks >= 0.0, rank, -1.0)
        rows = own if g == 0 else other
        for r in range(4):
            e = peer ^ r
            gate = scratch[2 * g, pl.ds(e, 1), :]
            place = scratch[2 * g + 1, pl.ds(e, 1), :]
            match = slot == place
            matchb = jnp.where(match, 1.0, 0.0).astype(BF16)
            matches_ref[g, r] = matchb
            column = jnp.sum(jnp.where(match, gate, 0.0), axis=1, keepdims=True)
            at = slice(g * capacity, (g + 1) * capacity)
            _first[r][at, :block] = dot(matchb, rows, ((1,), (0,))).astype(BF16)
            _first[r][at, block:] = jnp.broadcast_to(column, (capacity, GATE_LANES)).astype(BF16)


def rest_kernel(block, capacity, grad_ref, other_ref, matches_ref, *outs):
    chip, core, _ = coordinates()
    tokens = grad_ref.shape[0]
    for k in range(1, 4):
        chunk = chip ^ (3 - k)
        own = grad_ref[:, pl.ds(pl.multiple_of((2 * chunk + core) * block, block), block)]
        other = other_ref[:tokens, pl.ds(pl.multiple_of(chunk * block, block), block)]
        to = slice(0, block) if k < 3 else slice(block, 2 * block)
        for g in range(2):
            for r in range(4):
                out = outs[r if k == 1 else 4 + r]
                out[g * capacity : (g + 1) * capacity, to] = dot(
                    matches_ref[g, r], own if g == 0 else other, ((1,), (0,))
                ).astype(BF16)


def first_kernel(block, capacity, p0, p1, p2, p3, hidden_ref, other_ref, part_ref, scaled_ref, rows_ref):
    _, _, peer = coordinates()
    for r, piece in enumerate((p0, p1, p2, p3)):
        source = pl.ds(pl.multiple_of((peer ^ r) * capacity, 32), capacity)
        for g, hidden in enumerate((hidden_ref, other_ref)):
            at = slice((2 * r + g) * capacity, (2 * r + g + 1) * capacity)
            gate = piece[g * capacity : (g + 1) * capacity, block : block + 1].astype(F32)
            scaled_ref[at, :] = (gate * hidden[source, :].astype(F32)).astype(BF16)
            rows_ref[at, :] = piece[g * capacity : (g + 1) * capacity, :block]
    part_ref[...] = dot(rows_ref[...], scaled_ref[...], ((0,), (0,))).astype(part_ref.dtype)


def part_kernel(p0, p1, p2, p3, scaled_ref, *outs):
    *parts, rows_ref = outs
    size = p0.shape[0]
    for r, piece in enumerate((p0, p1, p2, p3)):
        rows_ref[r * size : (r + 1) * size, :] = piece[...]
    block = parts[0].shape[0]
    for i, part in enumerate(parts):
        part[...] = dot(
            rows_ref[:, i * block : (i + 1) * block], scaled_ref[...], ((0,), (0,))
        ).astype(part.dtype)


def update_kernel(block, capacity, rows0, rows1, rows23, weight_ref, own_ref, other_ref):
    chip, core, _ = coordinates()
    total = None
    for k in range(4):
        start = pl.multiple_of((2 * (chip ^ (3 - k)) + core) * block, block)
        rows = (rows0, rows1, rows23, rows23)[k]
        at = slice(block, 2 * block) if k == 3 else slice(0, block)
        term = dot(rows[:, at], weight_ref[:, pl.ds(start, block)], ((1,), (1,)))
        total = term if total is None else total + term
    for r in range(4):
        to = slice(r * capacity, (r + 1) * capacity)
        own_ref[to, :] = total[2 * r * capacity : (2 * r + 1) * capacity, :]
        other_ref[to, :] = total[(2 * r + 1) * capacity : (2 * r + 2) * capacity, :]


def hidden_kernel(block, capacity, own_ref, come_ref, p0, p1, p2, p3, hidden_ref, out_ref, *pairs):
    _, _, peer = coordinates()
    for r, piece in enumerate((p0, p1, p2, p3)):
        at = slice(r * capacity, (r + 1) * capacity)
        source = pl.ds(pl.multiple_of((peer ^ r) * capacity, 32), capacity)
        update = own_ref[at, :] + come_ref[at, :]
        gate = piece[:capacity, block : block + 1].astype(F32)
        out_ref[source, :] = (gate * update).astype(BF16)
        pair = jnp.sum(hidden_ref[source, :].astype(F32) * update, axis=1, keepdims=True)
        pairs[r][...] = jnp.broadcast_to(pair, (capacity, 128))


def gate_kernel(ids_ref, matches_ref, b0, b1, b2, b3, out_ref):
    _, _, peer = coordinates()
    ids = ids_ref[...]
    total = jnp.zeros(ids.shape, F32)
    for r, back in enumerate((b0, b1, b2, b3)):
        at_token = jnp.sum(
            jnp.where(matches_ref[0, r].astype(F32) > 0.0, back[...], 0.0), axis=0, keepdims=True
        )
        total = jnp.where(ids == (peer ^ r) * EXP_DEV, at_token, total)
    out_ref[...] = total


def call(kernel, outs, flops=0, scratch=()):
    size = lambda s: s.size * s.dtype.itemsize
    multiple = isinstance(outs, (list, tuple))
    every = outs if multiple else [outs]

    def run(*args):
        moved = sum(size(a) for a in args) + sum(size(o) for o in every)
        return pl.pallas_call(
            kernel,
            out_shape=outs,
            scratch_shapes=list(scratch),
            compiler_params=pltpu.CompilerParams(vmem_limit_bytes=40 * 2**20),
            cost_estimate=pl.CostEstimate(flops=flops, bytes_accessed=moved, transcendentals=0),
        )(*args)

    return run


def arr(shape, dtype):
    return jax.ShapeDtypeStruct(shape, dtype)


def over(axis, size, mask):
    pairs = [(i, i ^ mask) for i in range(size)]
    return lambda x: lax.ppermute(x, axis, pairs)


def per_device(grad_out, expert_ids, gate_weights, saved_hidden, down_weight):
    groups, peers = lax.axis_size("dp"), lax.axis_size("expert")
    tokens, features = grad_out.shape
    hidden, weight = saved_hidden[0], down_weight[0]
    slots, units = hidden.shape
    capacity = slots // peers
    block = features // groups
    half = features // 2
    core_swap, near, far = (over("dp", groups, m) for m in (1, 2, 4))
    to_peer = [lambda x: x] + [over("expert", peers, r) for r in range(1, peers)]
    ids_t, gates_t = expert_ids.T, gate_weights.T

    send, marks = call(
        functools.partial(swap_kernel, block),
        [arr((tokens + 16, half), BF16), arr((16, tokens), BF16)],
    )(ids_t, gates_t, grad_out)
    other = core_swap(send)
    other_hidden = core_swap(hidden)
    *first, matches = call(
        functools.partial(gather_kernel, block, capacity),
        [arr((2 * capacity, block + GATE_LANES), BF16)] * peers
        + [arr((2, peers, capacity, tokens), BF16)],
        flops=4 * peers * capacity * tokens * block,
        scratch=[pltpu.VMEM((4, 16, tokens), F32)],
    )(grad_out, marks, other)
    first = [to_peer[r](first[r]) for r in range(peers)]
    rest = call(
        functools.partial(rest_kernel, block, capacity),
        [arr((2 * capacity, block), BF16)] * peers + [arr((2 * capacity, 2 * block), BF16)] * peers,
        flops=12 * peers * capacity * tokens * block,
    )(grad_out, other, matches)
    second = [to_peer[r](rest[r]) for r in range(peers)]
    third = [to_peer[r](rest[peers + r]) for r in range(peers)]

    part_flops = 2 * block * 2 * slots * units
    part0, scaled, rows0 = call(
        functools.partial(first_kernel, block, capacity),
        [arr((block, units), BF16), arr((2 * slots, units), BF16), arr((2 * slots, block), BF16)],
        flops=part_flops,
    )(*first, hidden, other_hidden)
    come0 = near(part0)
    part1, rows1 = call(
        part_kernel,
        [arr((block, units), F32), arr((2 * slots, block), BF16)],
        flops=part_flops,
    )(*second, scaled)
    come1 = far((part1 + come0.astype(F32)).astype(BF16))
    part2, part3, rows23 = call(
        part_kernel,
        [arr((block, units), BF16), arr((block, units), F32), arr((2 * slots, 2 * block), BF16)],
        flops=2 * part_flops,
    )(*third, scaled)
    come2 = near(part2)
    mine, theirs = call(
        functools.partial(update_kernel, block, capacity),
        [arr((slots, units), F32)] * 2,
        flops=4 * part_flops,
    )(rows0, rows1, rows23, weight)
    update = core_swap(theirs)
    grad_hidden, *pairs = call(
        functools.partial(hidden_kernel, block, capacity),
        [arr((slots, units), BF16)] + [arr((capacity, 128), F32)] * peers,
    )(mine, update, *first, hidden)
    back = [to_peer[r](pairs[r]) for r in range(peers)]
    gate_grad = call(gate_kernel, arr((TOP, tokens), F32))(ids_t, matches, *back).T
    weight_grad = part3 + come2.astype(F32) + come1.astype(F32)
    return grad_hidden[None], gate_grad, weight_grad[None]


def solution(mesh):
    placed = (
        P(("dp", "expert"), None),
        P(("dp", "expert"), None),
        P(("dp", "expert"), None),
        P("expert", "dp", None),
        P("expert", None, None),
    )
    small = mesh.shape["dp"] == 8 and mesh.shape["expert"] == 4
    return jax.shard_map(
        per_device if small else per_device_general,
        mesh=mesh,
        in_specs=placed,
        out_specs=(P("expert", "dp", None), P(("dp", "expert"), None), P("expert", "dp", None)),
        check_vma=False,
    )
```

time: 140 us -> 70.1 us (0.50)
  waiting for transfers between devices: 70.6 us -> 36.1 us
  blocking collectives: 31.8 us -> 0 us
  starting transfers between devices: 3.26 us -> 21.6 us
  between operations: 14.2 us -> 0.75 us
  matrix products: 10.3 us -> 0 us
  Pallas kernels: 0 us -> 6.27 us
  other arithmetic: 5.49 us -> 1.05 us
    reduce_scatter x1 -> x0, waiting for transfers between devices: 66.4 us -> none  [per_device(): lax.psum_scatter(grad_term, 'dp', scatter_dimension=0, tiled=True)]
    ppermute x0 -> x18, waiting for transfers between devices: none -> 36.1 us  [over(): return lambda x: lax.ppermute(x, axis, pairs)]
    all_to_all x2 -> x0, blocking collectives: 31.8 us -> none  [the longest x1 24.9 us: per_device(): lax.all_to_all(send_rows.reshape(peer_count, capacity, -1), 'expert', spl...]
    ppermute x0 -> x18, starting transfers between devices: none -> 21.6 us  [over(): return lambda x: lax.ppermute(x, axis, pairs)]
    dot_general x3 -> x0, matrix products: 10.3 us -> none  [the longest x1 6.1 us: per_device(): lax.dot_general(slot_rows, scaled, (((0,), (0,)), ((), ())), preferred_el...]
    pallas_call x0 -> x9, Pallas kernels: none -> 6.27 us  [run(): pl.pallas_call(kernel, out_shape=outs, scratch_shapes=list(scratch), comp...]
    all_to_all x1 -> x0, waiting for transfers between devices: 4.26 us -> none  [per_device(): lax.all_to_all(pair_grad.reshape(peer_count, capacity), 'expert', split_a...]
    all_to_all x1 -> x0, starting transfers between devices: 3.22 us -> none  [per_device(): lax.all_to_all(pair_grad.reshape(peer_count, capacity), 'expert', split_a...]
  transfers between devices with their start and end apart: 2 -> 18, of which waited for: 2 -> 7; matrix products, arithmetic and copies ran while one was open for 2% -> 2% of each run, Pallas kernels for 0% -> 5%
where the time goes in v1:
time: 70.1 us; the launch traced here: 69.8 us
  waiting for transfers between devices  36.1 us (51%)
  starting transfers between devices  21.6 us (31%)
  Pallas kernels  6.27 us (9%)
  local copies, waits for them, and re-layouts  3.98 us (6%)
  other arithmetic  1.05 us (1%)
  between operations  0.75 us (1%)
    ppermute x18, waiting for transfers between devices, over(): return lambda x: lax.ppermute(x, axis, pairs)  36.1 us
    ppermute x18, starting transfers between devices, over(): return lambda x: lax.ppermute(x, axis, pairs)  21.6 us
    pallas_call x9, Pallas kernels, run(): pl.pallas_call(kernel, out_shape=outs, scratch_shapes=list(scratch), comp...  6.27 us
    unnamed x14, local copies, waits for them, and re-layouts  3.98 us
  transfers between devices with their start and end apart: 18, of which 7 were waited for; matrix products, arithmetic and copies ran while one was open for 2% of the time, Pallas kernels for 5%

profile of v1, /device:TPU:0, one launch (start us, length us, event | category | flops | bytes accessed | tf_op | source)
XLA Modules:
  0.0 69.8 jit_solution(8731325076787022362)
XLA Ops:
  1.1 1.0 %copy-done = bf16[128,2048]{1,0:T(8,128)(2,1)S(1)} copy-done((bf16[128,2048]{1,0:T(8,128)(2,1)S(1)}, bf16[128,2048]{1,0:T(8,128)(2,1)}, u32[]{:S(2)}) %copy-start) | copy-done | bytes 524312
  3.7 1.5 %collective-permute-done.other_ref = bf16[144,1024]{1,0:T(8,128)(2,1)S(1)} collective-permute-done((bf16[144,1024]{1,0:T(8,128)(2,1)S(1)}, bf16[144,1024]{1,0:T(8,128)(2,1)S(1)}, u32[]{:S(2)}, u32[]{:S(2)}) %collective-permute-start) | collective-permute-done | bytes 294944 | tf_op jit(solution)/shard_map/ppermute | solution.py:229
  5.3 1.0 %copy-done.1 = bf16[128,2048]{1,0:T(8,128)(2,1)S(1)} copy-done((bf16[128,2048]{1,0:T(8,128)(2,1)S(1)}, bf16[128,2048]{1,0:T(8,128)(2,1)}, u32[]{:S(2)}) %copy-start.1) | copy-done | bytes 524312
  6.8 2.7 %collective-permute-start.1 = (bf16[192,384]{1,0:T(8,128)(2,1)S(1)}, bf16[192,384]{1,0:T(8,128)(2,1)S(1)}, u32[]{:S(2)}, u32[]{:S(2)}) collective-permute-start(bf16[192,384]{1,0:T(8,128)(2,1)S(1)} %get-tuple-element.36), channel_id=1, source_target_pairs={{0,1},{1,0},{2,3},{3,2},{4,5},{5,4},{6,7},{7,6},{8,9},{9,8},{10,11... | collective-permute-start | bytes 442376 | tf_op jit(solution)/shard_map/ppermute | solution.py:229
  9.5 1.5 %collective-permute-start.2 = (bf16[192,384]{1,0:T(8,128)(2,1)S(1)}, bf16[192,384]{1,0:T(8,128)(2,1)S(1)}, u32[]{:S(2)}, u32[]{:S(2)}) collective-permute-start(bf16[192,384]{1,0:T(8,128)(2,1)S(1)} %get-tuple-element.37), channel_id=1, source_target_pairs={{0,2},{1,3},{2,0},{3,1},{4,6},{5,7},{6,4},{7,5},{8,10},{9,11},{10,... | collective-permute-start | bytes 442376 | tf_op jit(solution)/shard_map/ppermute | solution.py:229
  12.1 1.4 %collective-permute-start.3 = (bf16[192,384]{1,0:T(8,128)(2,1)S(1)}, bf16[192,384]{1,0:T(8,128)(2,1)S(1)}, u32[]{:S(2)}, u32[]{:S(2)}) collective-permute-start(bf16[192,384]{1,0:T(8,128)(2,1)S(1)} %get-tuple-element.38), channel_id=1, source_target_pairs={{0,3},{1,2},{2,1},{3,0},{4,7},{5,6},{6,5},{7,4},{8,11},{9,10},{10,... | collective-permute-start | bytes 442376 | tf_op jit(solution)/shard_map/ppermute | solution.py:229
  13.6 3.7 %collective-permute-done.5.p1 = bf16[192,256]{1,0:T(8,128)(2,1)S(1)} collective-permute-done((bf16[192,256]{1,0:T(8,128)(2,1)S(1)}, bf16[192,256]{1,0:T(8,128)(2,1)S(1)}, u32[]{:S(2)}, u32[]{:S(2)}) %collective-permute-start.5) | collective-permute-done | bytes 98336 | tf_op jit(solution)/shard_map/ppermute | solution.py:229
  17.3 1.0 %collective-permute-start.8 = (bf16[192,512]{1,0:T(8,128)(2,1)S(1)}, bf16[192,512]{1,0:T(8,128)(2,1)S(1)}, u32[]{:S(2)}, u32[]{:S(2)}) collective-permute-start(bf16[192,512]{1,0:T(8,128)(2,1)S(1)} %get-tuple-element.48), channel_id=1, source_target_pairs={{0,1},{1,0},{2,3},{3,2},{4,5},{5,4},{6,7},{7,6},{8,9},{9,8},{10,11... | collective-permute-start | bytes 589832 | tf_op jit(solution)/shard_map/ppermute | solution.py:229
  18.3 1.5 %collective-permute-start.9 = (bf16[192,512]{1,0:T(8,128)(2,1)S(1)}, bf16[192,512]{1,0:T(8,128)(2,1)S(1)}, u32[]{:S(2)}, u32[]{:S(2)}) collective-permute-start(bf16[192,512]{1,0:T(8,128)(2,1)S(1)} %get-tuple-element.49), channel_id=1, source_target_pairs={{0,2},{1,3},{2,0},{3,1},{4,6},{5,7},{6,4},{7,5},{8,10},{9,11},{10,... | collective-permute-start | bytes 589832 | tf_op jit(solution)/shard_map/ppermute | solution.py:229
  19.8 0.9 %collective-permute-start.10 = (bf16[192,512]{1,0:T(8,128)(2,1)S(1)}, bf16[192,512]{1,0:T(8,128)(2,1)S(1)}, u32[]{:S(2)}, u32[]{:S(2)}) collective-permute-start(bf16[192,512]{1,0:T(8,128)(2,1)S(1)} %get-tuple-element.50), channel_id=1, source_target_pairs={{0,3},{1,2},{2,1},{3,0},{4,7},{5,6},{6,5},{7,4},{8,11},{9,10},{10,... | collective-permute-start | bytes 589832 | tf_op jit(solution)/shard_map/ppermute | solution.py:229
  20.9 0.9 %collective-permute-start.6 = (bf16[192,256]{1,0:T(8,128)(2,1)S(1)}, bf16[192,256]{1,0:T(8,128)(2,1)S(1)}, u32[]{:S(2)}, u32[]{:S(2)}) collective-permute-start(bf16[192,256]{1,0:T(8,128)(2,1)S(1)} %get-tuple-element.43), channel_id=1, source_target_pairs={{0,2},{1,3},{2,0},{3,1},{4,6},{5,7},{6,4},{7,5},{8,10},{9,11},{10,... | collective-permute-start | bytes 294920 | tf_op jit(solution)/shard_map/ppermute | solution.py:229
  21.8 2.1 %collective-permute-start.7 = (bf16[192,256]{1,0:T(8,128)(2,1)S(1)}, bf16[192,256]{1,0:T(8,128)(2,1)S(1)}, u32[]{:S(2)}, u32[]{:S(2)}) collective-permute-start(bf16[192,256]{1,0:T(8,128)(2,1)S(1)} %get-tuple-element.44), channel_id=1, source_target_pairs={{0,3},{1,2},{2,1},{3,0},{4,7},{5,6},{6,5},{7,4},{8,11},{9,10},{10,... | collective-permute-start | bytes 294920 | tf_op jit(solution)/shard_map/ppermute | solution.py:229
  24.6 8.4 %collective-permute-done.6.p2 = bf16[192,256]{1,0:T(8,128)(2,1)S(1)} collective-permute-done((bf16[192,256]{1,0:T(8,128)(2,1)S(1)}, bf16[192,256]{1,0:T(8,128)(2,1)S(1)}, u32[]{:S(2)}, u32[]{:S(2)}) %collective-permute-start.6) | collective-permute-done | bytes 98336 | tf_op jit(solution)/shard_map/ppermute | solution.py:229
  33.6 0.8 %shard_map.81 = (bf16[256,768]{1,0:T(8,128)(2,1)S(1)}, f32[256,768]{1,0:T(8,128)S(1)}, bf16[768,512]{1,0:T(8,128)(2,1)S(1)}) custom-call(bf16[192,512]{1,0:T(8,128)(2,1)S(1)} %get-tuple-element.47.p0, bf16[192,512]{1,0:T(8,128)(2,1)S(1)} %collective-permute-done.8.p1, bf16[192,512]{1,0:T(8,128)(2,1)S(1)} %collective-permute-done.9.p2, ...), custom_call_target="tpu_custom_call" | custom-call | flops 603979776 | bytes 3932160 | tf_op jit(solution)/shard_map/pallas_call | solution.py:212
  34.9 1.4 %shard_map.82 = (f32[384,768]{1,0:T(8,128)S(1)}, f32[384,768]{1,0:T(8,128)S(1)}) custom-call(bf16[768,256]{1,0:T(8,128)(2,1)S(1)} %get-tuple-element.39.rows0, bf16[768,256]{1,0:T(8,128)(2,1)S(1)} %get-tuple-element.46.rows1, bf16[768,512]{1,0:T(8,128)(2,1)S(1)} %get-tuple-element.51.rows23, bf16[768,2048]{1,0:T(8,128)(2,1)S(1)} %bitcast.8), custom_call_target="tpu_custom_call" | custom-call | flops 1207959552 | bytes 7077888 | tf_op jit(solution)/shard_map/pallas_call | solution.py:212
  36.4 1.6 %collective-permute-start.16 = (bf16[256,768]{1,0:T(8,128)(2,1)S(1)}, bf16[256,768]{1,0:T(8,128)(2,1)S(1)}, u32[]{:S(2)}, u32[]{:S(2)}) collective-permute-start(bf16[256,768]{1,0:T(8,128)(2,1)S(1)} %get-tuple-element.62), channel_id=1, source_target_pairs={{0,8},{4,12},{8,0},{12,4},{16,24},{20,28},{24,16},{28,20},{1,9},{5... | collective-permute-start | bytes 1179656 | tf_op jit(solution)/shard_map/ppermute | solution.py:229
  38.5 9.9 %collective-permute-done.16 = bf16[256,768]{1,0:T(8,128)(2,1)S(1)} collective-permute-done((bf16[256,768]{1,0:T(8,128)(2,1)S(1)}, bf16[256,768]{1,0:T(8,128)(2,1)S(1)}, u32[]{:S(2)}, u32[]{:S(2)}) %collective-permute-start.16) | collective-permute-done | bytes 393248 | tf_op jit(solution)/shard_map/ppermute | solution.py:229
  48.5 2.7 %collective-permute-start.17 = (bf16[256,768]{1,0:T(8,128)(2,1)S(1)}, bf16[256,768]{1,0:T(8,128)(2,1)S(1)}, u32[]{:S(2)}, u32[]{:S(2)}) collective-permute-start(bf16[256,768]{1,0:T(8,128)(2,1)S(1)} %add_convert_fusion), channel_id=1, source_target_pairs={{0,16},{4,20},{8,24},{12,28},{16,0},{20,4},{24,8},{28,12},{1,17},{... | collective-permute-start | bytes 1179656 | tf_op jit(solution)/shard_map/ppermute | solution.py:229
  51.1 1.1 %shard_map.83 = (bf16[384,768]{1,0:T(8,128)(2,1)}, f32[96,128]{1,0:T(8,128)S(1)}, f32[96,128]{1,0:T(8,128)S(1)}, f32[96,128]{1,0:T(8,128)S(1)}, f32[96,128]{1,0:T(8,128)S(1)}) custom-call(f32[384,768]{1,0:T(8,128)S(1)} %get-tuple-element.52.own_ref, f32[384,768]{1,0:T(8,128)S(1)} %collective-permute-done.11.come_ref, ...), custom_call_target="tpu_custom_call" | custom-call | bytes 4325376 | tf_op jit(solution)/shard_map/pallas_call | solution.py:212
  52.3 1.5 %collective-permute-start.12 = (f32[96,128]{1,0:T(8,128)S(1)}, f32[96,128]{1,0:T(8,128)S(1)}, u32[]{:S(2)}, u32[]{:S(2)}) collective-permute-start(f32[96,128]{1,0:T(8,128)S(1)} %get-tuple-element.56), channel_id=1, source_target_pairs={{0,1},{1,0},{2,3},{3,2},{4,5},{5,4},{6,7},{7,6},{8,9},{9,8},{10,11... | collective-permute-start | bytes 147464 | tf_op jit(solution)/shard_map/ppermute | solution.py:229
  54.3 1.5 %collective-permute-start.14 = (f32[96,128]{1,0:T(8,128)S(1)}, f32[96,128]{1,0:T(8,128)S(1)}, u32[]{:S(2)}, u32[]{:S(2)}) collective-permute-start(f32[96,128]{1,0:T(8,128)S(1)} %get-tuple-element.58), channel_id=1, source_target_pairs={{0,3},{1,2},{2,1},{3,0},{4,7},{5,6},{6,5},{7,4},{8,11},{9,10},{10,... | collective-permute-start | bytes 147464 | tf_op jit(solution)/shard_map/ppermute | solution.py:229
  55.8 7.8 %collective-permute-done.15 = bf16[256,768]{1,0:T(8,128)(2,1)S(1)} collective-permute-done((bf16[256,768]{1,0:T(8,128)(2,1)S(1)}, bf16[256,768]{1,0:T(8,128)(2,1)S(1)}, u32[]{:S(2)}, u32[]{:S(2)}) %collective-permute-start.15) | collective-permute-done | bytes 393248 | tf_op jit(solution)/shard_map/ppermute | solution.py:229
  63.6 4.5 %collective-permute-done.17 = bf16[256,768]{1,0:T(8,128)(2,1)S(1)} collective-permute-done((bf16[256,768]{1,0:T(8,128)(2,1)S(1)}, bf16[256,768]{1,0:T(8,128)(2,1)S(1)}, u32[]{:S(2)}, u32[]{:S(2)}) %collective-permute-start.17) | collective-permute-done | bytes 393248 | tf_op jit(solution)/shard_map/ppermute | solution.py:229
  68.2 1.0 %add_bitcast_fusion = f32[1,256,768]{2,1,0:T(8,128)} fusion(bf16[256,768]{1,0:T(8,128)(2,1)S(1)} %collective-permute-done.17, f32[256,768]{1,0:T(8,128)S(1)} %get-tuple-element.59, bf16[256,768]{1,0:T(8,128)(2,1)S(1)} %collective-permute-done.15), kind=kLoop, calls=%fused_computation | loop fusion | flops 786432 | bytes 2359296 | tf_op jit(solution)/shard_map/broadcast_in_dim | solution.py:298
  (37 shorter events, 7.3 us)
Async XLA Ops:
  0.6 21.2 %collective-permute-start.4 = (bf16[384,768]{1,0:T(8,128)(2,1)}, bf16[384,768]{1,0:T(8,128)(2,1)S(1)}, u32[]{:S(2)}, u32[]{:S(2)}) collective-permute-start(bf16[384,768]{1,0:T(8,128)(2,1)} %bitcast.9), channel_id=1, source_target_pairs={{0,4},{4,0},{8,12},{12,8},{16,20},{20,16},{24,28},{28,24},{1,5},{5... | collective-permute-start | bytes 1769480 | tf_op jit(solution)/shard_map/ppermute | solution.py:229
  1.1 1.0 %copy-start = (bf16[128,2048]{1,0:T(8,128)(2,1)S(1)}, bf16[128,2048]{1,0:T(8,128)(2,1)}, u32[]{:S(2)}) copy-start(bf16[128,2048]{1,0:T(8,128)(2,1)} %grad_ref.5) | copy-start | bytes 1572868
  2.2 0.7 copy-start.4
  3.6 1.6 %collective-permute-start = (bf16[144,1024]{1,0:T(8,128)(2,1)S(1)}, bf16[144,1024]{1,0:T(8,128)(2,1)S(1)}, u32[]{:S(2)}, u32[]{:S(2)}) collective-permute-start(bf16[144,1024]{1,0:T(8,128)(2,1)S(1)} %get-tuple-element.34), channel_id=1, source_target_pairs={{0,4},{4,0},{8,12},{12,8},{16,20},{20,16},{24,28},{28,24},{1,5},{5... | collective-permute-start | bytes 884744 | tf_op jit(solution)/shard_map/ppermute | solution.py:229
  5.3 1.0 %copy-start.1 = (bf16[128,2048]{1,0:T(8,128)(2,1)S(1)}, bf16[128,2048]{1,0:T(8,128)(2,1)}, u32[]{:S(2)}) copy-start(bf16[128,2048]{1,0:T(8,128)(2,1)} %grad_ref.5) | copy-start | bytes 1572868
  6.3 17.6 %copy-start.3 = (bf16[1,384,768]{2,1,0:T(8,128)(2,1)S(1)}, bf16[1,384,768]{2,1,0:T(8,128)(2,1)}, u32[]{:S(2)}) copy-start(bf16[1,384,768]{2,1,0:T(8,128)(2,1)} %param.8) | copy-start | bytes 1769476
  6.8 11.5 %collective-permute-start.1 = (bf16[192,384]{1,0:T(8,128)(2,1)S(1)}, bf16[192,384]{1,0:T(8,128)(2,1)S(1)}, u32[]{:S(2)}, u32[]{:S(2)}) collective-permute-start(bf16[192,384]{1,0:T(8,128)(2,1)S(1)} %get-tuple-element.36), channel_id=1, source_target_pairs={{0,1},{1,0},{2,3},{3,2},{4,5},{5,4},{6,7},{7,6},{8,9},{9,8},{10,11... | collective-permute-start | bytes 442376 | tf_op jit(solution)/shard_map/ppermute | solution.py:229
  9.5 10.3 %collective-permute-start.2 = (bf16[192,384]{1,0:T(8,128)(2,1)S(1)}, bf16[192,384]{1,0:T(8,128)(2,1)S(1)}, u32[]{:S(2)}, u32[]{:S(2)}) collective-permute-start(bf16[192,384]{1,0:T(8,128)(2,1)S(1)} %get-tuple-element.37), channel_id=1, source_target_pairs={{0,2},{1,3},{2,0},{3,1},{4,6},{5,7},{6,4},{7,5},{8,10},{9,11},{10,... | collective-permute-start | bytes 442376 | tf_op jit(solution)/shard_map/ppermute | solution.py:229
  11.5 5.8 %collective-permute-start.5 = (bf16[192,256]{1,0:T(8,128)(2,1)S(1)}, bf16[192,256]{1,0:T(8,128)(2,1)S(1)}, u32[]{:S(2)}, u32[]{:S(2)}) collective-permute-start(bf16[192,256]{1,0:T(8,128)(2,1)S(1)} %get-tuple-element.42), channel_id=1, source_target_pairs={{0,1},{1,0},{2,3},{3,2},{4,5},{5,4},{6,7},{7,6},{8,9},{9,8},{10,11... | collective-permute-start | bytes 294920 | tf_op jit(solution)/shard_map/ppermute | solution.py:229
  12.1 8.8 %collective-permute-start.3 = (bf16[192,384]{1,0:T(8,128)(2,1)S(1)}, bf16[192,384]{1,0:T(8,128)(2,1)S(1)}, u32[]{:S(2)}, u32[]{:S(2)}) collective-permute-start(bf16[192,384]{1,0:T(8,128)(2,1)S(1)} %get-tuple-element.38), channel_id=1, source_target_pairs={{0,3},{1,2},{2,1},{3,0},{4,7},{5,6},{6,5},{7,4},{8,11},{9,10},{10,... | collective-permute-start | bytes 442376 | tf_op jit(solution)/shard_map/ppermute | solution.py:229
  17.3 16.3 %collective-permute-start.8 = (bf16[192,512]{1,0:T(8,128)(2,1)S(1)}, bf16[192,512]{1,0:T(8,128)(2,1)S(1)}, u32[]{:S(2)}, u32[]{:S(2)}) collective-permute-start(bf16[192,512]{1,0:T(8,128)(2,1)S(1)} %get-tuple-element.48), channel_id=1, source_target_pairs={{0,1},{1,0},{2,3},{3,2},{4,5},{5,4},{6,7},{7,6},{8,9},{9,8},{10,11... | collective-permute-start | bytes 589832 | tf_op jit(solution)/shard_map/ppermute | solution.py:229
  18.3 15.3 %collective-permute-start.9 = (bf16[192,512]{1,0:T(8,128)(2,1)S(1)}, bf16[192,512]{1,0:T(8,128)(2,1)S(1)}, u32[]{:S(2)}, u32[]{:S(2)}) collective-permute-start(bf16[192,512]{1,0:T(8,128)(2,1)S(1)} %get-tuple-element.49), channel_id=1, source_target_pairs={{0,2},{1,3},{2,0},{3,1},{4,6},{5,7},{6,4},{7,5},{8,10},{9,11},{10,... | collective-permute-start | bytes 589832 | tf_op jit(solution)/shard_map/ppermute | solution.py:229
  19.8 13.7 %collective-permute-start.10 = (bf16[192,512]{1,0:T(8,128)(2,1)S(1)}, bf16[192,512]{1,0:T(8,128)(2,1)S(1)}, u32[]{:S(2)}, u32[]{:S(2)}) collective-permute-start(bf16[192,512]{1,0:T(8,128)(2,1)S(1)} %get-tuple-element.50), channel_id=1, source_target_pairs={{0,3},{1,2},{2,1},{3,0},{4,7},{5,6},{6,5},{7,4},{8,11},{9,10},{10,... | collective-permute-start | bytes 589832 | tf_op jit(solution)/shard_map/ppermute | solution.py:229
  20.9 12.1 %collective-permute-start.6 = (bf16[192,256]{1,0:T(8,128)(2,1)S(1)}, bf16[192,256]{1,0:T(8,128)(2,1)S(1)}, u32[]{:S(2)}, u32[]{:S(2)}) collective-permute-start(bf16[192,256]{1,0:T(8,128)(2,1)S(1)} %get-tuple-element.43), channel_id=1, source_target_pairs={{0,2},{1,3},{2,0},{3,1},{4,6},{5,7},{6,4},{7,5},{8,10},{9,11},{10,... | collective-permute-start | bytes 294920 | tf_op jit(solution)/shard_map/ppermute | solution.py:229
  21.8 11.2 %collective-permute-start.7 = (bf16[192,256]{1,0:T(8,128)(2,1)S(1)}, bf16[192,256]{1,0:T(8,128)(2,1)S(1)}, u32[]{:S(2)}, u32[]{:S(2)}) collective-permute-start(bf16[192,256]{1,0:T(8,128)(2,1)S(1)} %get-tuple-element.44), channel_id=1, source_target_pairs={{0,3},{1,2},{2,1},{3,0},{4,7},{5,6},{6,5},{7,4},{8,11},{9,10},{10,... | collective-permute-start | bytes 294920 | tf_op jit(solution)/shard_map/ppermute | solution.py:229
  33.0 1.9 %copy-start.2 = (bf16[1,768,2048]{2,1,0:T(8,128)(2,1)S(1)}, bf16[1,768,2048]{2,1,0:T(8,128)(2,1)}, u32[]{:S(2)}) copy-start(bf16[1,768,2048]{2,1,0:T(8,128)(2,1)} %param.9) | copy-start | bytes 9437188
  36.4 14.8 %collective-permute-start.11 = (f32[384,768]{1,0:T(8,128)S(1)}, f32[384,768]{1,0:T(8,128)S(1)}, u32[]{:S(2)}, u32[]{:S(2)}) collective-permute-start(f32[384,768]{1,0:T(8,128)S(1)} %get-tuple-element.53), channel_id=1, source_target_pairs={{0,4},{4,0},{8,12},{12,8},{16,20},{20,16},{24,28},{28,24},{1,5},{5... | collective-permute-start | bytes 3538952 | tf_op jit(solution)/shard_map/ppermute | solution.py:229
  36.4 12.0 %collective-permute-start.16 = (bf16[256,768]{1,0:T(8,128)(2,1)S(1)}, bf16[256,768]{1,0:T(8,128)(2,1)S(1)}, u32[]{:S(2)}, u32[]{:S(2)}) collective-permute-start(bf16[256,768]{1,0:T(8,128)(2,1)S(1)} %get-tuple-element.62), channel_id=1, source_target_pairs={{0,8},{4,12},{8,0},{12,4},{16,24},{20,28},{24,16},{28,20},{1,9},{5... | collective-permute-start | bytes 1179656 | tf_op jit(solution)/shard_map/ppermute | solution.py:229
  38.1 25.5 %collective-permute-start.15 = (bf16[256,768]{1,0:T(8,128)(2,1)S(1)}, bf16[256,768]{1,0:T(8,128)(2,1)S(1)}, u32[]{:S(2)}, u32[]{:S(2)}) collective-permute-start(bf16[256,768]{1,0:T(8,128)(2,1)S(1)} %get-tuple-element.60), channel_id=1, source_target_pairs={{0,8},{4,12},{8,0},{12,4},{16,24},{20,28},{24,16},{28,20},{1,9},{5... | collective-permute-start | bytes 1179656 | tf_op jit(solution)/shard_map/ppermute | solution.py:229
  48.5 19.7 %collective-permute-start.17 = (bf16[256,768]{1,0:T(8,128)(2,1)S(1)}, bf16[256,768]{1,0:T(8,128)(2,1)S(1)}, u32[]{:S(2)}, u32[]{:S(2)}) collective-permute-start(bf16[256,768]{1,0:T(8,128)(2,1)S(1)} %add_convert_fusion), channel_id=1, source_target_pairs={{0,16},{4,20},{8,24},{12,28},{16,0},{20,4},{24,8},{28,12},{1,17},{... | collective-permute-start | bytes 1179656 | tf_op jit(solution)/shard_map/ppermute | solution.py:229
  52.3 16.9 %collective-permute-start.12 = (f32[96,128]{1,0:T(8,128)S(1)}, f32[96,128]{1,0:T(8,128)S(1)}, u32[]{:S(2)}, u32[]{:S(2)}) collective-permute-start(f32[96,128]{1,0:T(8,128)S(1)} %get-tuple-element.56), channel_id=1, source_target_pairs={{0,1},{1,0},{2,3},{3,2},{4,5},{5,4},{6,7},{7,6},{8,9},{9,8},{10,11... | collective-permute-start | bytes 147464 | tf_op jit(solution)/shard_map/ppermute | solution.py:229
  53.8 15.4 %collective-permute-start.13 = (f32[96,128]{1,0:T(8,128)S(1)}, f32[96,128]{1,0:T(8,128)S(1)}, u32[]{:S(2)}, u32[]{:S(2)}) collective-permute-start(f32[96,128]{1,0:T(8,128)S(1)} %get-tuple-element.57), channel_id=1, source_target_pairs={{0,2},{1,3},{2,0},{3,1},{4,6},{5,7},{6,4},{7,5},{8,10},{9,11},{10,... | collective-permute-start | bytes 147464 | tf_op jit(solution)/shard_map/ppermute | solution.py:229
  54.3 14.9 %collective-permute-start.14 = (f32[96,128]{1,0:T(8,128)S(1)}, f32[96,128]{1,0:T(8,128)S(1)}, u32[]{:S(2)}, u32[]{:S(2)}) collective-permute-start(f32[96,128]{1,0:T(8,128)S(1)} %get-tuple-element.58), channel_id=1, source_target_pairs={{0,3},{1,2},{2,1},{3,0},{4,7},{5,6},{6,5},{7,4},{8,11},{9,10},{10,... | collective-permute-start | bytes 147464 | tf_op jit(solution)/shard_map/ppermute | solution.py:229
  68.2 1.0 %copy-start.5 = (s32[128,8]{0,1:T(8,128)S(1)}, s32[128,8]{0,1:T(8,128)}, u32[]{:S(2)}) copy-start(s32[128,8]{0,1:T(8,128)} %param.6) | copy-start | bytes 12292
  (1 other events, 0.7 us)

commit v2 on v1

v2 whole, which is shorter than its diff:
```python
import functools

import jax
import jax.numpy as jnp
from jax import lax
from jax.experimental import pallas as pl
from jax.experimental.pallas import tpu as pltpu
from jax.sharding import PartitionSpec as P

TOP = 8
EXP_DEV = 4
F32 = jnp.float32
BF16 = jnp.bfloat16
GATE_LANES = 128


def per_device_general(grad_out, expert_ids, gate_weights, saved_hidden, down_weight):
    peer_count = lax.axis_size("expert")
    tok_rows = grad_out.shape[0]
    capacity = saved_hidden.shape[1] // peer_count
    slot_total = peer_count * capacity
    flat_ids = expert_ids.reshape(-1)
    flight = flat_ids % EXP_DEV == 0
    target = flat_ids // EXP_DEV
    onehot = (
        (target[:, None] == jnp.arange(peer_count, dtype=jnp.int32)[None, :]) & flight[:, None]
    ).astype(jnp.int32)
    slot_rank = jnp.cumsum(onehot, axis=0) - 1
    slot_index = jnp.sum(slot_rank * onehot, axis=1)
    slot_place = jnp.where(flight, target * capacity + slot_index, slot_total)
    slot_match = slot_place[None, :] == jnp.arange(slot_total, dtype=jnp.int32)[:, None]
    gates_flat = gate_weights.astype(F32).reshape(-1)
    send_gates = jnp.sum(jnp.where(slot_match, gates_flat[None, :], 0.0), axis=1).astype(BF16)
    token_match = jnp.any(slot_match.reshape(slot_total, tok_rows, TOP), axis=2).astype(BF16)
    send_rows = jnp.dot(token_match, grad_out, preferred_element_type=F32).astype(BF16)
    exchange = functools.partial(
        lax.all_to_all, axis_name="expert", split_axis=0, concat_axis=0, tiled=True
    )
    rows_in = exchange(send_rows.reshape(peer_count, capacity, -1))
    gates_in = exchange(send_gates.reshape(peer_count, capacity))
    slot_rows = rows_in.reshape(slot_total, -1)
    slot_gates = gates_in.reshape(slot_total).astype(F32)
    hidden = saved_hidden[0]
    weight = down_weight[0]
    update = lax.dot_general(
        slot_rows, weight, (((1,), (1,)), ((), ())), preferred_element_type=F32
    )
    grad_hidden = (slot_gates[:, None] * update).astype(BF16)
    pair_grad = jnp.sum(hidden.astype(F32) * update, axis=1)
    returned = exchange(pair_grad.reshape(peer_count, capacity))
    gate_flat = jnp.sum(jnp.where(slot_match, returned.reshape(slot_total)[:, None], 0.0), axis=0)
    gate_grad = gate_flat.reshape(tok_rows, TOP)
    scaled = (slot_gates[:, None] * hidden.astype(F32)).astype(BF16)
    grad_term = lax.dot_general(
        slot_rows, scaled, (((0,), (0,)), ((), ())), preferred_element_type=F32
    )
    weight_shard = lax.psum_scatter(grad_term, "dp", scatter_dimension=0, tiled=True)
    return (grad_hidden[None], gate_grad, weight_shard[None])


def coordinates():
    group = lax.axis_index("dp")
    return group // 2, group % 2, lax.axis_index("expert")


def dot(a, b, dims):
    return lax.dot_general(a, b, (dims, ((), ())), preferred_element_type=F32)


def swap_kernel(block, ids_hbm, gates_hbm, grad_hbm, send_ref, own_ref, marks_ref, ids_ref, gates_ref, sems):
    _, core, _ = coordinates()
    tokens = grad_hbm.shape[0]
    count = own_ref.shape[1] // block
    copies = [
        pltpu.make_async_copy(ids_hbm, ids_ref, sems.at[0]),
        pltpu.make_async_copy(gates_hbm, gates_ref, sems.at[1]),
    ]
    for i in range(count):
        at = slice(i * block, (i + 1) * block)
        for n, (side, ref) in enumerate(((1 - core, send_ref), (core, own_ref))):
            start = pl.multiple_of((2 * i + side) * block, block)
            copies.append(
                pltpu.make_async_copy(
                    grad_hbm.at[:, pl.ds(start, block)],
                    ref.at[pl.ds(0, tokens), at],
                    sems.at[2 + 2 * i + n],
                )
            )
    for copy in copies:
        copy.start()
    send_ref[tokens:, :] = jnp.zeros((16, send_ref.shape[1]), BF16)
    copies[0].wait()
    copies[1].wait()
    ids = ids_ref[...]
    gates = gates_ref[...].astype(F32)
    experts = ids.shape[0] // 2
    rows = []
    for j in range(experts):
        hit = ids == j * EXP_DEV
        value = jnp.sum(jnp.where(hit, gates, 0.0), axis=0, keepdims=True)
        live = jnp.sum(jnp.where(hit, 1.0, 0.0), axis=0, keepdims=True)
        rows.append(jnp.where(live > 0.0, value, -1.0))
    rows.append(jnp.full((marks_ref.shape[0] - experts, tokens), -1.0, F32))
    marks = jnp.concatenate(rows, axis=0).astype(BF16)
    marks_ref[...] = marks
    send_ref[tokens:, :tokens] = marks
    for copy in copies[2:]:
        copy.wait()


def gather_kernel(block, capacity, own_ref, marks_ref, other_ref, hidden_hbm, *outs):
    first, (matches_ref, hidden_ref, scratch, sem) = outs[:-4], outs[-4:]
    copy = pltpu.make_async_copy(hidden_hbm, hidden_ref, sem)
    copy.start()
    chip, _, peer = coordinates()
    tokens = own_ref.shape[0]
    before = (
        lax.broadcasted_iota(jnp.int32, (tokens, tokens), 0)
        < lax.broadcasted_iota(jnp.int32, (tokens, tokens), 1)
    ).astype(F32).astype(BF16)
    slot = lax.broadcasted_iota(jnp.int32, (capacity, tokens), 0).astype(F32)
    columns = pl.ds(pl.multiple_of((chip ^ 3) * block, block), block)
    gate_rows = [[], [], [], []]
    for g in range(2):
        marks = (marks_ref[...] if g == 0 else other_ref[tokens:, :tokens]).astype(F32)
        live = jnp.where(marks >= 0.0, 1.0, 0.0)
        rank = dot(live.astype(BF16), before, ((1,), (0,)))
        scratch[2 * g] = marks
        scratch[2 * g + 1] = jnp.where(marks >= 0.0, rank, -1.0)
        rows = (own_ref if g == 0 else other_ref)[:tokens, columns]
        for r in range(4):
            e = peer ^ r
            gate = scratch[2 * g, pl.ds(e, 1), :]
            place = scratch[2 * g + 1, pl.ds(e, 1), :]
            match = jnp.where(slot == place, 1.0, 0.0).astype(BF16)
            matches_ref[g, r] = match
            gate_rows[r].append(
                dot(jnp.broadcast_to(gate, (16, tokens)).astype(BF16), match, ((1,), (1,)))
            )
            first[r][g * capacity : (g + 1) * capacity, :] = dot(
                match, rows, ((1,), (0,))
            ).astype(BF16)
    row = lax.broadcasted_iota(jnp.int32, (16, capacity), 0)
    for r in range(4):
        both = jnp.where(row == 0, gate_rows[r][0], jnp.where(row == 1, gate_rows[r][1], 0.0))
        first[r][2 * capacity :, :] = jnp.zeros((16, first[r].shape[1]), BF16)
        first[r][2 * capacity :, :capacity] = both.astype(BF16)
    copy.wait()


def gate_column(piece, g, capacity):
    row = piece[2 * capacity :, :128].astype(F32)[g : g + 1, :]
    here = lax.broadcasted_iota(jnp.int32, (capacity, 128), 0) == lax.broadcasted_iota(
        jnp.int32, (capacity, 128), 1
    )
    return jnp.sum(jnp.where(here, row, 0.0), axis=1, keepdims=True)


def rest_kernel(block, capacity, chunks, own_ref, other_ref, matches_ref, *outs):
    chip, _, _ = coordinates()
    tokens = own_ref.shape[0]
    for i, k in enumerate(chunks):
        columns = pl.ds(pl.multiple_of((chip ^ (3 - k)) * block, block), block)
        to = slice(i * block, (i + 1) * block)
        for g in range(2):
            rows = (own_ref if g == 0 else other_ref)[:tokens, columns]
            for r in range(4):
                outs[r - 4][g * capacity : (g + 1) * capacity, to] = dot(
                    matches_ref[g, r], rows, ((1,), (0,))
                ).astype(BF16)


def split_rows(pieces, at_columns, capacity, all_ref, own_ref, cross_ref):
    slots = 4 * capacity
    for r, piece in enumerate(pieces):
        at = slice(r * capacity, (r + 1) * capacity)
        mine = piece[:capacity, at_columns]
        cross = piece[capacity : 2 * capacity, at_columns]
        own_ref[at, :] = mine
        cross_ref[at, :] = cross
        all_ref[at, :] = mine
        all_ref[slots + r * capacity : slots + (r + 1) * capacity, :] = cross


def first_kernel(
    capacity, p0, p1, p2, p3, hidden_ref, other_ref, low_ref, high_ref, scaled_ref, own_ref, cross_ref, all_ref
):
    _, _, peer = coordinates()
    pieces = (p0, p1, p2, p3)
    for r, piece in enumerate(pieces):
        source = pl.ds(pl.multiple_of((peer ^ r) * capacity, 32), capacity)
        for g, hidden in enumerate((hidden_ref, other_ref)):
            at = slice((4 * g + r) * capacity, (4 * g + r + 1) * capacity)
            gate = gate_column(piece, g, capacity)
            scaled_ref[at, :] = (gate * hidden[source, :].astype(F32)).astype(BF16)
    split_rows(pieces, slice(None), capacity, all_ref, own_ref, cross_ref)
    part = dot(all_ref[...], scaled_ref[...], ((0,), (0,))).astype(BF16)
    half = low_ref.shape[0]
    low_ref[...] = part[:half, :]
    high_ref[...] = part[half:, :]


def second_kernel(capacity, p0, p1, p2, p3, scaled_ref, low_ref, high_ref, sum_ref, own_ref, cross_ref, all_ref):
    block = own_ref.shape[1]
    split_rows((p0, p1, p2, p3), slice(0, block), capacity, all_ref, own_ref, cross_ref)
    part = dot(all_ref[...], scaled_ref[...], ((0,), (0,)))
    half = low_ref.shape[0]
    sum_ref[:half, :] = (part[:half, :] + low_ref[...].astype(F32)).astype(BF16)
    sum_ref[half:, :] = (part[half:, :] + high_ref[...].astype(F32)).astype(BF16)


def last_kernel(capacity, p0, p1, p2, p3, scaled_ref, _, part2_ref, part3_ref, own2, cross2, own3, cross3, all_ref):
    for i, (part, own, cross) in enumerate(((part2_ref, own2, cross2), (part3_ref, own3, cross3))):
        block = own.shape[1]
        at = slice((i + 1) * block, (i + 2) * block)
        split_rows((p0, p1, p2, p3), at, capacity, all_ref.at[i], own, cross)
        part[...] = dot(all_ref[i], scaled_ref[...], ((0,), (0,))).astype(part.dtype)


def update_kernel(capacity, *refs):
    rows, (p0, p1, p2, p3, hidden_ref, weight_ref, out_ref, *pairs) = refs[:8], refs[8:]
    chip, core, peer = coordinates()
    block = rows[0].shape[1]
    update = None
    for k in range(4):
        for i, side in enumerate((core, 1 - core)):
            start = pl.multiple_of((2 * (chip ^ (3 - k)) + side) * block, block)
            term = dot(rows[2 * k + i][...], weight_ref[:, pl.ds(start, block)], ((1,), (1,)))
            update = term if update is None else update + term
    for r, piece in enumerate((p0, p1, p2, p3)):
        source = pl.ds(pl.multiple_of((peer ^ r) * capacity, 32), capacity)
        here = update[r * capacity : (r + 1) * capacity, :]
        out_ref[source, :] = (gate_column(piece, 0, capacity) * here).astype(BF16)
        pair = jnp.sum(hidden_ref[source, :].astype(F32) * here, axis=1, keepdims=True)
        pairs[r][...] = jnp.broadcast_to(pair, (capacity, 128))


def gate_kernel(ids_ref, matches_ref, b0, b1, b2, b3, out_ref):
    _, _, peer = coordinates()
    ids = ids_ref[...]
    total = jnp.zeros(ids.shape, F32)
    for r, back in enumerate((b0, b1, b2, b3)):
        at_token = jnp.sum(
            jnp.where(matches_ref[0, r].astype(F32) > 0.0, back[...], 0.0), axis=0, keepdims=True
        )
        total = jnp.where(ids == (peer ^ r) * EXP_DEV, at_token, total)
    out_ref[...] = total


HBM = pl.BlockSpec(memory_space=pltpu.HBM)
ANY = pl.BlockSpec(memory_space=pl.ANY)
VMEM = pl.BlockSpec(memory_space=pltpu.VMEM)


def call(kernel, outs, specs=None, scratch=(), vmem=40 * 2**20):
    def run(*args):
        return pl.pallas_call(
            kernel,
            out_shape=outs,
            in_specs=specs or [VMEM] * len(args),
            out_specs=jax.tree.map(lambda _: VMEM, outs),
            scratch_shapes=list(scratch),
            compiler_params=pltpu.CompilerParams(vmem_limit_bytes=vmem),
            cost_estimate=pl.CostEstimate(flops=0, bytes_accessed=0, transcendentals=0),
        )(*args)

    return run


def arr(shape, dtype):
    return jax.ShapeDtypeStruct(shape, dtype)


def over(axis, size, mask):
    pairs = [(i, i ^ mask) for i in range(size)]
    return lambda x: lax.ppermute(x, axis, pairs)


def per_device(grad_out, expert_ids, gate_weights, saved_hidden, down_weight):
    groups, peers = lax.axis_size("dp"), lax.axis_size("expert")
    tokens, features = grad_out.shape
    hidden, weight = saved_hidden[0], down_weight[0]
    slots, units = hidden.shape
    capacity = slots // peers
    block = features // groups
    half = features // 2
    core_swap, near, far = (over("dp", groups, m) for m in (1, 2, 4))
    to_peer = [lambda x: x] + [over("expert", peers, r) for r in range(1, peers)]
    ids_t, gates_t = expert_ids.T, gate_weights.T

    send, own, marks = call(
        functools.partial(swap_kernel, block),
        [arr((tokens + 16, half), BF16), arr((tokens, half), BF16), arr((16, tokens), BF16)],
        specs=[HBM] * 3,
        scratch=[
            pltpu.VMEM((TOP, tokens), jnp.int32),
            pltpu.VMEM((TOP, tokens), BF16),
            pltpu.SemaphoreType.DMA((2 + groups,)),
        ],
    )(ids_t, gates_t, grad_out)
    other = core_swap(send)
    *first, matches, hidden = call(
        functools.partial(gather_kernel, block, capacity),
        [arr((2 * capacity + 16, block), BF16)] * peers
        + [arr((2, peers, capacity, tokens), BF16), arr((slots, units), BF16)],
        specs=[VMEM] * 3 + [HBM],
        scratch=[pltpu.VMEM((4, 16, tokens), F32), pltpu.SemaphoreType.DMA],
    )(own, marks, other, hidden)
    first = [to_peer[r](first[r]) for r in range(peers)]
    other_hidden = core_swap(hidden)

    def later(chunks, *after):
        pieces = call(
            functools.partial(rest_kernel, block, capacity, chunks),
            [arr((2 * capacity, len(chunks) * block), BF16)] * peers,
            specs=[VMEM] * 3 + [ANY] * len(after),
        )(own, other, matches, *after)
        return [to_peer[r](pieces[r]) for r in range(peers)]

    rest = later((1, 2, 3), matches)
    stack = (2 * slots, block)
    mine = arr((slots, block), BF16)
    low, high, scaled, own0, cross0 = call(
        functools.partial(first_kernel, capacity),
        [arr((block // 2, units), BF16)] * 2 + [arr((2 * slots, units), BF16), mine, mine],
        scratch=[pltpu.VMEM(stack, BF16)],
    )(*first, hidden, other_hidden)
    low, high = near(low), near(high)
    summed, own1, cross1 = call(
        functools.partial(second_kernel, capacity),
        [arr((block, units), BF16), mine, mine],
        scratch=[pltpu.VMEM(stack, BF16)],
    )(*rest, scaled, low, high)
    come1 = far(summed)
    part2, part3, own2, cross2, own3, cross3 = call(
        functools.partial(last_kernel, capacity),
        [arr((block, units), BF16), arr((block, units), F32), mine, mine, mine, mine],
        specs=[VMEM] * 5 + [ANY],
        scratch=[pltpu.VMEM((2,) + stack, BF16)],
    )(*rest, scaled, summed)
    come2 = near(part2)
    rows = []
    for own_k, cross_k in ((own0, cross0), (own1, cross1), (own2, cross2), (own3, cross3)):
        rows += [own_k, core_swap(cross_k)]
    grad_hidden, *pairs = call(
        functools.partial(update_kernel, capacity),
        [arr((slots, units), BF16)] + [arr((capacity, 128), F32)] * peers,
    )(*rows, *first, hidden, weight)
    back = [to_peer[r](pairs[r]) for r in range(peers)]
    gate_grad = call(gate_kernel, arr((TOP, tokens), F32))(ids_t, matches, *back).T
    weight_grad = part3 + come2.astype(F32) + come1.astype(F32)
    return grad_hidden[None], gate_grad, weight_grad[None]


def solution(mesh):
    placed = (
        P(("dp", "expert"), None),
        P(("dp", "expert"), None),
        P(("dp", "expert"), None),
        P("expert", "dp", None),
        P("expert", None, None),
    )
    small = mesh.shape["dp"] == 8 and mesh.shape["expert"] == 4
    return jax.shard_map(
        per_device if small else per_device_general,
        mesh=mesh,
        in_specs=placed,
        out_specs=(P("expert", "dp", None), P(("dp", "expert"), None), P("expert", "dp", None)),
        check_vma=False,
    )
```

time: 70.1 us -> 55 us (0.78)
  waiting for transfers between devices: 36.1 us -> 22.7 us
  starting transfers between devices: 21.6 us -> 20.4 us
    ppermute x18 -> x19, waiting for transfers between devices: 36.1 us -> 22.7 us  [over(): return lambda x: lax.ppermute(x, axis, pairs)]
    ppermute x18 -> x19, starting transfers between devices: 21.6 us -> 20.4 us  [over(): return lambda x: lax.ppermute(x, axis, pairs)]
    unnamed x14 -> x12, local copies, waits for them, and re-layouts: 3.98 us -> 3.48 us
    pallas_call x9 -> x8, Pallas kernels: 6.27 us -> 6.39 us  [run(): pl.pallas_call(kernel, out_shape=outs, in_specs=specs or [VMEM] * len(arg...]
  transfers between devices with their start and end apart: 18 -> 19, of which waited for: 7 -> 13; matrix products, arithmetic and copies ran while one was open for 2% -> 0% of each run, Pallas kernels for 5% -> 10%
where the time goes in v2:
time: 55 us; the launch traced here: 54.7 us
  waiting for transfers between devices  22.7 us (41%)
  starting transfers between devices  20.4 us (37%)
  Pallas kernels  6.39 us (12%)
  local copies, waits for them, and re-layouts  3.48 us (6%)
  other arithmetic  0.98 us (2%)
  between operations  0.72 us (1%)
    ppermute x19, waiting for transfers between devices, over(): return lambda x: lax.ppermute(x, axis, pairs)  22.7 us
    ppermute x19, starting transfers between devices, over(): return lambda x: lax.ppermute(x, axis, pairs)  20.4 us
    pallas_call x8, Pallas kernels, run(): pl.pallas_call(kernel, out_shape=outs, in_specs=specs or [VMEM] * len(arg...  6.39 us
    unnamed x12, local copies, waits for them, and re-layouts  3.48 us
  transfers between devices with their start and end apart: 19, of which 13 were waited for; matrix products, arithmetic and copies ran while one was open for 0% of the time, Pallas kernels for 10%

profile of v2, /device:TPU:0, one launch (start us, length us, event | category | flops | bytes accessed | tf_op | source)
XLA Modules:
  0.0 54.7 jit_solution(10949586159736217025)
XLA Ops:
  0.6 1.0 %copy-done.2 = bf16[128,2048]{1,0:T(8,128)(2,1)S(1)} copy-done((bf16[128,2048]{1,0:T(8,128)(2,1)S(1)}, bf16[128,2048]{1,0:T(8,128)(2,1)}, u32[]{:S(2)}) %copy-start.2) | copy-done | bytes 524312
  3.8 1.2 %collective-permute-done.other_ref = bf16[144,1024]{1,0:T(8,128)(2,1)S(1)} collective-permute-done((bf16[144,1024]{1,0:T(8,128)(2,1)S(1)}, bf16[144,1024]{1,0:T(8,128)(2,1)S(1)}, u32[]{:S(2)}, u32[]{:S(2)}) %collective-permute-start) | collective-permute-done | bytes 294944 | tf_op jit(solution)/shard_map/ppermute | solution.py:276
  5.0 1.1 %copy-done.1 = bf16[1,384,768]{2,1,0:T(8,128)(2,1)S(1)} copy-done((bf16[1,384,768]{2,1,0:T(8,128)(2,1)S(1)}, bf16[1,384,768]{2,1,0:T(8,128)(2,1)}, u32[]{:S(2)}) %copy-start.1) | copy-done | bytes 589848
  7.2 2.6 %collective-permute-start.1 = (bf16[208,256]{1,0:T(8,128)(2,1)S(1)}, bf16[208,256]{1,0:T(8,128)(2,1)S(1)}, u32[]{:S(2)}, u32[]{:S(2)}) collective-permute-start(bf16[208,256]{1,0:T(8,128)(2,1)S(1)} %get-tuple-element.39), channel_id=1, source_target_pairs={{0,1},{1,0},{2,3},{3,2},{4,5},{5,4},{6,7},{7,6},{8,9},{9,8},{10,11... | collective-permute-start | bytes 319496 | tf_op jit(solution)/shard_map/ppermute | solution.py:276
  9.8 1.5 %collective-permute-start.2 = (bf16[208,256]{1,0:T(8,128)(2,1)S(1)}, bf16[208,256]{1,0:T(8,128)(2,1)S(1)}, u32[]{:S(2)}, u32[]{:S(2)}) collective-permute-start(bf16[208,256]{1,0:T(8,128)(2,1)S(1)} %get-tuple-element.40), channel_id=1, source_target_pairs={{0,2},{1,3},{2,0},{3,1},{4,6},{5,7},{6,4},{7,5},{8,10},{9,11},{10,... | collective-permute-start | bytes 319496 | tf_op jit(solution)/shard_map/ppermute | solution.py:276
  12.4 1.4 %collective-permute-start.3 = (bf16[208,256]{1,0:T(8,128)(2,1)S(1)}, bf16[208,256]{1,0:T(8,128)(2,1)S(1)}, u32[]{:S(2)}, u32[]{:S(2)}) collective-permute-start(bf16[208,256]{1,0:T(8,128)(2,1)S(1)} %get-tuple-element.41), channel_id=1, source_target_pairs={{0,3},{1,2},{2,1},{3,0},{4,7},{5,6},{6,5},{7,4},{8,11},{9,10},{10,... | collective-permute-start | bytes 319496 | tf_op jit(solution)/shard_map/ppermute | solution.py:276
  13.9 1.5 %collective-permute-start.7 = (bf16[192,768]{1,0:T(8,128)(2,1)S(1)}, bf16[192,768]{1,0:T(8,128)(2,1)S(1)}, u32[]{:S(2)}, u32[]{:S(2)}) collective-permute-start(bf16[192,768]{1,0:T(8,128)(2,1)S(1)} %get-tuple-element.48), channel_id=1, source_target_pairs={{0,2},{1,3},{2,0},{3,1},{4,6},{5,7},{6,4},{7,5},{8,10},{9,11},{10,... | collective-permute-start | bytes 884744 | tf_op jit(solution)/shard_map/ppermute | solution.py:276
  15.4 1.3 %collective-permute-start.8 = (bf16[192,768]{1,0:T(8,128)(2,1)S(1)}, bf16[192,768]{1,0:T(8,128)(2,1)S(1)}, u32[]{:S(2)}, u32[]{:S(2)}) collective-permute-start(bf16[192,768]{1,0:T(8,128)(2,1)S(1)} %get-tuple-element.49), channel_id=1, source_target_pairs={{0,3},{1,2},{2,1},{3,0},{4,7},{5,6},{6,5},{7,4},{8,11},{9,10},{10,... | collective-permute-start | bytes 884744 | tf_op jit(solution)/shard_map/ppermute | solution.py:276
  16.7 7.4 %collective-permute-done.3.p3.refs_11_ = bf16[208,256]{1,0:T(8,128)(2,1)S(1)} collective-permute-done((bf16[208,256]{1,0:T(8,128)(2,1)S(1)}, bf16[208,256]{1,0:T(8,128)(2,1)S(1)}, u32[]{:S(2)}, u32[]{:S(2)}) %collective-permute-start.3) | collective-permute-done | bytes 106528 | tf_op jit(solution)/shard_map/ppermute | solution.py:276
  24.9 1.6 %collective-permute-start.9 = (bf16[128,768]{1,0:T(8,128)(2,1)S(1)}, bf16[128,768]{1,0:T(8,128)(2,1)S(1)}, u32[]{:S(2)}, u32[]{:S(2)}) collective-permute-start(bf16[128,768]{1,0:T(8,128)(2,1)S(1)} %get-tuple-element.51), channel_id=1, source_target_pairs={{0,8},{4,12},{8,0},{12,4},{16,24},{20,28},{24,16},{28,20},{1,9},{5... | collective-permute-start | bytes 589832 | tf_op jit(solution)/shard_map/ppermute | solution.py:276
  27.0 3.6 %collective-permute-done.7.p2 = bf16[192,768]{1,0:T(8,128)(2,1)S(1)} collective-permute-done((bf16[192,768]{1,0:T(8,128)(2,1)S(1)}, bf16[192,768]{1,0:T(8,128)(2,1)S(1)}, u32[]{:S(2)}, u32[]{:S(2)}) %collective-permute-start.7) | collective-permute-done | bytes 294944 | tf_op jit(solution)/shard_map/ppermute | solution.py:276
  30.6 1.5 %collective-permute-done.9.low_ref = bf16[128,768]{1,0:T(8,128)(2,1)S(1)} collective-permute-done((bf16[128,768]{1,0:T(8,128)(2,1)S(1)}, bf16[128,768]{1,0:T(8,128)(2,1)S(1)}, u32[]{:S(2)}, u32[]{:S(2)}) %collective-permute-start.9) | collective-permute-done | bytes 196640 | tf_op jit(solution)/shard_map/ppermute | solution.py:276
  32.1 2.1 %collective-permute-done.10.high_ref = bf16[128,768]{1,0:T(8,128)(2,1)S(1)} collective-permute-done((bf16[128,768]{1,0:T(8,128)(2,1)S(1)}, bf16[128,768]{1,0:T(8,128)(2,1)S(1)}, u32[]{:S(2)}, u32[]{:S(2)}) %collective-permute-start.10) | collective-permute-done | bytes 196640 | tf_op jit(solution)/shard_map/ppermute | solution.py:276
  34.8 2.7 %collective-permute-start.18 = (bf16[256,768]{1,0:T(8,128)(2,1)S(1)}, bf16[256,768]{1,0:T(8,128)(2,1)S(1)}, u32[]{:S(2)}, u32[]{:S(2)}) collective-permute-start(bf16[256,768]{1,0:T(8,128)(2,1)S(1)} %get-tuple-element.55._), channel_id=1, source_target_pairs={{0,16},{4,20},{8,24},{12,28},{16,0},{20,4},{24,8},{28,12},{1,17},{... | collective-permute-start | bytes 1179656 | tf_op jit(solution)/shard_map/ppermute | solution.py:276
  37.4 0.8 %shard_map.81 = (bf16[256,768]{1,0:T(8,128)(2,1)S(1)}, f32[256,768]{1,0:T(8,128)S(1)}, bf16[384,256]{1,0:T(8,128)(2,1)S(1)}, bf16[384,256]{1,0:T(8,128)(2,1)S(1)...) custom-call(bf16[192,768]{1,0:T(8,128)(2,1)S(1)} %get-tuple-element.46.p0, ...), custom_call_target="tpu_custom_call" | custom-call | tf_op jit(solution)/shard_map/pallas_call | solution.py:257
  38.3 1.6 %collective-permute-start.17 = (bf16[256,768]{1,0:T(8,128)(2,1)S(1)}, bf16[256,768]{1,0:T(8,128)(2,1)S(1)}, u32[]{:S(2)}, u32[]{:S(2)}) collective-permute-start(bf16[256,768]{1,0:T(8,128)(2,1)S(1)} %get-tuple-element.66), channel_id=1, source_target_pairs={{0,8},{4,12},{8,0},{12,4},{16,24},{20,28},{24,16},{28,20},{1,9},{5... | collective-permute-start | bytes 1179656 | tf_op jit(solution)/shard_map/ppermute | solution.py:276
  40.4 0.9 %collective-permute-done.11.refs_3_ = bf16[384,256]{1,0:T(8,128)(2,1)S(1)} collective-permute-done((bf16[384,256]{1,0:T(8,128)(2,1)S(1)}, bf16[384,256]{1,0:T(8,128)(2,1)S(1)}, u32[]{:S(2)}, u32[]{:S(2)}) %collective-permute-start.11) | collective-permute-done | bytes 196640 | tf_op jit(solution)/shard_map/ppermute | solution.py:276
  41.9 2.3 %shard_map.82 = (bf16[384,768]{1,0:T(8,128)(2,1)}, f32[96,128]{1,0:T(8,128)S(1)}, f32[96,128]{1,0:T(8,128)S(1)}, f32[96,128]{1,0:T(8,128)S(1)}, f32[96,128]{1,0:T(8,128)S(1)}) custom-call(bf16[384,256]{1,0:T(8,128)(2,1)S(1)} %get-tuple-element.43.refs_0_, bf16[384,256]{1,0:T(8,128)(2,1)S(1)} %collective-permute-done.5.refs_1_, ...), custom_call_target="tpu_custom_call" | custom-call | tf_op jit(solution)/shard_map/pallas_call | solution.py:257
  44.2 1.9 %collective-permute-start.14 = (f32[96,128]{1,0:T(8,128)S(1)}, f32[96,128]{1,0:T(8,128)S(1)}, u32[]{:S(2)}, u32[]{:S(2)}) collective-permute-start(f32[96,128]{1,0:T(8,128)S(1)} %get-tuple-element.62), channel_id=1, source_target_pairs={{0,1},{1,0},{2,3},{3,2},{4,5},{5,4},{6,7},{7,6},{8,9},{9,8},{10,11... | collective-permute-start | bytes 147464 | tf_op jit(solution)/shard_map/ppermute | solution.py:276
  46.1 1.5 %collective-permute-start.16 = (f32[96,128]{1,0:T(8,128)S(1)}, f32[96,128]{1,0:T(8,128)S(1)}, u32[]{:S(2)}, u32[]{:S(2)}) collective-permute-start(f32[96,128]{1,0:T(8,128)S(1)} %get-tuple-element.64), channel_id=1, source_target_pairs={{0,3},{1,2},{2,1},{3,0},{4,7},{5,6},{6,5},{7,4},{8,11},{9,10},{10,... | collective-permute-start | bytes 147464 | tf_op jit(solution)/shard_map/ppermute | solution.py:276
  48.3 2.3 %collective-permute-done.15.b2 = f32[96,128]{1,0:T(8,128)S(1)} collective-permute-done((f32[96,128]{1,0:T(8,128)S(1)}, f32[96,128]{1,0:T(8,128)S(1)}, u32[]{:S(2)}, u32[]{:S(2)}) %collective-permute-start.15) | collective-permute-done | bytes 49184 | tf_op jit(solution)/shard_map/ppermute | solution.py:276
  51.8 0.9 %collective-permute-done.18 = bf16[256,768]{1,0:T(8,128)(2,1)S(1)} collective-permute-done((bf16[256,768]{1,0:T(8,128)(2,1)S(1)}, bf16[256,768]{1,0:T(8,128)(2,1)S(1)}, u32[]{:S(2)}, u32[]{:S(2)}) %collective-permute-start.18) | collective-permute-done | bytes 393248 | tf_op jit(solution)/shard_map/ppermute | solution.py:276
  52.6 1.1 %collective-permute-done.17 = bf16[256,768]{1,0:T(8,128)(2,1)S(1)} collective-permute-done((bf16[256,768]{1,0:T(8,128)(2,1)S(1)}, bf16[256,768]{1,0:T(8,128)(2,1)S(1)}, u32[]{:S(2)}, u32[]{:S(2)}) %collective-permute-start.17) | collective-permute-done | bytes 393248 | tf_op jit(solution)/shard_map/ppermute | solution.py:276
  53.7 1.0 %add_bitcast_fusion = f32[1,256,768]{2,1,0:T(8,128)} fusion(bf16[256,768]{1,0:T(8,128)(2,1)S(1)} %collective-permute-done.18, f32[256,768]{1,0:T(8,128)S(1)} %get-tuple-element.65, bf16[256,768]{1,0:T(8,128)(2,1)S(1)} %collective-permute-done.17), kind=kLoop, calls=%fused_computation | loop fusion | flops 786432 | bytes 2359296 | tf_op jit(solution)/shard_map/broadcast_in_dim | solution.py:352
  (35 shorter events, 9.1 us)
Async XLA Ops:
  0.6 1.0 %copy-start.2 = (bf16[128,2048]{1,0:T(8,128)(2,1)S(1)}, bf16[128,2048]{1,0:T(8,128)(2,1)}, u32[]{:S(2)}) copy-start(bf16[128,2048]{1,0:T(8,128)(2,1)} %grad_hbm.1) | copy-start | bytes 1572868
  1.7 0.7 %copy-start.3 = (s32[128,8]{0,1:T(8,128)S(1)}, s32[128,8]{0,1:T(8,128)}, u32[]{:S(2)}) copy-start(s32[128,8]{0,1:T(8,128)} %param.6) | copy-start | bytes 12292
  3.3 1.7 %collective-permute-start = (bf16[144,1024]{1,0:T(8,128)(2,1)S(1)}, bf16[144,1024]{1,0:T(8,128)(2,1)S(1)}, u32[]{:S(2)}, u32[]{:S(2)}) collective-permute-start(bf16[144,1024]{1,0:T(8,128)(2,1)S(1)} %get-tuple-element.37), channel_id=1, source_target_pairs={{0,4},{4,0},{8,12},{12,8},{16,20},{20,16},{24,28},{28,24},{1,5},{5... | collective-permute-start | bytes 884744 | tf_op jit(solution)/shard_map/ppermute | solution.py:276
  5.0 1.1 %copy-start.1 = (bf16[1,384,768]{2,1,0:T(8,128)(2,1)S(1)}, bf16[1,384,768]{2,1,0:T(8,128)(2,1)}, u32[]{:S(2)}) copy-start(bf16[1,384,768]{2,1,0:T(8,128)(2,1)} %param.8) | copy-start | bytes 1769476
  6.8 17.4 %collective-permute-start.4 = (bf16[384,768]{1,0:T(8,128)(2,1)S(1)}, bf16[384,768]{1,0:T(8,128)(2,1)S(1)}, u32[]{:S(2)}, u32[]{:S(2)}) collective-permute-start(bf16[384,768]{1,0:T(8,128)(2,1)S(1)} %get-tuple-element.42.hidden_ref.refs_12_), channel_id=1, source_target_pairs={{0,4},{4,0},{8,12},{12,8},{16,20},{20,16},{24,28},{28,24},{1,5},{5... | collective-permute-start | bytes 1769480 | tf_op jit(solution)/shard_map/ppermute | solution.py:276
  7.2 6.7 %collective-permute-start.1 = (bf16[208,256]{1,0:T(8,128)(2,1)S(1)}, bf16[208,256]{1,0:T(8,128)(2,1)S(1)}, u32[]{:S(2)}, u32[]{:S(2)}) collective-permute-start(bf16[208,256]{1,0:T(8,128)(2,1)S(1)} %get-tuple-element.39), channel_id=1, source_target_pairs={{0,1},{1,0},{2,3},{3,2},{4,5},{5,4},{6,7},{7,6},{8,9},{9,8},{10,11... | collective-permute-start | bytes 319496 | tf_op jit(solution)/shard_map/ppermute | solution.py:276
  9.8 5.5 %collective-permute-start.2 = (bf16[208,256]{1,0:T(8,128)(2,1)S(1)}, bf16[208,256]{1,0:T(8,128)(2,1)S(1)}, u32[]{:S(2)}, u32[]{:S(2)}) collective-permute-start(bf16[208,256]{1,0:T(8,128)(2,1)S(1)} %get-tuple-element.40), channel_id=1, source_target_pairs={{0,2},{1,3},{2,0},{3,1},{4,6},{5,7},{6,4},{7,5},{8,10},{9,11},{10,... | collective-permute-start | bytes 319496 | tf_op jit(solution)/shard_map/ppermute | solution.py:276
  11.8 15.2 %collective-permute-start.6 = (bf16[192,768]{1,0:T(8,128)(2,1)S(1)}, bf16[192,768]{1,0:T(8,128)(2,1)S(1)}, u32[]{:S(2)}, u32[]{:S(2)}) collective-permute-start(bf16[192,768]{1,0:T(8,128)(2,1)S(1)} %get-tuple-element.47), channel_id=1, source_target_pairs={{0,1},{1,0},{2,3},{3,2},{4,5},{5,4},{6,7},{7,6},{8,9},{9,8},{10,11... | collective-permute-start | bytes 884744 | tf_op jit(solution)/shard_map/ppermute | solution.py:276
  12.4 11.7 %collective-permute-start.3 = (bf16[208,256]{1,0:T(8,128)(2,1)S(1)}, bf16[208,256]{1,0:T(8,128)(2,1)S(1)}, u32[]{:S(2)}, u32[]{:S(2)}) collective-permute-start(bf16[208,256]{1,0:T(8,128)(2,1)S(1)} %get-tuple-element.41), channel_id=1, source_target_pairs={{0,3},{1,2},{2,1},{3,0},{4,7},{5,6},{6,5},{7,4},{8,11},{9,10},{10,... | collective-permute-start | bytes 319496 | tf_op jit(solution)/shard_map/ppermute | solution.py:276
  13.9 16.8 %collective-permute-start.7 = (bf16[192,768]{1,0:T(8,128)(2,1)S(1)}, bf16[192,768]{1,0:T(8,128)(2,1)S(1)}, u32[]{:S(2)}, u32[]{:S(2)}) collective-permute-start(bf16[192,768]{1,0:T(8,128)(2,1)S(1)} %get-tuple-element.48), channel_id=1, source_target_pairs={{0,2},{1,3},{2,0},{3,1},{4,6},{5,7},{6,4},{7,5},{8,10},{9,11},{10,... | collective-permute-start | bytes 884744 | tf_op jit(solution)/shard_map/ppermute | solution.py:276
  15.4 15.3 %collective-permute-start.8 = (bf16[192,768]{1,0:T(8,128)(2,1)S(1)}, bf16[192,768]{1,0:T(8,128)(2,1)S(1)}, u32[]{:S(2)}, u32[]{:S(2)}) collective-permute-start(bf16[192,768]{1,0:T(8,128)(2,1)S(1)} %get-tuple-element.49), channel_id=1, source_target_pairs={{0,3},{1,2},{2,1},{3,0},{4,7},{5,6},{6,5},{7,4},{8,11},{9,10},{10,... | collective-permute-start | bytes 884744 | tf_op jit(solution)/shard_map/ppermute | solution.py:276
  24.9 17.0 %copy-start = (bf16[1,768,2048]{2,1,0:T(8,128)(2,1)S(1)}, bf16[1,768,2048]{2,1,0:T(8,128)(2,1)}, u32[]{:S(2)}) copy-start(bf16[1,768,2048]{2,1,0:T(8,128)(2,1)} %param.9) | copy-start | bytes 9437188
  24.9 7.2 %collective-permute-start.9 = (bf16[128,768]{1,0:T(8,128)(2,1)S(1)}, bf16[128,768]{1,0:T(8,128)(2,1)S(1)}, u32[]{:S(2)}, u32[]{:S(2)}) collective-permute-start(bf16[128,768]{1,0:T(8,128)(2,1)S(1)} %get-tuple-element.51), channel_id=1, source_target_pairs={{0,8},{4,12},{8,0},{12,4},{16,24},{20,28},{24,16},{28,20},{1,9},{5... | collective-permute-start | bytes 589832 | tf_op jit(solution)/shard_map/ppermute | solution.py:276
  26.6 7.7 %collective-permute-start.10 = (bf16[128,768]{1,0:T(8,128)(2,1)S(1)}, bf16[128,768]{1,0:T(8,128)(2,1)S(1)}, u32[]{:S(2)}, u32[]{:S(2)}) collective-permute-start(bf16[128,768]{1,0:T(8,128)(2,1)S(1)} %get-tuple-element.52), channel_id=1, source_target_pairs={{0,8},{4,12},{8,0},{12,4},{16,24},{20,28},{24,16},{28,20},{1,9},{5... | collective-permute-start | bytes 589832 | tf_op jit(solution)/shard_map/ppermute | solution.py:276
  27.0 13.4 %collective-permute-start.5 = (bf16[384,256]{1,0:T(8,128)(2,1)S(1)}, bf16[384,256]{1,0:T(8,128)(2,1)S(1)}, u32[]{:S(2)}, u32[]{:S(2)}) collective-permute-start(bf16[384,256]{1,0:T(8,128)(2,1)S(1)} %get-tuple-element.44), channel_id=1, source_target_pairs={{0,4},{4,0},{8,12},{12,8},{16,20},{20,16},{24,28},{28,24},{1,5},{5... | collective-permute-start | bytes 589832 | tf_op jit(solution)/shard_map/ppermute | solution.py:276
  34.8 17.9 %collective-permute-start.18 = (bf16[256,768]{1,0:T(8,128)(2,1)S(1)}, bf16[256,768]{1,0:T(8,128)(2,1)S(1)}, u32[]{:S(2)}, u32[]{:S(2)}) collective-permute-start(bf16[256,768]{1,0:T(8,128)(2,1)S(1)} %get-tuple-element.55._), channel_id=1, source_target_pairs={{0,16},{4,20},{8,24},{12,28},{16,0},{20,4},{24,8},{28,12},{1,17},{... | collective-permute-start | bytes 1179656 | tf_op jit(solution)/shard_map/ppermute | solution.py:276
  38.2 12.9 %copy-start.4 = (s32[128,8]{0,1:T(8,128)S(1)}, s32[128,8]{0,1:T(8,128)}, u32[]{:S(2)}) copy-start(s32[128,8]{0,1:T(8,128)} %param.6) | copy-start | bytes 12292
  38.3 15.4 %collective-permute-start.17 = (bf16[256,768]{1,0:T(8,128)(2,1)S(1)}, bf16[256,768]{1,0:T(8,128)(2,1)S(1)}, u32[]{:S(2)}, u32[]{:S(2)}) collective-permute-start(bf16[256,768]{1,0:T(8,128)(2,1)S(1)} %get-tuple-element.66), channel_id=1, source_target_pairs={{0,8},{4,12},{8,0},{12,4},{16,24},{20,28},{24,16},{28,20},{1,9},{5... | collective-permute-start | bytes 1179656 | tf_op jit(solution)/shard_map/ppermute | solution.py:276
  39.9 1.4 %collective-permute-start.11 = (bf16[384,256]{1,0:T(8,128)(2,1)S(1)}, bf16[384,256]{1,0:T(8,128)(2,1)S(1)}, u32[]{:S(2)}, u32[]{:S(2)}) collective-permute-start(bf16[384,256]{1,0:T(8,128)(2,1)S(1)} %get-tuple-element.54), channel_id=1, source_target_pairs={{0,4},{4,0},{8,12},{12,8},{16,20},{20,16},{24,28},{28,24},{1,5},{5... | collective-permute-start | bytes 589832 | tf_op jit(solution)/shard_map/ppermute | solution.py:276
  39.9 1.7 %collective-permute-start.12 = (bf16[384,256]{1,0:T(8,128)(2,1)S(1)}, bf16[384,256]{1,0:T(8,128)(2,1)S(1)}, u32[]{:S(2)}, u32[]{:S(2)}) collective-permute-start(bf16[384,256]{1,0:T(8,128)(2,1)S(1)} %get-tuple-element.57), channel_id=1, source_target_pairs={{0,4},{4,0},{8,12},{12,8},{16,20},{20,16},{24,28},{28,24},{1,5},{5... | collective-permute-start | bytes 589832 | tf_op jit(solution)/shard_map/ppermute | solution.py:276
  40.4 1.5 %collective-permute-start.13 = (bf16[384,256]{1,0:T(8,128)(2,1)S(1)}, bf16[384,256]{1,0:T(8,128)(2,1)S(1)}, u32[]{:S(2)}, u32[]{:S(2)}) collective-permute-start(bf16[384,256]{1,0:T(8,128)(2,1)S(1)} %get-tuple-element.59), channel_id=1, source_target_pairs={{0,4},{4,0},{8,12},{12,8},{16,20},{20,16},{24,28},{28,24},{1,5},{5... | collective-permute-start | bytes 589832 | tf_op jit(solution)/shard_map/ppermute | solution.py:276
  44.2 4.1 %collective-permute-start.14 = (f32[96,128]{1,0:T(8,128)S(1)}, f32[96,128]{1,0:T(8,128)S(1)}, u32[]{:S(2)}, u32[]{:S(2)}) collective-permute-start(f32[96,128]{1,0:T(8,128)S(1)} %get-tuple-element.62), channel_id=1, source_target_pairs={{0,1},{1,0},{2,3},{3,2},{4,5},{5,4},{6,7},{7,6},{8,9},{9,8},{10,11... | collective-permute-start | bytes 147464 | tf_op jit(solution)/shard_map/ppermute | solution.py:276
  46.1 4.5 %collective-permute-start.15 = (f32[96,128]{1,0:T(8,128)S(1)}, f32[96,128]{1,0:T(8,128)S(1)}, u32[]{:S(2)}, u32[]{:S(2)}) collective-permute-start(f32[96,128]{1,0:T(8,128)S(1)} %get-tuple-element.63), channel_id=1, source_target_pairs={{0,2},{1,3},{2,0},{3,1},{4,6},{5,7},{6,4},{7,5},{8,10},{9,11},{10,... | collective-permute-start | bytes 147464 | tf_op jit(solution)/shard_map/ppermute | solution.py:276
  46.1 5.0 %collective-permute-start.16 = (f32[96,128]{1,0:T(8,128)S(1)}, f32[96,128]{1,0:T(8,128)S(1)}, u32[]{:S(2)}, u32[]{:S(2)}) collective-permute-start(f32[96,128]{1,0:T(8,128)S(1)} %get-tuple-element.64), channel_id=1, source_target_pairs={{0,3},{1,2},{2,1},{3,0},{4,7},{5,6},{6,5},{7,4},{8,11},{9,10},{10,... | collective-permute-start | bytes 147464 | tf_op jit(solution)/shard_map/ppermute | solution.py:276
  (1 other events, 0.7 us)

commit v3 on v2

--- a/solution.py
+++ b/solution.py
@@ -67,51 +67,22 @@
     return lax.dot_general(a, b, (dims, ((), ())), preferred_element_type=F32)
 
 
-def swap_kernel(block, ids_hbm, gates_hbm, grad_hbm, send_ref, own_ref, marks_ref, ids_ref, gates_ref, sems):
+def swap_kernel(block, marks_in, grad_ref, send_ref, own_ref, marks_ref):
     _, core, _ = coordinates()
-    tokens = grad_hbm.shape[0]
-    count = own_ref.shape[1] // block
-    copies = [
-        pltpu.make_async_copy(ids_hbm, ids_ref, sems.at[0]),
-        pltpu.make_async_copy(gates_hbm, gates_ref, sems.at[1]),
-    ]
-    for i in range(count):
+    tokens = grad_ref.shape[0]
+    for i in range(own_ref.shape[1] // block):
         at = slice(i * block, (i + 1) * block)
-        for n, (side, ref) in enumerate(((1 - core, send_ref), (core, own_ref))):
+        for side, ref in ((1 - core, send_ref), (core, own_ref)):
             start = pl.multiple_of((2 * i + side) * block, block)
-            copies.append(
-                pltpu.make_async_copy(
-                    grad_hbm.at[:, pl.ds(start, block)],
-                    ref.at[pl.ds(0, tokens), at],
-                    sems.at[2 + 2 * i + n],
-                )
-            )
-    for copy in copies:
-        copy.start()
+            ref[:tokens, at] = grad_ref[:, pl.ds(start, block)]
+    marks = jnp.concatenate([marks_in[...], jnp.full((12, tokens), -1.0, F32)], axis=0)
+    marks_ref[...] = marks.astype(BF16)
     send_ref[tokens:, :] = jnp.zeros((16, send_ref.shape[1]), BF16)
-    copies[0].wait()
-    copies[1].wait()
-    ids = ids_ref[...]
-    gates = gates_ref[...].astype(F32)
-    experts = ids.shape[0] // 2
-    rows = []
-    for j in range(experts):
-        hit = ids == j * EXP_DEV
-        value = jnp.sum(jnp.where(hit, gates, 0.0), axis=0, keepdims=True)
-        live = jnp.sum(jnp.where(hit, 1.0, 0.0), axis=0, keepdims=True)
-        rows.append(jnp.where(live > 0.0, value, -1.0))
-    rows.append(jnp.full((marks_ref.shape[0] - experts, tokens), -1.0, F32))
-    marks = jnp.concatenate(rows, axis=0).astype(BF16)
-    marks_ref[...] = marks
-    send_ref[tokens:, :tokens] = marks
-    for copy in copies[2:]:
-        copy.wait()
-
-
-def gather_kernel(block, capacity, own_ref, marks_ref, other_ref, hidden_hbm, *outs):
-    first, (matches_ref, hidden_ref, scratch, sem) = outs[:-4], outs[-4:]
-    copy = pltpu.make_async_copy(hidden_hbm, hidden_ref, sem)
-    copy.start()
+    send_ref[tokens:, :tokens] = marks.astype(BF16)
+
+
+def gather_kernel(block, capacity, own_ref, marks_ref, other_ref, *outs):
+    first, (matches_ref, scratch) = outs[:-2], outs[-2:]
     chip, _, peer = coordinates()
     tokens = own_ref.shape[0]
     before = (
@@ -145,18 +116,23 @@
         both = jnp.where(row == 0, gate_rows[r][0], jnp.where(row == 1, gate_rows[r][1], 0.0))
         first[r][2 * capacity :, :] = jnp.zeros((16, first[r].shape[1]), BF16)
         first[r][2 * capacity :, :capacity] = both.astype(BF16)
-    copy.wait()
+
+
+def diagonal(capacity):
+    return lax.broadcasted_iota(jnp.int32, (capacity, 128), 0) == lax.broadcasted_iota(
+        jnp.int32, (capacity, 128), 1
+    )
 
 
 def gate_column(piece, g, capacity):
     row = piece[2 * capacity :, :128].astype(F32)[g : g + 1, :]
-    here = lax.broadcasted_iota(jnp.int32, (capacity, 128), 0) == lax.broadcasted_iota(
-        jnp.int32, (capacity, 128), 1
-    )
-    return jnp.sum(jnp.where(here, row, 0.0), axis=1, keepdims=True)
-
-
-def rest_kernel(block, capacity, chunks, own_ref, other_ref, matches_ref, *outs):
+    return jnp.sum(jnp.where(diagonal(capacity), row, 0.0), axis=1, keepdims=True)
+
+
+def rest_kernel(block, capacity, chunks, take, own_ref, other_ref, matches_ref, *outs):
+    if take:
+        outs[-1][...] = outs[0][...]
+        outs = outs[:-1]
     chip, _, _ = coordinates()
     tokens = own_ref.shape[0]
     for i, k in enumerate(chunks):
@@ -212,7 +188,7 @@
 def last_kernel(capacity, p0, p1, p2, p3, scaled_ref, _, part2_ref, part3_ref, own2, cross2, own3, cross3, all_ref):
     for i, (part, own, cross) in enumerate(((part2_ref, own2, cross2), (part3_ref, own3, cross3))):
         block = own.shape[1]
-        at = slice((i + 1) * block, (i + 2) * block)
+        at = slice(i * block, (i + 1) * block)
         split_rows((p0, p1, p2, p3), at, capacity, all_ref.at[i], own, cross)
         part[...] = dot(all_ref[i], scaled_ref[...], ((0,), (0,))).astype(part.dtype)
 
@@ -232,7 +208,8 @@
         here = update[r * capacity : (r + 1) * capacity, :]
         out_ref[source, :] = (gate_column(piece, 0, capacity) * here).astype(BF16)
         pair = jnp.sum(hidden_ref[source, :].astype(F32) * here, axis=1, keepdims=True)
-        pairs[r][...] = jnp.broadcast_to(pair, (capacity, 128))
+        line = jnp.sum(jnp.where(diagonal(capacity), pair, 0.0), axis=0, keepdims=True)
+        pairs[r][...] = jnp.broadcast_to(line, (8, 128))
 
 
 def gate_kernel(ids_ref, matches_ref, b0, b1, b2, b3, out_ref):
@@ -240,9 +217,11 @@
     ids = ids_ref[...]
     total = jnp.zeros(ids.shape, F32)
     for r, back in enumerate((b0, b1, b2, b3)):
-        at_token = jnp.sum(
-            jnp.where(matches_ref[0, r].astype(F32) > 0.0, back[...], 0.0), axis=0, keepdims=True
+        match = matches_ref[0, r].astype(F32)
+        column = jnp.sum(
+            jnp.where(diagonal(match.shape[0]), back[0:1, :], 0.0), axis=1, keepdims=True
         )
+        at_token = jnp.sum(jnp.where(match > 0.0, column, 0.0), axis=0, keepdims=True)
         total = jnp.where(ids == (peer ^ r) * EXP_DEV, at_token, total)
     out_ref[...] = total
 
@@ -288,36 +267,33 @@
     to_peer = [lambda x: x] + [over("expert", peers, r) for r in range(1, peers)]
     ids_t, gates_t = expert_ids.T, gate_weights.T
 
+    hit = ids_t == EXP_DEV * jnp.arange(peers, dtype=jnp.int32)[:, None, None]
+    marks = jnp.max(jnp.where(hit, gates_t, -jnp.ones((), BF16)), axis=1).astype(F32)
     send, own, marks = call(
         functools.partial(swap_kernel, block),
         [arr((tokens + 16, half), BF16), arr((tokens, half), BF16), arr((16, tokens), BF16)],
-        specs=[HBM] * 3,
-        scratch=[
-            pltpu.VMEM((TOP, tokens), jnp.int32),
-            pltpu.VMEM((TOP, tokens), BF16),
-            pltpu.SemaphoreType.DMA((2 + groups,)),
-        ],
-    )(ids_t, gates_t, grad_out)
+    )(marks, grad_out)
     other = core_swap(send)
-    *first, matches, hidden = call(
+    *first, matches = call(
         functools.partial(gather_kernel, block, capacity),
         [arr((2 * capacity + 16, block), BF16)] * peers
-        + [arr((2, peers, capacity, tokens), BF16), arr((slots, units), BF16)],
-        specs=[VMEM] * 3 + [HBM],
-        scratch=[pltpu.VMEM((4, 16, tokens), F32), pltpu.SemaphoreType.DMA],
-    )(own, marks, other, hidden)
+        + [arr((2, peers, capacity, tokens), BF16)],
+        scratch=[pltpu.VMEM((4, 16, tokens), F32)],
+    )(own, marks, other)
     first = [to_peer[r](first[r]) for r in range(peers)]
     other_hidden = core_swap(hidden)
 
-    def later(chunks, *after):
+    def later(chunks, *after, take=False):
         pieces = call(
-            functools.partial(rest_kernel, block, capacity, chunks),
-            [arr((2 * capacity, len(chunks) * block), BF16)] * peers,
-            specs=[VMEM] * 3 + [ANY] * len(after),
+            functools.partial(rest_kernel, block, capacity, chunks, take),
+            [arr((2 * capacity, len(chunks) * block), BF16)] * peers
+            + ([arr(after[0].shape, BF16)] if take else []),
+            specs=[VMEM] * 3 + [VMEM if take else ANY] + [ANY] * (len(after) - 1),
         )(own, other, matches, *after)
-        return [to_peer[r](pieces[r]) for r in range(peers)]
-
-    rest = later((1, 2, 3), matches)
+        sent = [to_peer[r](pieces[r]) for r in range(peers)]
+        return (sent, pieces[peers]) if take else sent
+
+    one, hidden = later((1,), hidden, take=True)
     stack = (2 * slots, block)
     mine = arr((slots, block), BF16)
     low, high, scaled, own0, cross0 = call(
@@ -325,12 +301,13 @@
         [arr((block // 2, units), BF16)] * 2 + [arr((2 * slots, units), BF16), mine, mine],
         scratch=[pltpu.VMEM(stack, BF16)],
     )(*first, hidden, other_hidden)
+    rest = later((2, 3), low)
     low, high = near(low), near(high)
     summed, own1, cross1 = call(
         functools.partial(second_kernel, capacity),
         [arr((block, units), BF16), mine, mine],
         scratch=[pltpu.VMEM(stack, BF16)],
-    )(*rest, scaled, low, high)
+    )(*one, scaled, low, high)
     come1 = far(summed)
     part2, part3, own2, cross2, own3, cross3 = call(
         functools.partial(last_kernel, capacity),
@@ -344,7 +321,7 @@
         rows += [own_k, core_swap(cross_k)]
     grad_hidden, *pairs = call(
         functools.partial(update_kernel, capacity),
-        [arr((slots, units), BF16)] + [arr((capacity, 128), F32)] * peers,
+        [arr((slots, units), BF16)] + [arr((8, 128), F32)] * peers,
     )(*rows, *first, hidden, weight)
     back = [to_peer[r](pairs[r]) for r in range(peers)]
     gate_grad = call(gate_kernel, arr((TOP, tokens), F32))(ids_t, matches, *back).T

time: 55 us -> 49.9 us (0.907)
  waiting for transfers between devices: 22.7 us -> 14.1 us
  starting transfers between devices: 20.4 us -> 24.4 us
  local copies, waits for them, and re-layouts: 3.48 us -> 2.11 us
  other arithmetic: 0.98 us -> 1.78 us
    ppermute x19 -> x22, waiting for transfers between devices: 22.7 us -> 14.1 us  [over(): return lambda x: lax.ppermute(x, axis, pairs)]
    ppermute x19 -> x22, starting transfers between devices: 20.4 us -> 24.4 us  [over(): return lambda x: lax.ppermute(x, axis, pairs)]
    unnamed x12 -> x8, local copies, waits for them, and re-layouts: 3.48 us -> 2.11 us
    reduce_max x0 -> x1, other arithmetic: none -> 0.78 us  [per_device(): jnp.max(jnp.where(hit, gates_t, -jnp.ones((), BF16)), axis=1).astype(F32)]
    pallas_call x8 -> x9, Pallas kernels: 6.39 us -> 6.52 us  [run(): pl.pallas_call(kernel, out_shape=outs, in_specs=specs or [VMEM] * len(arg...]
  transfers between devices with their start and end apart: 19 -> 22, of which waited for: 13 -> 13; matrix products, arithmetic and copies ran while one was open for 0% -> 2% of each run, Pallas kernels for 10% -> 13%
where the time goes in v3:
time: 49.9 us; the launch traced here: 49.7 us
  starting transfers between devices  24.4 us (49%)
  waiting for transfers between devices  14.1 us (28%)
  Pallas kernels  6.52 us (13%)
  local copies, waits for them, and re-layouts  2.11 us (4%)
  other arithmetic  1.78 us (4%)
  between operations  0.74 us (1%)
    ppermute x22, starting transfers between devices, over(): return lambda x: lax.ppermute(x, axis, pairs)  24.4 us
    ppermute x22, waiting for transfers between devices, over(): return lambda x: lax.ppermute(x, axis, pairs)  14.1 us
    pallas_call x9, Pallas kernels, run(): pl.pallas_call(kernel, out_shape=outs, in_specs=specs or [VMEM] * len(arg...  6.52 us
    unnamed x8, local copies, waits for them, and re-layouts  2.11 us
  transfers between devices with their start and end apart: 22, of which 13 were waited for; matrix products, arithmetic and copies ran while one was open for 2% of the time, Pallas kernels for 13%

profile of v3, /device:TPU:0, one launch (start us, length us, event | category | flops | bytes accessed | tf_op | source)
XLA Modules:
  0.0 49.7 jit_solution(8030561452890908136)
XLA Ops:
  2.0 1.0 %copy-done.2 = bf16[128,2048]{1,0:T(8,128)(2,1)S(1)} copy-done((bf16[128,2048]{1,0:T(8,128)(2,1)S(1)}, bf16[128,2048]{1,0:T(8,128)(2,1)}, u32[]{:S(2)}) %copy-start.2) | copy-done | bytes 524312
  3.2 1.5 %collective-permute-done.other_ref = bf16[144,1024]{1,0:T(8,128)(2,1)S(1)} collective-permute-done((bf16[144,1024]{1,0:T(8,128)(2,1)S(1)}, bf16[144,1024]{1,0:T(8,128)(2,1)S(1)}, u32[]{:S(2)}, u32[]{:S(2)}) %collective-permute-start) | collective-permute-done | bytes 294944 | tf_op jit(solution)/shard_map/ppermute | solution.py:255
  5.3 2.7 %collective-permute-start.1 = (bf16[208,256]{1,0:T(8,128)(2,1)S(1)}, bf16[208,256]{1,0:T(8,128)(2,1)S(1)}, u32[]{:S(2)}, u32[]{:S(2)}) collective-permute-start(bf16[208,256]{1,0:T(8,128)(2,1)S(1)} %get-tuple-element.43), channel_id=1, source_target_pairs={{0,1},{1,0},{2,3},{3,2},{4,5},{5,4},{6,7},{7,6},{8,9},{9,8},{10,11... | collective-permute-start | bytes 319496 | tf_op jit(solution)/shard_map/ppermute | solution.py:255
  8.0 1.5 %collective-permute-start.2 = (bf16[208,256]{1,0:T(8,128)(2,1)S(1)}, bf16[208,256]{1,0:T(8,128)(2,1)S(1)}, u32[]{:S(2)}, u32[]{:S(2)}) collective-permute-start(bf16[208,256]{1,0:T(8,128)(2,1)S(1)} %get-tuple-element.44), channel_id=1, source_target_pairs={{0,2},{1,3},{2,0},{3,1},{4,6},{5,7},{6,4},{7,5},{8,10},{9,11},{10,... | collective-permute-start | bytes 319496 | tf_op jit(solution)/shard_map/ppermute | solution.py:255
  9.5 1.1 %copy-done.1 = bf16[1,384,768]{2,1,0:T(8,128)(2,1)S(1)} copy-done((bf16[1,384,768]{2,1,0:T(8,128)(2,1)S(1)}, bf16[1,384,768]{2,1,0:T(8,128)(2,1)}, u32[]{:S(2)}) %copy-start.1) | copy-done | bytes 589848
  10.9 2.0 %collective-permute-start.6 = (bf16[192,256]{1,0:T(8,128)(2,1)S(1)}, bf16[192,256]{1,0:T(8,128)(2,1)S(1)}, u32[]{:S(2)}, u32[]{:S(2)}) collective-permute-start(bf16[192,256]{1,0:T(8,128)(2,1)S(1)} %get-tuple-element.51), channel_id=1, source_target_pairs={{0,1},{1,0},{2,3},{3,2},{4,5},{5,4},{6,7},{7,6},{8,9},{9,8},{10,11... | collective-permute-start | bytes 294920 | tf_op jit(solution)/shard_map/ppermute | solution.py:255
  12.9 1.5 %collective-permute-start.7 = (bf16[192,256]{1,0:T(8,128)(2,1)S(1)}, bf16[192,256]{1,0:T(8,128)(2,1)S(1)}, u32[]{:S(2)}, u32[]{:S(2)}) collective-permute-start(bf16[192,256]{1,0:T(8,128)(2,1)S(1)} %get-tuple-element.52), channel_id=1, source_target_pairs={{0,2},{1,3},{2,0},{3,1},{4,6},{5,7},{6,4},{7,5},{8,10},{9,11},{10,... | collective-permute-start | bytes 294920 | tf_op jit(solution)/shard_map/ppermute | solution.py:255
  14.6 1.9 %collective-permute-start.8 = (bf16[192,256]{1,0:T(8,128)(2,1)S(1)}, bf16[192,256]{1,0:T(8,128)(2,1)S(1)}, u32[]{:S(2)}, u32[]{:S(2)}) collective-permute-start(bf16[192,256]{1,0:T(8,128)(2,1)S(1)} %get-tuple-element.53), channel_id=1, source_target_pairs={{0,3},{1,2},{2,1},{3,0},{4,7},{5,6},{6,5},{7,4},{8,11},{9,10},{10,... | collective-permute-start | bytes 294920 | tf_op jit(solution)/shard_map/ppermute | solution.py:255
  17.4 1.6 %collective-permute-start.10 = (bf16[128,768]{1,0:T(8,128)(2,1)S(1)}, bf16[128,768]{1,0:T(8,128)(2,1)S(1)}, u32[]{:S(2)}, u32[]{:S(2)}) collective-permute-start(bf16[128,768]{1,0:T(8,128)(2,1)S(1)} %get-tuple-element.56), channel_id=1, source_target_pairs={{0,8},{4,12},{8,0},{12,4},{16,24},{20,28},{24,16},{28,20},{1,9},{5... | collective-permute-start | bytes 589832 | tf_op jit(solution)/shard_map/ppermute | solution.py:255
  19.8 2.0 %collective-permute-start.12 = (bf16[192,512]{1,0:T(8,128)(2,1)S(1)}, bf16[192,512]{1,0:T(8,128)(2,1)S(1)}, u32[]{:S(2)}, u32[]{:S(2)}) collective-permute-start(bf16[192,512]{1,0:T(8,128)(2,1)S(1)} %get-tuple-element.60), channel_id=1, source_target_pairs={{0,1},{1,0},{2,3},{3,2},{4,5},{5,4},{6,7},{7,6},{8,9},{9,8},{10,11... | collective-permute-start | bytes 589832 | tf_op jit(solution)/shard_map/ppermute | solution.py:255
  21.9 1.5 %collective-permute-start.14 = (bf16[192,512]{1,0:T(8,128)(2,1)S(1)}, bf16[192,512]{1,0:T(8,128)(2,1)S(1)}, u32[]{:S(2)}, u32[]{:S(2)}) collective-permute-start(bf16[192,512]{1,0:T(8,128)(2,1)S(1)} %get-tuple-element.62), channel_id=1, source_target_pairs={{0,3},{1,2},{2,1},{3,0},{4,7},{5,6},{6,5},{7,4},{8,11},{9,10},{10,... | collective-permute-start | bytes 589832 | tf_op jit(solution)/shard_map/ppermute | solution.py:255
  23.6 2.1 %collective-permute-done.9.low_ref = bf16[128,768]{1,0:T(8,128)(2,1)S(1)} collective-permute-done((bf16[128,768]{1,0:T(8,128)(2,1)S(1)}, bf16[128,768]{1,0:T(8,128)(2,1)S(1)}, u32[]{:S(2)}, u32[]{:S(2)}) %collective-permute-start.9) | collective-permute-done | bytes 196640 | tf_op jit(solution)/shard_map/ppermute | solution.py:255
  26.3 1.2 %collective-permute-done.12.p1 = bf16[192,512]{1,0:T(8,128)(2,1)S(1)} collective-permute-done((bf16[192,512]{1,0:T(8,128)(2,1)S(1)}, bf16[192,512]{1,0:T(8,128)(2,1)S(1)}, u32[]{:S(2)}, u32[]{:S(2)}) %collective-permute-start.12) | collective-permute-done | bytes 196640 | tf_op jit(solution)/shard_map/ppermute | solution.py:255
  27.4 2.7 %collective-permute-done.13.p2 = bf16[192,512]{1,0:T(8,128)(2,1)S(1)} collective-permute-done((bf16[192,512]{1,0:T(8,128)(2,1)S(1)}, bf16[192,512]{1,0:T(8,128)(2,1)S(1)}, u32[]{:S(2)}, u32[]{:S(2)}) %collective-permute-start.13) | collective-permute-done | bytes 196640 | tf_op jit(solution)/shard_map/ppermute | solution.py:255
  30.1 0.8 %shard_map.82 = (bf16[256,768]{1,0:T(8,128)(2,1)S(1)}, f32[256,768]{1,0:T(8,128)S(1)}, bf16[384,256]{1,0:T(8,128)(2,1)S(1)}, bf16[384,256]{1,0:T(8,128)(2,1)S(1)...) custom-call(bf16[192,512]{1,0:T(8,128)(2,1)S(1)} %get-tuple-element.59.p0, ...), custom_call_target="tpu_custom_call" | custom-call | tf_op jit(solution)/shard_map/pallas_call | solution.py:236
  30.9 1.7 %collective-permute-start.20 = (bf16[256,768]{1,0:T(8,128)(2,1)S(1)}, bf16[256,768]{1,0:T(8,128)(2,1)S(1)}, u32[]{:S(2)}, u32[]{:S(2)}) collective-permute-start(bf16[256,768]{1,0:T(8,128)(2,1)S(1)} %get-tuple-element.74), channel_id=1, source_target_pairs={{0,8},{4,12},{8,0},{12,4},{16,24},{20,28},{24,16},{28,20},{1,9},{5... | collective-permute-start | bytes 1179656 | tf_op jit(solution)/shard_map/ppermute | solution.py:255
  32.7 2.6 %collective-permute-start.21 = (bf16[256,768]{1,0:T(8,128)(2,1)S(1)}, bf16[256,768]{1,0:T(8,128)(2,1)S(1)}, u32[]{:S(2)}, u32[]{:S(2)}) collective-permute-start(bf16[256,768]{1,0:T(8,128)(2,1)S(1)} %get-tuple-element.63._), channel_id=1, source_target_pairs={{0,16},{4,20},{8,24},{12,28},{16,0},{20,4},{24,8},{28,12},{1,17},{... | collective-permute-start | bytes 1179656 | tf_op jit(solution)/shard_map/ppermute | solution.py:255
  35.8 0.9 %collective-permute-done.11.refs_3_ = bf16[384,256]{1,0:T(8,128)(2,1)S(1)} collective-permute-done((bf16[384,256]{1,0:T(8,128)(2,1)S(1)}, bf16[384,256]{1,0:T(8,128)(2,1)S(1)}, u32[]{:S(2)}, u32[]{:S(2)}) %collective-permute-start.11) | collective-permute-done | bytes 196640 | tf_op jit(solution)/shard_map/ppermute | solution.py:255
  37.3 2.4 %shard_map.83 = (bf16[384,768]{1,0:T(8,128)(2,1)}, f32[8,128]{1,0:T(8,128)S(1)}, f32[8,128]{1,0:T(8,128)S(1)}, f32[8,128]{1,0:T(8,128)S(1)}, f32[8,128]{1,0:T(8,128)S(1)}) custom-call(bf16[384,256]{1,0:T(8,128)(2,1)S(1)} %get-tuple-element.48.refs_0_, bf16[384,256]{1,0:T(8,128)(2,1)S(1)} %collective-permute-done.5.refs_1_, ...), custom_call_target="tpu_custom_call" | custom-call | tf_op jit(solution)/shard_map/pallas_call | solution.py:236
  40.0 1.4 %collective-permute-start.18 = (f32[8,128]{1,0:T(8,128)S(1)}, f32[8,128]{1,0:T(8,128)S(1)}, u32[]{:S(2)}, u32[]{:S(2)}) collective-permute-start(f32[8,128]{1,0:T(8,128)S(1)} %get-tuple-element.71), channel_id=1, source_target_pairs={{0,2},{1,3},{2,0},{3,1},{4,6},{5,7},{6,4},{7,5},{8,10},{9,11},{10,... | collective-permute-start | bytes 12296 | tf_op jit(solution)/shard_map/ppermute | solution.py:255
  41.4 1.8 %collective-permute-start.19 = (f32[8,128]{1,0:T(8,128)S(1)}, f32[8,128]{1,0:T(8,128)S(1)}, u32[]{:S(2)}, u32[]{:S(2)}) collective-permute-start(f32[8,128]{1,0:T(8,128)S(1)} %get-tuple-element.72), channel_id=1, source_target_pairs={{0,3},{1,2},{2,1},{3,0},{4,7},{5,6},{6,5},{7,4},{8,11},{9,10},{10,... | collective-permute-start | bytes 12296 | tf_op jit(solution)/shard_map/ppermute | solution.py:255
  43.6 2.3 %collective-permute-done.19.b3 = f32[8,128]{1,0:T(8,128)S(1)} collective-permute-done((f32[8,128]{1,0:T(8,128)S(1)}, f32[8,128]{1,0:T(8,128)S(1)}, u32[]{:S(2)}, u32[]{:S(2)}) %collective-permute-start.19) | collective-permute-done | bytes 4128 | tf_op jit(solution)/shard_map/ppermute | solution.py:255
  46.6 2.0 %collective-permute-done.21 = bf16[256,768]{1,0:T(8,128)(2,1)S(1)} collective-permute-done((bf16[256,768]{1,0:T(8,128)(2,1)S(1)}, bf16[256,768]{1,0:T(8,128)(2,1)S(1)}, u32[]{:S(2)}, u32[]{:S(2)}) %collective-permute-start.21) | collective-permute-done | bytes 393248 | tf_op jit(solution)/shard_map/ppermute | solution.py:255
  48.7 1.0 %add_bitcast_fusion = f32[1,256,768]{2,1,0:T(8,128)} fusion(bf16[256,768]{1,0:T(8,128)(2,1)S(1)} %collective-permute-done.21, f32[256,768]{1,0:T(8,128)S(1)} %get-tuple-element.73, bf16[256,768]{1,0:T(8,128)(2,1)S(1)} %collective-permute-done.20), kind=kLoop, calls=%fused_computation | loop fusion | flops 786432 | bytes 2359296 | tf_op jit(solution)/shard_map/broadcast_in_dim | solution.py:329
  (41 shorter events, 7.6 us)
Async XLA Ops:
  0.6 15.9 %collective-permute-start.4 = (bf16[384,768]{1,0:T(8,128)(2,1)}, bf16[384,768]{1,0:T(8,128)(2,1)S(1)}, u32[]{:S(2)}, u32[]{:S(2)}) collective-permute-start(bf16[384,768]{1,0:T(8,128)(2,1)} %bitcast.9), channel_id=1, source_target_pairs={{0,4},{4,0},{8,12},{12,8},{16,20},{20,16},{24,28},{28,24},{1,5},{5... | collective-permute-start | bytes 1769480 | tf_op jit(solution)/shard_map/ppermute | solution.py:255
  3.1 1.6 %collective-permute-start = (bf16[144,1024]{1,0:T(8,128)(2,1)S(1)}, bf16[144,1024]{1,0:T(8,128)(2,1)S(1)}, u32[]{:S(2)}, u32[]{:S(2)}) collective-permute-start(bf16[144,1024]{1,0:T(8,128)(2,1)S(1)} %get-tuple-element.41), channel_id=1, source_target_pairs={{0,4},{4,0},{8,12},{12,8},{16,20},{20,16},{24,28},{28,24},{1,5},{5... | collective-permute-start | bytes 884744 | tf_op jit(solution)/shard_map/ppermute | solution.py:255
  5.3 7.6 %collective-permute-start.1 = (bf16[208,256]{1,0:T(8,128)(2,1)S(1)}, bf16[208,256]{1,0:T(8,128)(2,1)S(1)}, u32[]{:S(2)}, u32[]{:S(2)}) collective-permute-start(bf16[208,256]{1,0:T(8,128)(2,1)S(1)} %get-tuple-element.43), channel_id=1, source_target_pairs={{0,1},{1,0},{2,3},{3,2},{4,5},{5,4},{6,7},{7,6},{8,9},{9,8},{10,11... | collective-permute-start | bytes 319496 | tf_op jit(solution)/shard_map/ppermute | solution.py:255
  8.0 6.6 %collective-permute-start.2 = (bf16[208,256]{1,0:T(8,128)(2,1)S(1)}, bf16[208,256]{1,0:T(8,128)(2,1)S(1)}, u32[]{:S(2)}, u32[]{:S(2)}) collective-permute-start(bf16[208,256]{1,0:T(8,128)(2,1)S(1)} %get-tuple-element.44), channel_id=1, source_target_pairs={{0,2},{1,3},{2,0},{3,1},{4,6},{5,7},{6,4},{7,5},{8,10},{9,11},{10,... | collective-permute-start | bytes 319496 | tf_op jit(solution)/shard_map/ppermute | solution.py:255
  9.5 7.0 %collective-permute-start.3 = (bf16[208,256]{1,0:T(8,128)(2,1)S(1)}, bf16[208,256]{1,0:T(8,128)(2,1)S(1)}, u32[]{:S(2)}, u32[]{:S(2)}) collective-permute-start(bf16[208,256]{1,0:T(8,128)(2,1)S(1)} %get-tuple-element.45), channel_id=1, source_target_pairs={{0,3},{1,2},{2,1},{3,0},{4,7},{5,6},{6,5},{7,4},{8,11},{9,10},{10,... | collective-permute-start | bytes 319496 | tf_op jit(solution)/shard_map/ppermute | solution.py:255
  10.9 8.9 %collective-permute-start.6 = (bf16[192,256]{1,0:T(8,128)(2,1)S(1)}, bf16[192,256]{1,0:T(8,128)(2,1)S(1)}, u32[]{:S(2)}, u32[]{:S(2)}) collective-permute-start(bf16[192,256]{1,0:T(8,128)(2,1)S(1)} %get-tuple-element.51), channel_id=1, source_target_pairs={{0,1},{1,0},{2,3},{3,2},{4,5},{5,4},{6,7},{7,6},{8,9},{9,8},{10,11... | collective-permute-start | bytes 294920 | tf_op jit(solution)/shard_map/ppermute | solution.py:255
  12.9 9.0 %collective-permute-start.7 = (bf16[192,256]{1,0:T(8,128)(2,1)S(1)}, bf16[192,256]{1,0:T(8,128)(2,1)S(1)}, u32[]{:S(2)}, u32[]{:S(2)}) collective-permute-start(bf16[192,256]{1,0:T(8,128)(2,1)S(1)} %get-tuple-element.52), channel_id=1, source_target_pairs={{0,2},{1,3},{2,0},{3,1},{4,6},{5,7},{6,4},{7,5},{8,10},{9,11},{10,... | collective-permute-start | bytes 294920 | tf_op jit(solution)/shard_map/ppermute | solution.py:255
  14.6 7.3 %collective-permute-start.8 = (bf16[192,256]{1,0:T(8,128)(2,1)S(1)}, bf16[192,256]{1,0:T(8,128)(2,1)S(1)}, u32[]{:S(2)}, u32[]{:S(2)}) collective-permute-start(bf16[192,256]{1,0:T(8,128)(2,1)S(1)} %get-tuple-element.53), channel_id=1, source_target_pairs={{0,3},{1,2},{2,1},{3,0},{4,7},{5,6},{6,5},{7,4},{8,11},{9,10},{10,... | collective-permute-start | bytes 294920 | tf_op jit(solution)/shard_map/ppermute | solution.py:255
  16.6 20.7 %copy-start = (bf16[1,768,2048]{2,1,0:T(8,128)(2,1)S(1)}, bf16[1,768,2048]{2,1,0:T(8,128)(2,1)}, u32[]{:S(2)}) copy-start(bf16[1,768,2048]{2,1,0:T(8,128)(2,1)} %param.9) | copy-start | bytes 9437188
  17.4 6.3 %collective-permute-start.10 = (bf16[128,768]{1,0:T(8,128)(2,1)S(1)}, bf16[128,768]{1,0:T(8,128)(2,1)S(1)}, u32[]{:S(2)}, u32[]{:S(2)}) collective-permute-start(bf16[128,768]{1,0:T(8,128)(2,1)S(1)} %get-tuple-element.56), channel_id=1, source_target_pairs={{0,8},{4,12},{8,0},{12,4},{16,24},{20,28},{24,16},{28,20},{1,9},{5... | collective-permute-start | bytes 589832 | tf_op jit(solution)/shard_map/ppermute | solution.py:255
  19.0 6.7 %collective-permute-start.9 = (bf16[128,768]{1,0:T(8,128)(2,1)S(1)}, bf16[128,768]{1,0:T(8,128)(2,1)S(1)}, u32[]{:S(2)}, u32[]{:S(2)}) collective-permute-start(bf16[128,768]{1,0:T(8,128)(2,1)S(1)} %get-tuple-element.55.outs_0_), channel_id=1, source_target_pairs={{0,8},{4,12},{8,0},{12,4},{16,24},{20,28},{24,16},{28,20},{1,9},{5... | collective-permute-start | bytes 589832 | tf_op jit(solution)/shard_map/ppermute | solution.py:255
  19.8 7.6 %collective-permute-start.12 = (bf16[192,512]{1,0:T(8,128)(2,1)S(1)}, bf16[192,512]{1,0:T(8,128)(2,1)S(1)}, u32[]{:S(2)}, u32[]{:S(2)}) collective-permute-start(bf16[192,512]{1,0:T(8,128)(2,1)S(1)} %get-tuple-element.60), channel_id=1, source_target_pairs={{0,1},{1,0},{2,3},{3,2},{4,5},{5,4},{6,7},{7,6},{8,9},{9,8},{10,11... | collective-permute-start | bytes 589832 | tf_op jit(solution)/shard_map/ppermute | solution.py:255
  21.9 8.2 %collective-permute-start.13 = (bf16[192,512]{1,0:T(8,128)(2,1)S(1)}, bf16[192,512]{1,0:T(8,128)(2,1)S(1)}, u32[]{:S(2)}, u32[]{:S(2)}) collective-permute-start(bf16[192,512]{1,0:T(8,128)(2,1)S(1)} %get-tuple-element.61), channel_id=1, source_target_pairs={{0,2},{1,3},{2,0},{3,1},{4,6},{5,7},{6,4},{7,5},{8,10},{9,11},{10,... | collective-permute-start | bytes 589832 | tf_op jit(solution)/shard_map/ppermute | solution.py:255
  21.9 8.2 %collective-permute-start.14 = (bf16[192,512]{1,0:T(8,128)(2,1)S(1)}, bf16[192,512]{1,0:T(8,128)(2,1)S(1)}, u32[]{:S(2)}, u32[]{:S(2)}) collective-permute-start(bf16[192,512]{1,0:T(8,128)(2,1)S(1)} %get-tuple-element.62), channel_id=1, source_target_pairs={{0,3},{1,2},{2,1},{3,0},{4,7},{5,6},{6,5},{7,4},{8,11},{9,10},{10,... | collective-permute-start | bytes 589832 | tf_op jit(solution)/shard_map/ppermute | solution.py:255
  23.6 12.1 %collective-permute-start.5 = (bf16[384,256]{1,0:T(8,128)(2,1)S(1)}, bf16[384,256]{1,0:T(8,128)(2,1)S(1)}, u32[]{:S(2)}, u32[]{:S(2)}) collective-permute-start(bf16[384,256]{1,0:T(8,128)(2,1)S(1)} %get-tuple-element.49), channel_id=1, source_target_pairs={{0,4},{4,0},{8,12},{12,8},{16,20},{20,16},{24,28},{28,24},{1,5},{5... | collective-permute-start | bytes 589832 | tf_op jit(solution)/shard_map/ppermute | solution.py:255
  30.9 15.0 %copy-start.3 = (s32[128,8]{0,1:T(8,128)S(1)}, s32[128,8]{0,1:T(8,128)}, u32[]{:S(2)}) copy-start(s32[128,8]{0,1:T(8,128)} %param.6) | copy-start | bytes 12292
  30.9 15.7 %collective-permute-start.20 = (bf16[256,768]{1,0:T(8,128)(2,1)S(1)}, bf16[256,768]{1,0:T(8,128)(2,1)S(1)}, u32[]{:S(2)}, u32[]{:S(2)}) collective-permute-start(bf16[256,768]{1,0:T(8,128)(2,1)S(1)} %get-tuple-element.74), channel_id=1, source_target_pairs={{0,8},{4,12},{8,0},{12,4},{16,24},{20,28},{24,16},{28,20},{1,9},{5... | collective-permute-start | bytes 1179656 | tf_op jit(solution)/shard_map/ppermute | solution.py:255
  32.7 16.0 %collective-permute-start.21 = (bf16[256,768]{1,0:T(8,128)(2,1)S(1)}, bf16[256,768]{1,0:T(8,128)(2,1)S(1)}, u32[]{:S(2)}, u32[]{:S(2)}) collective-permute-start(bf16[256,768]{1,0:T(8,128)(2,1)S(1)} %get-tuple-element.63._), channel_id=1, source_target_pairs={{0,16},{4,20},{8,24},{12,28},{16,0},{20,4},{24,8},{28,12},{1,17},{... | collective-permute-start | bytes 1179656 | tf_op jit(solution)/shard_map/ppermute | solution.py:255
  35.3 1.4 %collective-permute-start.11 = (bf16[384,256]{1,0:T(8,128)(2,1)S(1)}, bf16[384,256]{1,0:T(8,128)(2,1)S(1)}, u32[]{:S(2)}, u32[]{:S(2)}) collective-permute-start(bf16[384,256]{1,0:T(8,128)(2,1)S(1)} %get-tuple-element.58), channel_id=1, source_target_pairs={{0,4},{4,0},{8,12},{12,8},{16,20},{20,16},{24,28},{28,24},{1,5},{5... | collective-permute-start | bytes 589832 | tf_op jit(solution)/shard_map/ppermute | solution.py:255
  35.3 1.7 %collective-permute-start.15 = (bf16[384,256]{1,0:T(8,128)(2,1)S(1)}, bf16[384,256]{1,0:T(8,128)(2,1)S(1)}, u32[]{:S(2)}, u32[]{:S(2)}) collective-permute-start(bf16[384,256]{1,0:T(8,128)(2,1)S(1)} %get-tuple-element.65), channel_id=1, source_target_pairs={{0,4},{4,0},{8,12},{12,8},{16,20},{20,16},{24,28},{28,24},{1,5},{5... | collective-permute-start | bytes 589832 | tf_op jit(solution)/shard_map/ppermute | solution.py:255
  35.8 1.5 %collective-permute-start.16 = (bf16[384,256]{1,0:T(8,128)(2,1)S(1)}, bf16[384,256]{1,0:T(8,128)(2,1)S(1)}, u32[]{:S(2)}, u32[]{:S(2)}) collective-permute-start(bf16[384,256]{1,0:T(8,128)(2,1)S(1)} %get-tuple-element.67), channel_id=1, source_target_pairs={{0,4},{4,0},{8,12},{12,8},{16,20},{20,16},{24,28},{28,24},{1,5},{5... | collective-permute-start | bytes 589832 | tf_op jit(solution)/shard_map/ppermute | solution.py:255
  39.7 3.6 %collective-permute-start.17 = (f32[8,128]{1,0:T(8,128)S(1)}, f32[8,128]{1,0:T(8,128)S(1)}, u32[]{:S(2)}, u32[]{:S(2)}) collective-permute-start(f32[8,128]{1,0:T(8,128)S(1)} %get-tuple-element.70), channel_id=1, source_target_pairs={{0,1},{1,0},{2,3},{3,2},{4,5},{5,4},{6,7},{7,6},{8,9},{9,8},{10,11... | collective-permute-start | bytes 12296 | tf_op jit(solution)/shard_map/ppermute | solution.py:255
  40.0 3.6 %collective-permute-start.18 = (f32[8,128]{1,0:T(8,128)S(1)}, f32[8,128]{1,0:T(8,128)S(1)}, u32[]{:S(2)}, u32[]{:S(2)}) collective-permute-start(f32[8,128]{1,0:T(8,128)S(1)} %get-tuple-element.71), channel_id=1, source_target_pairs={{0,2},{1,3},{2,0},{3,1},{4,6},{5,7},{6,4},{7,5},{8,10},{9,11},{10,... | collective-permute-start | bytes 12296 | tf_op jit(solution)/shard_map/ppermute | solution.py:255
  41.4 4.5 %collective-permute-start.19 = (f32[8,128]{1,0:T(8,128)S(1)}, f32[8,128]{1,0:T(8,128)S(1)}, u32[]{:S(2)}, u32[]{:S(2)}) collective-permute-start(f32[8,128]{1,0:T(8,128)S(1)} %get-tuple-element.72), channel_id=1, source_target_pairs={{0,3},{1,2},{2,1},{3,0},{4,7},{5,6},{6,5},{7,4},{8,11},{9,10},{10,... | collective-permute-start | bytes 12296 | tf_op jit(solution)/shard_map/ppermute | solution.py:255
  (2 other events, 2.1 us)

commit v4 on v3

--- a/solution.py
+++ b/solution.py
@@ -212,7 +212,7 @@
         pairs[r][...] = jnp.broadcast_to(line, (8, 128))
 
 
-def gate_kernel(ids_ref, matches_ref, b0, b1, b2, b3, out_ref):
+def gate_kernel(ids_ref, matches_ref, b0, b1, b2, b3, part_ref, far_ref, out_ref, sum_ref):
     _, _, peer = coordinates()
     ids = ids_ref[...]
     total = jnp.zeros(ids.shape, F32)
@@ -224,6 +224,7 @@
         at_token = jnp.sum(jnp.where(match > 0.0, column, 0.0), axis=0, keepdims=True)
         total = jnp.where(ids == (peer ^ r) * EXP_DEV, at_token, total)
     out_ref[...] = total
+    sum_ref[...] = part_ref[...] + far_ref[...].astype(F32)
 
 
 HBM = pl.BlockSpec(memory_space=pltpu.HBM)
@@ -231,7 +232,7 @@
 VMEM = pl.BlockSpec(memory_space=pltpu.VMEM)
 
 
-def call(kernel, outs, specs=None, scratch=(), vmem=40 * 2**20):
+def call(kernel, outs, specs=None, scratch=(), cost=0, vmem=40 * 2**20):
     def run(*args):
         return pl.pallas_call(
             kernel,
@@ -240,7 +241,7 @@
             out_specs=jax.tree.map(lambda _: VMEM, outs),
             scratch_shapes=list(scratch),
             compiler_params=pltpu.CompilerParams(vmem_limit_bytes=vmem),
-            cost_estimate=pl.CostEstimate(flops=0, bytes_accessed=0, transcendentals=0),
+            cost_estimate=pl.CostEstimate(flops=0, bytes_accessed=cost, transcendentals=0),
         )(*args)
 
     return run
@@ -324,9 +325,11 @@
         [arr((slots, units), BF16)] + [arr((8, 128), F32)] * peers,
     )(*rows, *first, hidden, weight)
     back = [to_peer[r](pairs[r]) for r in range(peers)]
-    gate_grad = call(gate_kernel, arr((TOP, tokens), F32))(ids_t, matches, *back).T
-    weight_grad = part3 + come2.astype(F32) + come1.astype(F32)
-    return grad_hidden[None], gate_grad, weight_grad[None]
+    gate_grad, most = call(
+        gate_kernel, [arr((TOP, tokens), F32), arr((block, units), F32)], cost=4 * block * units
+    )(ids_t, matches, *back, part3, come1)
+    weight_grad = most + come2.astype(F32)
+    return grad_hidden[None], gate_grad.T, weight_grad[None]
 
 
 def solution(mesh):

time: 49.9 us -> 47.5 us (0.952)
  waiting for transfers between devices: 14.1 us -> 11.7 us
    ppermute x22, waiting for transfers between devices: 14.1 us -> 11.7 us  [over(): return lambda x: lax.ppermute(x, axis, pairs)]
  transfers between devices with their start and end apart: 22 -> 22, of which waited for: 13 -> 13; matrix products, arithmetic and copies ran while one was open for 2% -> 2% of each run, Pallas kernels for 13% -> 14%
where the time goes in v4:
time: 47.5 us; the launch traced here: 47.2 us
  starting transfers between devices  24.4 us (51%)
  waiting for transfers between devices  11.7 us (25%)
  Pallas kernels  6.51 us (14%)
  local copies, waits for them, and re-layouts  2.11 us (4%)
  other arithmetic  1.74 us (4%)
  between operations  0.74 us (2%)
    ppermute x22, starting transfers between devices, over(): return lambda x: lax.ppermute(x, axis, pairs)  24.4 us
    ppermute x22, waiting for transfers between devices, over(): return lambda x: lax.ppermute(x, axis, pairs)  11.7 us
    pallas_call x9, Pallas kernels, run(): pl.pallas_call(kernel, out_shape=outs, in_specs=specs or [VMEM] * len(arg...  6.51 us
    unnamed x8, local copies, waits for them, and re-layouts  2.11 us
  transfers between devices with their start and end apart: 22, of which 13 were waited for; matrix products, arithmetic and copies ran while one was open for 2% of the time, Pallas kernels for 14%

profile of v4, /device:TPU:0, one launch (start us, length us, event | category | flops | bytes accessed | tf_op | source)
XLA Modules:
  0.0 47.2 jit_solution(9472180163822490212)
XLA Ops:
  2.0 1.0 %copy-done.2 = bf16[128,2048]{1,0:T(8,128)(2,1)S(1)} copy-done((bf16[128,2048]{1,0:T(8,128)(2,1)S(1)}, bf16[128,2048]{1,0:T(8,128)(2,1)}, u32[]{:S(2)}) %copy-start.2) | copy-done | bytes 524312
  3.2 1.5 %collective-permute-done.other_ref = bf16[144,1024]{1,0:T(8,128)(2,1)S(1)} collective-permute-done((bf16[144,1024]{1,0:T(8,128)(2,1)S(1)}, bf16[144,1024]{1,0:T(8,128)(2,1)S(1)}, u32[]{:S(2)}, u32[]{:S(2)}) %collective-permute-start) | collective-permute-done | bytes 294944 | tf_op jit(solution)/shard_map/ppermute | solution.py:256
  5.3 2.7 %collective-permute-start.1 = (bf16[208,256]{1,0:T(8,128)(2,1)S(1)}, bf16[208,256]{1,0:T(8,128)(2,1)S(1)}, u32[]{:S(2)}, u32[]{:S(2)}) collective-permute-start(bf16[208,256]{1,0:T(8,128)(2,1)S(1)} %get-tuple-element.45), channel_id=1, source_target_pairs={{0,1},{1,0},{2,3},{3,2},{4,5},{5,4},{6,7},{7,6},{8,9},{9,8},{10,11... | collective-permute-start | bytes 319496 | tf_op jit(solution)/shard_map/ppermute | solution.py:256
  8.0 1.5 %collective-permute-start.2 = (bf16[208,256]{1,0:T(8,128)(2,1)S(1)}, bf16[208,256]{1,0:T(8,128)(2,1)S(1)}, u32[]{:S(2)}, u32[]{:S(2)}) collective-permute-start(bf16[208,256]{1,0:T(8,128)(2,1)S(1)} %get-tuple-element.46), channel_id=1, source_target_pairs={{0,2},{1,3},{2,0},{3,1},{4,6},{5,7},{6,4},{7,5},{8,10},{9,11},{10,... | collective-permute-start | bytes 319496 | tf_op jit(solution)/shard_map/ppermute | solution.py:256
  9.5 1.1 %copy-done.1 = bf16[1,384,768]{2,1,0:T(8,128)(2,1)S(1)} copy-done((bf16[1,384,768]{2,1,0:T(8,128)(2,1)S(1)}, bf16[1,384,768]{2,1,0:T(8,128)(2,1)}, u32[]{:S(2)}) %copy-start.1) | copy-done | bytes 589848
  10.9 2.0 %collective-permute-start.6 = (bf16[192,256]{1,0:T(8,128)(2,1)S(1)}, bf16[192,256]{1,0:T(8,128)(2,1)S(1)}, u32[]{:S(2)}, u32[]{:S(2)}) collective-permute-start(bf16[192,256]{1,0:T(8,128)(2,1)S(1)} %get-tuple-element.53), channel_id=1, source_target_pairs={{0,1},{1,0},{2,3},{3,2},{4,5},{5,4},{6,7},{7,6},{8,9},{9,8},{10,11... | collective-permute-start | bytes 294920 | tf_op jit(solution)/shard_map/ppermute | solution.py:256
  12.9 1.5 %collective-permute-start.7 = (bf16[192,256]{1,0:T(8,128)(2,1)S(1)}, bf16[192,256]{1,0:T(8,128)(2,1)S(1)}, u32[]{:S(2)}, u32[]{:S(2)}) collective-permute-start(bf16[192,256]{1,0:T(8,128)(2,1)S(1)} %get-tuple-element.54), channel_id=1, source_target_pairs={{0,2},{1,3},{2,0},{3,1},{4,6},{5,7},{6,4},{7,5},{8,10},{9,11},{10,... | collective-permute-start | bytes 294920 | tf_op jit(solution)/shard_map/ppermute | solution.py:256
  14.6 1.9 %collective-permute-start.8 = (bf16[192,256]{1,0:T(8,128)(2,1)S(1)}, bf16[192,256]{1,0:T(8,128)(2,1)S(1)}, u32[]{:S(2)}, u32[]{:S(2)}) collective-permute-start(bf16[192,256]{1,0:T(8,128)(2,1)S(1)} %get-tuple-element.55), channel_id=1, source_target_pairs={{0,3},{1,2},{2,1},{3,0},{4,7},{5,6},{6,5},{7,4},{8,11},{9,10},{10,... | collective-permute-start | bytes 294920 | tf_op jit(solution)/shard_map/ppermute | solution.py:256
  17.4 1.6 %collective-permute-start.10 = (bf16[128,768]{1,0:T(8,128)(2,1)S(1)}, bf16[128,768]{1,0:T(8,128)(2,1)S(1)}, u32[]{:S(2)}, u32[]{:S(2)}) collective-permute-start(bf16[128,768]{1,0:T(8,128)(2,1)S(1)} %get-tuple-element.58), channel_id=1, source_target_pairs={{0,8},{4,12},{8,0},{12,4},{16,24},{20,28},{24,16},{28,20},{1,9},{5... | collective-permute-start | bytes 589832 | tf_op jit(solution)/shard_map/ppermute | solution.py:256
  19.8 2.0 %collective-permute-start.12 = (bf16[192,512]{1,0:T(8,128)(2,1)S(1)}, bf16[192,512]{1,0:T(8,128)(2,1)S(1)}, u32[]{:S(2)}, u32[]{:S(2)}) collective-permute-start(bf16[192,512]{1,0:T(8,128)(2,1)S(1)} %get-tuple-element.62), channel_id=1, source_target_pairs={{0,1},{1,0},{2,3},{3,2},{4,5},{5,4},{6,7},{7,6},{8,9},{9,8},{10,11... | collective-permute-start | bytes 589832 | tf_op jit(solution)/shard_map/ppermute | solution.py:256
  21.9 1.5 %collective-permute-start.14 = (bf16[192,512]{1,0:T(8,128)(2,1)S(1)}, bf16[192,512]{1,0:T(8,128)(2,1)S(1)}, u32[]{:S(2)}, u32[]{:S(2)}) collective-permute-start(bf16[192,512]{1,0:T(8,128)(2,1)S(1)} %get-tuple-element.64), channel_id=1, source_target_pairs={{0,3},{1,2},{2,1},{3,0},{4,7},{5,6},{6,5},{7,4},{8,11},{9,10},{10,... | collective-permute-start | bytes 589832 | tf_op jit(solution)/shard_map/ppermute | solution.py:256
  23.6 2.1 %collective-permute-done.9.low_ref = bf16[128,768]{1,0:T(8,128)(2,1)S(1)} collective-permute-done((bf16[128,768]{1,0:T(8,128)(2,1)S(1)}, bf16[128,768]{1,0:T(8,128)(2,1)S(1)}, u32[]{:S(2)}, u32[]{:S(2)}) %collective-permute-start.9) | collective-permute-done | bytes 196640 | tf_op jit(solution)/shard_map/ppermute | solution.py:256
  26.3 2.6 %collective-permute-start.20 = (bf16[256,768]{1,0:T(8,128)(2,1)S(1)}, bf16[256,768]{1,0:T(8,128)(2,1)S(1)}, u32[]{:S(2)}, u32[]{:S(2)}) collective-permute-start(bf16[256,768]{1,0:T(8,128)(2,1)S(1)} %get-tuple-element.65._), channel_id=1, source_target_pairs={{0,16},{4,20},{8,24},{12,28},{16,0},{20,4},{24,8},{28,12},{1,17},{... | collective-permute-start | bytes 1179656 | tf_op jit(solution)/shard_map/ppermute | solution.py:256
  28.9 1.2 %collective-permute-done.13.p2 = bf16[192,512]{1,0:T(8,128)(2,1)S(1)} collective-permute-done((bf16[192,512]{1,0:T(8,128)(2,1)S(1)}, bf16[192,512]{1,0:T(8,128)(2,1)S(1)}, u32[]{:S(2)}, u32[]{:S(2)}) %collective-permute-start.13) | collective-permute-done | bytes 196640 | tf_op jit(solution)/shard_map/ppermute | solution.py:256
  30.1 0.8 %shard_map.82 = (bf16[256,768]{1,0:T(8,128)(2,1)S(1)}, f32[256,768]{1,0:T(8,128)S(1)}, bf16[384,256]{1,0:T(8,128)(2,1)S(1)}, bf16[384,256]{1,0:T(8,128)(2,1)S(1)...) custom-call(bf16[192,512]{1,0:T(8,128)(2,1)S(1)} %get-tuple-element.61.p0, ...), custom_call_target="tpu_custom_call" | custom-call | tf_op jit(solution)/shard_map/pallas_call | solution.py:237
  30.9 1.7 %collective-permute-start.21 = (bf16[256,768]{1,0:T(8,128)(2,1)S(1)}, bf16[256,768]{1,0:T(8,128)(2,1)S(1)}, u32[]{:S(2)}, u32[]{:S(2)}) collective-permute-start(bf16[256,768]{1,0:T(8,128)(2,1)S(1)} %get-tuple-element.78), channel_id=1, source_target_pairs={{0,8},{4,12},{8,0},{12,4},{16,24},{20,28},{24,16},{28,20},{1,9},{5... | collective-permute-start | bytes 1179656 | tf_op jit(solution)/shard_map/ppermute | solution.py:256
  33.2 0.9 %collective-permute-done.11.refs_3_ = bf16[384,256]{1,0:T(8,128)(2,1)S(1)} collective-permute-done((bf16[384,256]{1,0:T(8,128)(2,1)S(1)}, bf16[384,256]{1,0:T(8,128)(2,1)S(1)}, u32[]{:S(2)}, u32[]{:S(2)}) %collective-permute-start.11) | collective-permute-done | bytes 196640 | tf_op jit(solution)/shard_map/ppermute | solution.py:256
  34.7 2.4 %shard_map.83 = (bf16[384,768]{1,0:T(8,128)(2,1)}, f32[8,128]{1,0:T(8,128)S(1)}, f32[8,128]{1,0:T(8,128)S(1)}, f32[8,128]{1,0:T(8,128)S(1)}, f32[8,128]{1,0:T(8,128)S(1)}) custom-call(bf16[384,256]{1,0:T(8,128)(2,1)S(1)} %get-tuple-element.50.refs_0_, bf16[384,256]{1,0:T(8,128)(2,1)S(1)} %collective-permute-done.5.refs_1_, ...), custom_call_target="tpu_custom_call" | custom-call | tf_op jit(solution)/shard_map/pallas_call | solution.py:237
  37.0 1.6 %collective-permute-start.17 = (f32[8,128]{1,0:T(8,128)S(1)}, f32[8,128]{1,0:T(8,128)S(1)}, u32[]{:S(2)}, u32[]{:S(2)}) collective-permute-start(f32[8,128]{1,0:T(8,128)S(1)} %get-tuple-element.72), channel_id=1, source_target_pairs={{0,1},{1,0},{2,3},{3,2},{4,5},{5,4},{6,7},{7,6},{8,9},{9,8},{10,11... | collective-permute-start | bytes 12296 | tf_op jit(solution)/shard_map/ppermute | solution.py:256
  38.8 1.8 %collective-permute-start.19 = (f32[8,128]{1,0:T(8,128)S(1)}, f32[8,128]{1,0:T(8,128)S(1)}, u32[]{:S(2)}, u32[]{:S(2)}) collective-permute-start(f32[8,128]{1,0:T(8,128)S(1)} %get-tuple-element.74), channel_id=1, source_target_pairs={{0,3},{1,2},{2,1},{3,0},{4,7},{5,6},{6,5},{7,4},{8,11},{9,10},{10,... | collective-permute-start | bytes 12296 | tf_op jit(solution)/shard_map/ppermute | solution.py:256
  40.7 1.6 %collective-permute-done.18.b2 = f32[8,128]{1,0:T(8,128)S(1)} collective-permute-done((f32[8,128]{1,0:T(8,128)S(1)}, f32[8,128]{1,0:T(8,128)S(1)}, u32[]{:S(2)}, u32[]{:S(2)}) %collective-permute-start.18) | collective-permute-done | bytes 4128 | tf_op jit(solution)/shard_map/ppermute | solution.py:256
  42.2 1.1 %collective-permute-done.19.b3 = f32[8,128]{1,0:T(8,128)S(1)} collective-permute-done((f32[8,128]{1,0:T(8,128)S(1)}, f32[8,128]{1,0:T(8,128)S(1)}, u32[]{:S(2)}, u32[]{:S(2)}) %collective-permute-start.19) | collective-permute-done | bytes 4128 | tf_op jit(solution)/shard_map/ppermute | solution.py:256
  43.3 1.9 %collective-permute-done.20.far_ref = bf16[256,768]{1,0:T(8,128)(2,1)S(1)} collective-permute-done((bf16[256,768]{1,0:T(8,128)(2,1)S(1)}, bf16[256,768]{1,0:T(8,128)(2,1)S(1)}, u32[]{:S(2)}, u32[]{:S(2)}) %collective-permute-start.20) | collective-permute-done | bytes 393248 | tf_op jit(solution)/shard_map/ppermute | solution.py:256
  46.3 0.9 %add_bitcast_fusion = f32[1,256,768]{2,1,0:T(8,128)} fusion(f32[256,768]{1,0:T(8,128)S(1)} %get-tuple-element.77, bf16[256,768]{1,0:T(8,128)(2,1)S(1)} %collective-permute-done.21), kind=kLoop, calls=%fused_computation | loop fusion | flops 393216 | bytes 1966080 | tf_op jit(solution)/shard_map/broadcast_in_dim | solution.py:332
  (41 shorter events, 7.4 us)
Async XLA Ops:
  0.6 15.9 %collective-permute-start.4 = (bf16[384,768]{1,0:T(8,128)(2,1)}, bf16[384,768]{1,0:T(8,128)(2,1)S(1)}, u32[]{:S(2)}, u32[]{:S(2)}) collective-permute-start(bf16[384,768]{1,0:T(8,128)(2,1)} %bitcast.9), channel_id=1, source_target_pairs={{0,4},{4,0},{8,12},{12,8},{16,20},{20,16},{24,28},{28,24},{1,5},{5... | collective-permute-start | bytes 1769480 | tf_op jit(solution)/shard_map/ppermute | solution.py:256
  3.1 1.6 %collective-permute-start = (bf16[144,1024]{1,0:T(8,128)(2,1)S(1)}, bf16[144,1024]{1,0:T(8,128)(2,1)S(1)}, u32[]{:S(2)}, u32[]{:S(2)}) collective-permute-start(bf16[144,1024]{1,0:T(8,128)(2,1)S(1)} %get-tuple-element.43), channel_id=1, source_target_pairs={{0,4},{4,0},{8,12},{12,8},{16,20},{20,16},{24,28},{28,24},{1,5},{5... | collective-permute-start | bytes 884744 | tf_op jit(solution)/shard_map/ppermute | solution.py:256
  5.3 7.6 %collective-permute-start.1 = (bf16[208,256]{1,0:T(8,128)(2,1)S(1)}, bf16[208,256]{1,0:T(8,128)(2,1)S(1)}, u32[]{:S(2)}, u32[]{:S(2)}) collective-permute-start(bf16[208,256]{1,0:T(8,128)(2,1)S(1)} %get-tuple-element.45), channel_id=1, source_target_pairs={{0,1},{1,0},{2,3},{3,2},{4,5},{5,4},{6,7},{7,6},{8,9},{9,8},{10,11... | collective-permute-start | bytes 319496 | tf_op jit(solution)/shard_map/ppermute | solution.py:256
  8.0 6.6 %collective-permute-start.2 = (bf16[208,256]{1,0:T(8,128)(2,1)S(1)}, bf16[208,256]{1,0:T(8,128)(2,1)S(1)}, u32[]{:S(2)}, u32[]{:S(2)}) collective-permute-start(bf16[208,256]{1,0:T(8,128)(2,1)S(1)} %get-tuple-element.46), channel_id=1, source_target_pairs={{0,2},{1,3},{2,0},{3,1},{4,6},{5,7},{6,4},{7,5},{8,10},{9,11},{10,... | collective-permute-start | bytes 319496 | tf_op jit(solution)/shard_map/ppermute | solution.py:256
  9.5 7.0 %collective-permute-start.3 = (bf16[208,256]{1,0:T(8,128)(2,1)S(1)}, bf16[208,256]{1,0:T(8,128)(2,1)S(1)}, u32[]{:S(2)}, u32[]{:S(2)}) collective-permute-start(bf16[208,256]{1,0:T(8,128)(2,1)S(1)} %get-tuple-element.47), channel_id=1, source_target_pairs={{0,3},{1,2},{2,1},{3,0},{4,7},{5,6},{6,5},{7,4},{8,11},{9,10},{10,... | collective-permute-start | bytes 319496 | tf_op jit(solution)/shard_map/ppermute | solution.py:256
  10.9 8.9 %collective-permute-start.6 = (bf16[192,256]{1,0:T(8,128)(2,1)S(1)}, bf16[192,256]{1,0:T(8,128)(2,1)S(1)}, u32[]{:S(2)}, u32[]{:S(2)}) collective-permute-start(bf16[192,256]{1,0:T(8,128)(2,1)S(1)} %get-tuple-element.53), channel_id=1, source_target_pairs={{0,1},{1,0},{2,3},{3,2},{4,5},{5,4},{6,7},{7,6},{8,9},{9,8},{10,11... | collective-permute-start | bytes 294920 | tf_op jit(solution)/shard_map/ppermute | solution.py:256
  12.9 9.0 %collective-permute-start.7 = (bf16[192,256]{1,0:T(8,128)(2,1)S(1)}, bf16[192,256]{1,0:T(8,128)(2,1)S(1)}, u32[]{:S(2)}, u32[]{:S(2)}) collective-permute-start(bf16[192,256]{1,0:T(8,128)(2,1)S(1)} %get-tuple-element.54), channel_id=1, source_target_pairs={{0,2},{1,3},{2,0},{3,1},{4,6},{5,7},{6,4},{7,5},{8,10},{9,11},{10,... | collective-permute-start | bytes 294920 | tf_op jit(solution)/shard_map/ppermute | solution.py:256
  14.6 7.3 %collective-permute-start.8 = (bf16[192,256]{1,0:T(8,128)(2,1)S(1)}, bf16[192,256]{1,0:T(8,128)(2,1)S(1)}, u32[]{:S(2)}, u32[]{:S(2)}) collective-permute-start(bf16[192,256]{1,0:T(8,128)(2,1)S(1)} %get-tuple-element.55), channel_id=1, source_target_pairs={{0,3},{1,2},{2,1},{3,0},{4,7},{5,6},{6,5},{7,4},{8,11},{9,10},{10,... | collective-permute-start | bytes 294920 | tf_op jit(solution)/shard_map/ppermute | solution.py:256
  16.6 18.1 %copy-start = (bf16[1,768,2048]{2,1,0:T(8,128)(2,1)S(1)}, bf16[1,768,2048]{2,1,0:T(8,128)(2,1)}, u32[]{:S(2)}) copy-start(bf16[1,768,2048]{2,1,0:T(8,128)(2,1)} %param.9) | copy-start | bytes 9437188
  17.4 6.3 %collective-permute-start.10 = (bf16[128,768]{1,0:T(8,128)(2,1)S(1)}, bf16[128,768]{1,0:T(8,128)(2,1)S(1)}, u32[]{:S(2)}, u32[]{:S(2)}) collective-permute-start(bf16[128,768]{1,0:T(8,128)(2,1)S(1)} %get-tuple-element.58), channel_id=1, source_target_pairs={{0,8},{4,12},{8,0},{12,4},{16,24},{20,28},{24,16},{28,20},{1,9},{5... | collective-permute-start | bytes 589832 | tf_op jit(solution)/shard_map/ppermute | solution.py:256
  19.0 6.7 %collective-permute-start.9 = (bf16[128,768]{1,0:T(8,128)(2,1)S(1)}, bf16[128,768]{1,0:T(8,128)(2,1)S(1)}, u32[]{:S(2)}, u32[]{:S(2)}) collective-permute-start(bf16[128,768]{1,0:T(8,128)(2,1)S(1)} %get-tuple-element.57.outs_0_), channel_id=1, source_target_pairs={{0,8},{4,12},{8,0},{12,4},{16,24},{20,28},{24,16},{28,20},{1,9},{5... | collective-permute-start | bytes 589832 | tf_op jit(solution)/shard_map/ppermute | solution.py:256
  19.8 9.1 %collective-permute-start.12 = (bf16[192,512]{1,0:T(8,128)(2,1)S(1)}, bf16[192,512]{1,0:T(8,128)(2,1)S(1)}, u32[]{:S(2)}, u32[]{:S(2)}) collective-permute-start(bf16[192,512]{1,0:T(8,128)(2,1)S(1)} %get-tuple-element.62), channel_id=1, source_target_pairs={{0,1},{1,0},{2,3},{3,2},{4,5},{5,4},{6,7},{7,6},{8,9},{9,8},{10,11... | collective-permute-start | bytes 589832 | tf_op jit(solution)/shard_map/ppermute | solution.py:256
  21.9 8.2 %collective-permute-start.13 = (bf16[192,512]{1,0:T(8,128)(2,1)S(1)}, bf16[192,512]{1,0:T(8,128)(2,1)S(1)}, u32[]{:S(2)}, u32[]{:S(2)}) collective-permute-start(bf16[192,512]{1,0:T(8,128)(2,1)S(1)} %get-tuple-element.63), channel_id=1, source_target_pairs={{0,2},{1,3},{2,0},{3,1},{4,6},{5,7},{6,4},{7,5},{8,10},{9,11},{10,... | collective-permute-start | bytes 589832 | tf_op jit(solution)/shard_map/ppermute | solution.py:256
  21.9 8.2 %collective-permute-start.14 = (bf16[192,512]{1,0:T(8,128)(2,1)S(1)}, bf16[192,512]{1,0:T(8,128)(2,1)S(1)}, u32[]{:S(2)}, u32[]{:S(2)}) collective-permute-start(bf16[192,512]{1,0:T(8,128)(2,1)S(1)} %get-tuple-element.64), channel_id=1, source_target_pairs={{0,3},{1,2},{2,1},{3,0},{4,7},{5,6},{6,5},{7,4},{8,11},{9,10},{10,... | collective-permute-start | bytes 589832 | tf_op jit(solution)/shard_map/ppermute | solution.py:256
  23.6 9.5 %collective-permute-start.5 = (bf16[384,256]{1,0:T(8,128)(2,1)S(1)}, bf16[384,256]{1,0:T(8,128)(2,1)S(1)}, u32[]{:S(2)}, u32[]{:S(2)}) collective-permute-start(bf16[384,256]{1,0:T(8,128)(2,1)S(1)} %get-tuple-element.51), channel_id=1, source_target_pairs={{0,4},{4,0},{8,12},{12,8},{16,20},{20,16},{24,28},{28,24},{1,5},{5... | collective-permute-start | bytes 589832 | tf_op jit(solution)/shard_map/ppermute | solution.py:256
  26.3 18.9 %collective-permute-start.20 = (bf16[256,768]{1,0:T(8,128)(2,1)S(1)}, bf16[256,768]{1,0:T(8,128)(2,1)S(1)}, u32[]{:S(2)}, u32[]{:S(2)}) collective-permute-start(bf16[256,768]{1,0:T(8,128)(2,1)S(1)} %get-tuple-element.65._), channel_id=1, source_target_pairs={{0,16},{4,20},{8,24},{12,28},{16,0},{20,4},{24,8},{28,12},{1,17},{... | collective-permute-start | bytes 1179656 | tf_op jit(solution)/shard_map/ppermute | solution.py:256
  30.9 14.3 %copy-start.3 = (s32[128,8]{0,1:T(8,128)S(1)}, s32[128,8]{0,1:T(8,128)}, u32[]{:S(2)}) copy-start(s32[128,8]{0,1:T(8,128)} %param.6) | copy-start | bytes 12292
  30.9 15.4 %collective-permute-start.21 = (bf16[256,768]{1,0:T(8,128)(2,1)S(1)}, bf16[256,768]{1,0:T(8,128)(2,1)S(1)}, u32[]{:S(2)}, u32[]{:S(2)}) collective-permute-start(bf16[256,768]{1,0:T(8,128)(2,1)S(1)} %get-tuple-element.78), channel_id=1, source_target_pairs={{0,8},{4,12},{8,0},{12,4},{16,24},{20,28},{24,16},{28,20},{1,9},{5... | collective-permute-start | bytes 1179656 | tf_op jit(solution)/shard_map/ppermute | solution.py:256
  32.7 1.4 %collective-permute-start.11 = (bf16[384,256]{1,0:T(8,128)(2,1)S(1)}, bf16[384,256]{1,0:T(8,128)(2,1)S(1)}, u32[]{:S(2)}, u32[]{:S(2)}) collective-permute-start(bf16[384,256]{1,0:T(8,128)(2,1)S(1)} %get-tuple-element.60), channel_id=1, source_target_pairs={{0,4},{4,0},{8,12},{12,8},{16,20},{20,16},{24,28},{28,24},{1,5},{5... | collective-permute-start | bytes 589832 | tf_op jit(solution)/shard_map/ppermute | solution.py:256
  32.7 1.7 %collective-permute-start.15 = (bf16[384,256]{1,0:T(8,128)(2,1)S(1)}, bf16[384,256]{1,0:T(8,128)(2,1)S(1)}, u32[]{:S(2)}, u32[]{:S(2)}) collective-permute-start(bf16[384,256]{1,0:T(8,128)(2,1)S(1)} %get-tuple-element.67), channel_id=1, source_target_pairs={{0,4},{4,0},{8,12},{12,8},{16,20},{20,16},{24,28},{28,24},{1,5},{5... | collective-permute-start | bytes 589832 | tf_op jit(solution)/shard_map/ppermute | solution.py:256
  33.2 1.5 %collective-permute-start.16 = (bf16[384,256]{1,0:T(8,128)(2,1)S(1)}, bf16[384,256]{1,0:T(8,128)(2,1)S(1)}, u32[]{:S(2)}, u32[]{:S(2)}) collective-permute-start(bf16[384,256]{1,0:T(8,128)(2,1)S(1)} %get-tuple-element.69), channel_id=1, source_target_pairs={{0,4},{4,0},{8,12},{12,8},{16,20},{20,16},{24,28},{28,24},{1,5},{5... | collective-permute-start | bytes 589832 | tf_op jit(solution)/shard_map/ppermute | solution.py:256
  37.0 3.6 %collective-permute-start.17 = (f32[8,128]{1,0:T(8,128)S(1)}, f32[8,128]{1,0:T(8,128)S(1)}, u32[]{:S(2)}, u32[]{:S(2)}) collective-permute-start(f32[8,128]{1,0:T(8,128)S(1)} %get-tuple-element.72), channel_id=1, source_target_pairs={{0,1},{1,0},{2,3},{3,2},{4,5},{5,4},{6,7},{7,6},{8,9},{9,8},{10,11... | collective-permute-start | bytes 12296 | tf_op jit(solution)/shard_map/ppermute | solution.py:256
  38.6 3.6 %collective-permute-start.18 = (f32[8,128]{1,0:T(8,128)S(1)}, f32[8,128]{1,0:T(8,128)S(1)}, u32[]{:S(2)}, u32[]{:S(2)}) collective-permute-start(f32[8,128]{1,0:T(8,128)S(1)} %get-tuple-element.73), channel_id=1, source_target_pairs={{0,2},{1,3},{2,0},{3,1},{4,6},{5,7},{6,4},{7,5},{8,10},{9,11},{10,... | collective-permute-start | bytes 12296 | tf_op jit(solution)/shard_map/ppermute | solution.py:256
  38.8 4.5 %collective-permute-start.19 = (f32[8,128]{1,0:T(8,128)S(1)}, f32[8,128]{1,0:T(8,128)S(1)}, u32[]{:S(2)}, u32[]{:S(2)}) collective-permute-start(f32[8,128]{1,0:T(8,128)S(1)} %get-tuple-element.74), channel_id=1, source_target_pairs={{0,3},{1,2},{2,1},{3,0},{4,7},{5,6},{6,5},{7,4},{8,11},{9,10},{10,... | collective-permute-start | bytes 12296 | tf_op jit(solution)/shard_map/ppermute | solution.py:256
  (2 other events, 2.1 us)

commit v5 on v4

--- a/solution.py
+++ b/solution.py
@@ -67,38 +67,28 @@
     return lax.dot_general(a, b, (dims, ((), ())), preferred_element_type=F32)
 
 
-def swap_kernel(block, marks_in, grad_ref, send_ref, own_ref, marks_ref):
-    _, core, _ = coordinates()
-    tokens = grad_ref.shape[0]
-    for i in range(own_ref.shape[1] // block):
-        at = slice(i * block, (i + 1) * block)
-        for side, ref in ((1 - core, send_ref), (core, own_ref)):
-            start = pl.multiple_of((2 * i + side) * block, block)
-            ref[:tokens, at] = grad_ref[:, pl.ds(start, block)]
-    marks = jnp.concatenate([marks_in[...], jnp.full((12, tokens), -1.0, F32)], axis=0)
-    marks_ref[...] = marks.astype(BF16)
-    send_ref[tokens:, :] = jnp.zeros((16, send_ref.shape[1]), BF16)
-    send_ref[tokens:, :tokens] = marks.astype(BF16)
-
-
-def gather_kernel(block, capacity, own_ref, marks_ref, other_ref, *outs):
+def copy_kernel(from_ref, to_ref):
+    to_ref[...] = from_ref[...]
+
+
+def gather_kernel(block, capacity, own_ref, marks_ref, other_ref, other_marks_ref, *outs):
     first, (matches_ref, scratch) = outs[:-2], outs[-2:]
-    chip, _, peer = coordinates()
+    chip, core, peer = coordinates()
     tokens = own_ref.shape[0]
     before = (
         lax.broadcasted_iota(jnp.int32, (tokens, tokens), 0)
         < lax.broadcasted_iota(jnp.int32, (tokens, tokens), 1)
     ).astype(F32).astype(BF16)
     slot = lax.broadcasted_iota(jnp.int32, (capacity, tokens), 0).astype(F32)
-    columns = pl.ds(pl.multiple_of((chip ^ 3) * block, block), block)
+    columns = pl.ds(pl.multiple_of((2 * (chip ^ 3) + core) * block, block), block)
     gate_rows = [[], [], [], []]
     for g in range(2):
-        marks = (marks_ref[...] if g == 0 else other_ref[tokens:, :tokens]).astype(F32)
+        marks = (marks_ref if g == 0 else other_marks_ref)[...].astype(F32)
         live = jnp.where(marks >= 0.0, 1.0, 0.0)
         rank = dot(live.astype(BF16), before, ((1,), (0,)))
         scratch[2 * g] = marks
         scratch[2 * g + 1] = jnp.where(marks >= 0.0, rank, -1.0)
-        rows = (own_ref if g == 0 else other_ref)[:tokens, columns]
+        rows = (own_ref if g == 0 else other_ref)[:, columns]
         for r in range(4):
             e = peer ^ r
             gate = scratch[2 * g, pl.ds(e, 1), :]
@@ -133,13 +123,12 @@
     if take:
         outs[-1][...] = outs[0][...]
         outs = outs[:-1]
-    chip, _, _ = coordinates()
-    tokens = own_ref.shape[0]
+    chip, core, _ = coordinates()
     for i, k in enumerate(chunks):
-        columns = pl.ds(pl.multiple_of((chip ^ (3 - k)) * block, block), block)
+        columns = pl.ds(pl.multiple_of((2 * (chip ^ (3 - k)) + core) * block, block), block)
         to = slice(i * block, (i + 1) * block)
         for g in range(2):
-            rows = (own_ref if g == 0 else other_ref)[:tokens, columns]
+            rows = (own_ref if g == 0 else other_ref)[:, columns]
             for r in range(4):
                 outs[r - 4][g * capacity : (g + 1) * capacity, to] = dot(
                     matches_ref[g, r], rows, ((1,), (0,))
@@ -268,19 +257,16 @@
     to_peer = [lambda x: x] + [over("expert", peers, r) for r in range(1, peers)]
     ids_t, gates_t = expert_ids.T, gate_weights.T
 
-    hit = ids_t == EXP_DEV * jnp.arange(peers, dtype=jnp.int32)[:, None, None]
-    marks = jnp.max(jnp.where(hit, gates_t, -jnp.ones((), BF16)), axis=1).astype(F32)
-    send, own, marks = call(
-        functools.partial(swap_kernel, block),
-        [arr((tokens + 16, half), BF16), arr((tokens, half), BF16), arr((16, tokens), BF16)],
-    )(marks, grad_out)
-    other = core_swap(send)
+    hit = ids_t == EXP_DEV * jnp.arange(16, dtype=jnp.int32)[:, None, None]
+    marks = jnp.max(jnp.where(hit, gates_t, -jnp.ones((), BF16)), axis=1)
+    other, other_marks = core_swap(grad_out), core_swap(marks)
+    own = call(copy_kernel, arr(grad_out.shape, BF16))(grad_out)
     *first, matches = call(
         functools.partial(gather_kernel, block, capacity),
         [arr((2 * capacity + 16, block), BF16)] * peers
         + [arr((2, peers, capacity, tokens), BF16)],
         scratch=[pltpu.VMEM((4, 16, tokens), F32)],
-    )(own, marks, other)
+    )(own, marks, other, other_marks)
     first = [to_peer[r](first[r]) for r in range(peers)]
     other_hidden = core_swap(hidden)
 

time: 47.5 us -> 46.4 us (0.977)
  starting transfers between devices: 24.4 us -> 23.3 us
    ppermute x22 -> x23, starting transfers between devices: 24.4 us -> 23.3 us  [over(): return lambda x: lax.ppermute(x, axis, pairs)]
    ppermute x22 -> x23, waiting for transfers between devices: 11.7 us -> 11.8 us  [over(): return lambda x: lax.ppermute(x, axis, pairs)]
  transfers between devices with their start and end apart: 22 -> 23, of which waited for: 13 -> 12; matrix products, arithmetic and copies ran while one was open for 2% -> 2% of each run, Pallas kernels for 14% -> 14%
where the time goes in v5:
time: 46.4 us; the launch traced here: 46.2 us
  starting transfers between devices  23.3 us (50%)
  waiting for transfers between devices  11.8 us (25%)
  Pallas kernels  6.47 us (14%)
  local copies, waits for them, and re-layouts  2.12 us (5%)
  other arithmetic  1.74 us (4%)
  between operations  0.75 us (2%)
    ppermute x23, starting transfers between devices, over(): return lambda x: lax.ppermute(x, axis, pairs)  23.3 us
    ppermute x23, waiting for transfers between devices, over(): return lambda x: lax.ppermute(x, axis, pairs)  11.8 us
    pallas_call x9, Pallas kernels, run(): pl.pallas_call(kernel, out_shape=outs, in_specs=specs or [VMEM] * len(arg...  6.47 us
    unnamed x8, local copies, waits for them, and re-layouts  2.12 us
    broadcast_in_dim x1, other arithmetic, per_device(): return (grad_hidden[None], gate_grad.T, weight_grad[None])  0.95 us
  transfers between devices with their start and end apart: 23, of which 12 were waited for; matrix products, arithmetic and copies ran while one was open for 2% of the time, Pallas kernels for 14%

profile of v5, /device:TPU:0, one launch (start us, length us, event | category | flops | bytes accessed | tf_op | source)
XLA Modules:
  0.0 46.2 jit_solution(5872624055682914952)
XLA Ops:
  1.2 0.8 %fusion.marks_ref = bf16[16,128]{1,0:T(8,128)(2,1)S(1)} fusion(s32[8,128]{1,0:T(8,128)} %bitcast.11, s32[16]{0:T(128)S(1)} %iota_multiply_fusion, bf16[8,128]{1,0:T(8,128)(2,1)} %bitcast.13), kind=kLoop, calls=%fused_computation.2 | loop fusion | flops 47104 | bytes 10304 | tf_op jit(solution)/shard_map/reduce_max | solution.py:261
  2.5 1.0 %copy-done.2 = bf16[128,2048]{1,0:T(8,128)(2,1)S(1)} copy-done((bf16[128,2048]{1,0:T(8,128)(2,1)S(1)}, bf16[128,2048]{1,0:T(8,128)(2,1)}, u32[]{:S(2)}) %copy-start.2) | copy-done | bytes 524312
  4.2 2.8 %collective-permute-start.2 = (bf16[208,256]{1,0:T(8,128)(2,1)S(1)}, bf16[208,256]{1,0:T(8,128)(2,1)S(1)}, u32[]{:S(2)}, u32[]{:S(2)}) collective-permute-start(bf16[208,256]{1,0:T(8,128)(2,1)S(1)} %get-tuple-element.39), channel_id=1, source_target_pairs={{0,1},{1,0},{2,3},{3,2},{4,5},{5,4},{6,7},{7,6},{8,9},{9,8},{10,11... | collective-permute-start | bytes 319496 | tf_op jit(solution)/shard_map/ppermute | solution.py:245
  7.0 1.5 %collective-permute-start.3 = (bf16[208,256]{1,0:T(8,128)(2,1)S(1)}, bf16[208,256]{1,0:T(8,128)(2,1)S(1)}, u32[]{:S(2)}, u32[]{:S(2)}) collective-permute-start(bf16[208,256]{1,0:T(8,128)(2,1)S(1)} %get-tuple-element.40), channel_id=1, source_target_pairs={{0,2},{1,3},{2,0},{3,1},{4,6},{5,7},{6,4},{7,5},{8,10},{9,11},{10,... | collective-permute-start | bytes 319496 | tf_op jit(solution)/shard_map/ppermute | solution.py:245
  8.6 1.1 %copy-done.1 = bf16[1,384,768]{2,1,0:T(8,128)(2,1)S(1)} copy-done((bf16[1,384,768]{2,1,0:T(8,128)(2,1)S(1)}, bf16[1,384,768]{2,1,0:T(8,128)(2,1)}, u32[]{:S(2)}) %copy-start.1) | copy-done | bytes 589848
  9.9 2.0 %collective-permute-start.7 = (bf16[192,256]{1,0:T(8,128)(2,1)S(1)}, bf16[192,256]{1,0:T(8,128)(2,1)S(1)}, u32[]{:S(2)}, u32[]{:S(2)}) collective-permute-start(bf16[192,256]{1,0:T(8,128)(2,1)S(1)} %get-tuple-element.47), channel_id=1, source_target_pairs={{0,1},{1,0},{2,3},{3,2},{4,5},{5,4},{6,7},{7,6},{8,9},{9,8},{10,11... | collective-permute-start | bytes 294920 | tf_op jit(solution)/shard_map/ppermute | solution.py:245
  12.0 1.5 %collective-permute-start.8 = (bf16[192,256]{1,0:T(8,128)(2,1)S(1)}, bf16[192,256]{1,0:T(8,128)(2,1)S(1)}, u32[]{:S(2)}, u32[]{:S(2)}) collective-permute-start(bf16[192,256]{1,0:T(8,128)(2,1)S(1)} %get-tuple-element.48), channel_id=1, source_target_pairs={{0,2},{1,3},{2,0},{3,1},{4,6},{5,7},{6,4},{7,5},{8,10},{9,11},{10,... | collective-permute-start | bytes 294920 | tf_op jit(solution)/shard_map/ppermute | solution.py:245
  13.8 1.2 %collective-permute-done.4.p3.refs_11_ = bf16[208,256]{1,0:T(8,128)(2,1)S(1)} collective-permute-done((bf16[208,256]{1,0:T(8,128)(2,1)S(1)}, bf16[208,256]{1,0:T(8,128)(2,1)S(1)}, u32[]{:S(2)}, u32[]{:S(2)}) %collective-permute-start.4) | collective-permute-done | bytes 106528 | tf_op jit(solution)/shard_map/ppermute | solution.py:245
  15.8 1.6 %collective-permute-start.11 = (bf16[128,768]{1,0:T(8,128)(2,1)S(1)}, bf16[128,768]{1,0:T(8,128)(2,1)S(1)}, u32[]{:S(2)}, u32[]{:S(2)}) collective-permute-start(bf16[128,768]{1,0:T(8,128)(2,1)S(1)} %get-tuple-element.52), channel_id=1, source_target_pairs={{0,8},{4,12},{8,0},{12,4},{16,24},{20,28},{24,16},{28,20},{1,9},{5... | collective-permute-start | bytes 589832 | tf_op jit(solution)/shard_map/ppermute | solution.py:245
  18.3 0.9 %collective-permute-start.13 = (bf16[192,512]{1,0:T(8,128)(2,1)S(1)}, bf16[192,512]{1,0:T(8,128)(2,1)S(1)}, u32[]{:S(2)}, u32[]{:S(2)}) collective-permute-start(bf16[192,512]{1,0:T(8,128)(2,1)S(1)} %get-tuple-element.56), channel_id=1, source_target_pairs={{0,1},{1,0},{2,3},{3,2},{4,5},{5,4},{6,7},{7,6},{8,9},{9,8},{10,11... | collective-permute-start | bytes 589832 | tf_op jit(solution)/shard_map/ppermute | solution.py:245
  19.1 1.2 %collective-permute-start.14 = (bf16[192,512]{1,0:T(8,128)(2,1)S(1)}, bf16[192,512]{1,0:T(8,128)(2,1)S(1)}, u32[]{:S(2)}, u32[]{:S(2)}) collective-permute-start(bf16[192,512]{1,0:T(8,128)(2,1)S(1)} %get-tuple-element.57), channel_id=1, source_target_pairs={{0,2},{1,3},{2,0},{3,1},{4,6},{5,7},{6,4},{7,5},{8,10},{9,11},{10,... | collective-permute-start | bytes 589832 | tf_op jit(solution)/shard_map/ppermute | solution.py:245
  20.3 1.5 %collective-permute-start.15 = (bf16[192,512]{1,0:T(8,128)(2,1)S(1)}, bf16[192,512]{1,0:T(8,128)(2,1)S(1)}, u32[]{:S(2)}, u32[]{:S(2)}) collective-permute-start(bf16[192,512]{1,0:T(8,128)(2,1)S(1)} %get-tuple-element.58), channel_id=1, source_target_pairs={{0,3},{1,2},{2,1},{3,0},{4,7},{5,6},{6,5},{7,4},{8,11},{9,10},{10,... | collective-permute-start | bytes 589832 | tf_op jit(solution)/shard_map/ppermute | solution.py:245
  22.6 2.1 %collective-permute-done.10.low_ref = bf16[128,768]{1,0:T(8,128)(2,1)S(1)} collective-permute-done((bf16[128,768]{1,0:T(8,128)(2,1)S(1)}, bf16[128,768]{1,0:T(8,128)(2,1)S(1)}, u32[]{:S(2)}, u32[]{:S(2)}) %collective-permute-start.10) | collective-permute-done | bytes 196640 | tf_op jit(solution)/shard_map/ppermute | solution.py:245
  25.2 2.7 %collective-permute-start.21 = (bf16[256,768]{1,0:T(8,128)(2,1)S(1)}, bf16[256,768]{1,0:T(8,128)(2,1)S(1)}, u32[]{:S(2)}, u32[]{:S(2)}) collective-permute-start(bf16[256,768]{1,0:T(8,128)(2,1)S(1)} %get-tuple-element.59._), channel_id=1, source_target_pairs={{0,16},{4,20},{8,24},{12,28},{16,0},{20,4},{24,8},{28,12},{1,17},{... | collective-permute-start | bytes 1179656 | tf_op jit(solution)/shard_map/ppermute | solution.py:245
  28.3 0.8 %shard_map.82 = (bf16[256,768]{1,0:T(8,128)(2,1)S(1)}, f32[256,768]{1,0:T(8,128)S(1)}, bf16[384,256]{1,0:T(8,128)(2,1)S(1)}, bf16[384,256]{1,0:T(8,128)(2,1)S(1)...) custom-call(bf16[192,512]{1,0:T(8,128)(2,1)S(1)} %get-tuple-element.55.p0, ...), custom_call_target="tpu_custom_call" | custom-call | tf_op jit(solution)/shard_map/pallas_call | solution.py:226
  29.1 1.7 %collective-permute-start.22 = (bf16[256,768]{1,0:T(8,128)(2,1)S(1)}, bf16[256,768]{1,0:T(8,128)(2,1)S(1)}, u32[]{:S(2)}, u32[]{:S(2)}) collective-permute-start(bf16[256,768]{1,0:T(8,128)(2,1)S(1)} %get-tuple-element.72), channel_id=1, source_target_pairs={{0,8},{4,12},{8,0},{12,4},{16,24},{20,28},{24,16},{28,20},{1,9},{5... | collective-permute-start | bytes 1179656 | tf_op jit(solution)/shard_map/ppermute | solution.py:245
  31.3 0.9 %collective-permute-done.16.refs_5_ = bf16[384,256]{1,0:T(8,128)(2,1)S(1)} collective-permute-done((bf16[384,256]{1,0:T(8,128)(2,1)S(1)}, bf16[384,256]{1,0:T(8,128)(2,1)S(1)}, u32[]{:S(2)}, u32[]{:S(2)}) %collective-permute-start.16) | collective-permute-done | bytes 196640 | tf_op jit(solution)/shard_map/ppermute | solution.py:245
  32.8 2.4 %shard_map.83 = (bf16[384,768]{1,0:T(8,128)(2,1)}, f32[8,128]{1,0:T(8,128)S(1)}, f32[8,128]{1,0:T(8,128)S(1)}, f32[8,128]{1,0:T(8,128)S(1)}, f32[8,128]{1,0:T(8,128)S(1)}) custom-call(bf16[384,256]{1,0:T(8,128)(2,1)S(1)} %get-tuple-element.44.refs_0_, bf16[384,256]{1,0:T(8,128)(2,1)S(1)} %collective-permute-done.6.refs_1_, ...), custom_call_target="tpu_custom_call" | custom-call | tf_op jit(solution)/shard_map/pallas_call | solution.py:226
  35.2 1.6 %collective-permute-start.18 = (f32[8,128]{1,0:T(8,128)S(1)}, f32[8,128]{1,0:T(8,128)S(1)}, u32[]{:S(2)}, u32[]{:S(2)}) collective-permute-start(f32[8,128]{1,0:T(8,128)S(1)} %get-tuple-element.66), channel_id=1, source_target_pairs={{0,1},{1,0},{2,3},{3,2},{4,5},{5,4},{6,7},{7,6},{8,9},{9,8},{10,11... | collective-permute-start | bytes 12296 | tf_op jit(solution)/shard_map/ppermute | solution.py:245
  37.5 1.2 %collective-permute-start.20 = (f32[8,128]{1,0:T(8,128)S(1)}, f32[8,128]{1,0:T(8,128)S(1)}, u32[]{:S(2)}, u32[]{:S(2)}) collective-permute-start(f32[8,128]{1,0:T(8,128)S(1)} %get-tuple-element.68), channel_id=1, source_target_pairs={{0,3},{1,2},{2,1},{3,0},{4,7},{5,6},{6,5},{7,4},{8,11},{9,10},{10,... | collective-permute-start | bytes 12296 | tf_op jit(solution)/shard_map/ppermute | solution.py:245
  38.8 1.6 %collective-permute-done.19.b2 = f32[8,128]{1,0:T(8,128)S(1)} collective-permute-done((f32[8,128]{1,0:T(8,128)S(1)}, f32[8,128]{1,0:T(8,128)S(1)}, u32[]{:S(2)}, u32[]{:S(2)}) %collective-permute-start.19) | collective-permute-done | bytes 4128 | tf_op jit(solution)/shard_map/ppermute | solution.py:245
  40.3 1.6 %collective-permute-done.20.b3 = f32[8,128]{1,0:T(8,128)S(1)} collective-permute-done((f32[8,128]{1,0:T(8,128)S(1)}, f32[8,128]{1,0:T(8,128)S(1)}, u32[]{:S(2)}, u32[]{:S(2)}) %collective-permute-start.20) | collective-permute-done | bytes 4128 | tf_op jit(solution)/shard_map/ppermute | solution.py:245
  42.0 2.2 %collective-permute-done.21.far_ref = bf16[256,768]{1,0:T(8,128)(2,1)S(1)} collective-permute-done((bf16[256,768]{1,0:T(8,128)(2,1)S(1)}, bf16[256,768]{1,0:T(8,128)(2,1)S(1)}, u32[]{:S(2)}, u32[]{:S(2)}) %collective-permute-start.21) | collective-permute-done | bytes 393248 | tf_op jit(solution)/shard_map/ppermute | solution.py:245
  45.2 0.9 %add_bitcast_fusion = f32[1,256,768]{2,1,0:T(8,128)} fusion(f32[256,768]{1,0:T(8,128)S(1)} %get-tuple-element.71, bf16[256,768]{1,0:T(8,128)(2,1)S(1)} %collective-permute-done.22), kind=kLoop, calls=%fused_computation | loop fusion | flops 393216 | bytes 1966080 | tf_op jit(solution)/shard_map/broadcast_in_dim | solution.py:318
  (42 shorter events, 8.7 us)
Async XLA Ops:
  0.6 3.0 %collective-permute-start = (bf16[128,2048]{1,0:T(8,128)(2,1)}, bf16[128,2048]{1,0:T(8,128)(2,1)S(1)}, u32[]{:S(2)}, u32[]{:S(2)}) collective-permute-start(bf16[128,2048]{1,0:T(8,128)(2,1)} %from_ref.1), channel_id=1, source_target_pairs={{0,4},{4,0},{8,12},{12,8},{16,20},{20,16},{24,28},{28,24},{1,5},{5... | collective-permute-start | bytes 1572872 | tf_op jit(solution)/shard_map/ppermute | solution.py:245
  1.1 10.8 %collective-permute-start.5 = (bf16[384,768]{1,0:T(8,128)(2,1)}, bf16[384,768]{1,0:T(8,128)(2,1)S(1)}, u32[]{:S(2)}, u32[]{:S(2)}) collective-permute-start(bf16[384,768]{1,0:T(8,128)(2,1)} %bitcast.9), channel_id=1, source_target_pairs={{0,4},{4,0},{8,12},{12,8},{16,20},{20,16},{24,28},{28,24},{1,5},{5... | collective-permute-start | bytes 1769480 | tf_op jit(solution)/shard_map/ppermute | solution.py:245
  2.0 1.6 %collective-permute-start.1 = (bf16[16,128]{1,0:T(8,128)(2,1)S(1)}, bf16[16,128]{1,0:T(8,128)(2,1)S(1)}, u32[]{:S(2)}, u32[]{:S(2)}) collective-permute-start(bf16[16,128]{1,0:T(8,128)(2,1)S(1)} %fusion.marks_ref), channel_id=1, source_target_pairs={{0,4},{4,0},{8,12},{12,8},{16,20},{20,16},{24,28},{28,24},{1,5},{5... | collective-permute-start | bytes 12296 | tf_op jit(solution)/shard_map/ppermute | solution.py:245
  4.2 9.3 %collective-permute-start.2 = (bf16[208,256]{1,0:T(8,128)(2,1)S(1)}, bf16[208,256]{1,0:T(8,128)(2,1)S(1)}, u32[]{:S(2)}, u32[]{:S(2)}) collective-permute-start(bf16[208,256]{1,0:T(8,128)(2,1)S(1)} %get-tuple-element.39), channel_id=1, source_target_pairs={{0,1},{1,0},{2,3},{3,2},{4,5},{5,4},{6,7},{7,6},{8,9},{9,8},{10,11... | collective-permute-start | bytes 319496 | tf_op jit(solution)/shard_map/ppermute | solution.py:245
  7.0 6.8 %collective-permute-start.3 = (bf16[208,256]{1,0:T(8,128)(2,1)S(1)}, bf16[208,256]{1,0:T(8,128)(2,1)S(1)}, u32[]{:S(2)}, u32[]{:S(2)}) collective-permute-start(bf16[208,256]{1,0:T(8,128)(2,1)S(1)} %get-tuple-element.40), channel_id=1, source_target_pairs={{0,2},{1,3},{2,0},{3,1},{4,6},{5,7},{6,4},{7,5},{8,10},{9,11},{10,... | collective-permute-start | bytes 319496 | tf_op jit(solution)/shard_map/ppermute | solution.py:245
  8.6 6.5 %collective-permute-start.4 = (bf16[208,256]{1,0:T(8,128)(2,1)S(1)}, bf16[208,256]{1,0:T(8,128)(2,1)S(1)}, u32[]{:S(2)}, u32[]{:S(2)}) collective-permute-start(bf16[208,256]{1,0:T(8,128)(2,1)S(1)} %get-tuple-element.41), channel_id=1, source_target_pairs={{0,3},{1,2},{2,1},{3,0},{4,7},{5,6},{6,5},{7,4},{8,11},{9,10},{10,... | collective-permute-start | bytes 319496 | tf_op jit(solution)/shard_map/ppermute | solution.py:245
  9.9 8.3 %collective-permute-start.7 = (bf16[192,256]{1,0:T(8,128)(2,1)S(1)}, bf16[192,256]{1,0:T(8,128)(2,1)S(1)}, u32[]{:S(2)}, u32[]{:S(2)}) collective-permute-start(bf16[192,256]{1,0:T(8,128)(2,1)S(1)} %get-tuple-element.47), channel_id=1, source_target_pairs={{0,1},{1,0},{2,3},{3,2},{4,5},{5,4},{6,7},{7,6},{8,9},{9,8},{10,11... | collective-permute-start | bytes 294920 | tf_op jit(solution)/shard_map/ppermute | solution.py:245
  12.0 7.2 %collective-permute-start.8 = (bf16[192,256]{1,0:T(8,128)(2,1)S(1)}, bf16[192,256]{1,0:T(8,128)(2,1)S(1)}, u32[]{:S(2)}, u32[]{:S(2)}) collective-permute-start(bf16[192,256]{1,0:T(8,128)(2,1)S(1)} %get-tuple-element.48), channel_id=1, source_target_pairs={{0,2},{1,3},{2,0},{3,1},{4,6},{5,7},{6,4},{7,5},{8,10},{9,11},{10,... | collective-permute-start | bytes 294920 | tf_op jit(solution)/shard_map/ppermute | solution.py:245
  13.5 6.8 %collective-permute-start.9 = (bf16[192,256]{1,0:T(8,128)(2,1)S(1)}, bf16[192,256]{1,0:T(8,128)(2,1)S(1)}, u32[]{:S(2)}, u32[]{:S(2)}) collective-permute-start(bf16[192,256]{1,0:T(8,128)(2,1)S(1)} %get-tuple-element.49), channel_id=1, source_target_pairs={{0,3},{1,2},{2,1},{3,0},{4,7},{5,6},{6,5},{7,4},{8,11},{9,10},{10,... | collective-permute-start | bytes 294920 | tf_op jit(solution)/shard_map/ppermute | solution.py:245
  15.8 17.0 %copy-start = (bf16[1,768,2048]{2,1,0:T(8,128)(2,1)S(1)}, bf16[1,768,2048]{2,1,0:T(8,128)(2,1)}, u32[]{:S(2)}) copy-start(bf16[1,768,2048]{2,1,0:T(8,128)(2,1)} %param.9) | copy-start | bytes 9437188
  15.8 6.8 %collective-permute-start.11 = (bf16[128,768]{1,0:T(8,128)(2,1)S(1)}, bf16[128,768]{1,0:T(8,128)(2,1)S(1)}, u32[]{:S(2)}, u32[]{:S(2)}) collective-permute-start(bf16[128,768]{1,0:T(8,128)(2,1)S(1)} %get-tuple-element.52), channel_id=1, source_target_pairs={{0,8},{4,12},{8,0},{12,4},{16,24},{20,28},{24,16},{28,20},{1,9},{5... | collective-permute-start | bytes 589832 | tf_op jit(solution)/shard_map/ppermute | solution.py:245
  17.4 7.2 %collective-permute-start.10 = (bf16[128,768]{1,0:T(8,128)(2,1)S(1)}, bf16[128,768]{1,0:T(8,128)(2,1)S(1)}, u32[]{:S(2)}, u32[]{:S(2)}) collective-permute-start(bf16[128,768]{1,0:T(8,128)(2,1)S(1)} %get-tuple-element.51.outs_0_), channel_id=1, source_target_pairs={{0,8},{4,12},{8,0},{12,4},{16,24},{20,28},{24,16},{28,20},{1,9},{5... | collective-permute-start | bytes 589832 | tf_op jit(solution)/shard_map/ppermute | solution.py:245
  18.3 9.6 %collective-permute-start.13 = (bf16[192,512]{1,0:T(8,128)(2,1)S(1)}, bf16[192,512]{1,0:T(8,128)(2,1)S(1)}, u32[]{:S(2)}, u32[]{:S(2)}) collective-permute-start(bf16[192,512]{1,0:T(8,128)(2,1)S(1)} %get-tuple-element.56), channel_id=1, source_target_pairs={{0,1},{1,0},{2,3},{3,2},{4,5},{5,4},{6,7},{7,6},{8,9},{9,8},{10,11... | collective-permute-start | bytes 589832 | tf_op jit(solution)/shard_map/ppermute | solution.py:245
  19.1 9.2 %collective-permute-start.14 = (bf16[192,512]{1,0:T(8,128)(2,1)S(1)}, bf16[192,512]{1,0:T(8,128)(2,1)S(1)}, u32[]{:S(2)}, u32[]{:S(2)}) collective-permute-start(bf16[192,512]{1,0:T(8,128)(2,1)S(1)} %get-tuple-element.57), channel_id=1, source_target_pairs={{0,2},{1,3},{2,0},{3,1},{4,6},{5,7},{6,4},{7,5},{8,10},{9,11},{10,... | collective-permute-start | bytes 589832 | tf_op jit(solution)/shard_map/ppermute | solution.py:245
  20.3 8.0 %collective-permute-start.15 = (bf16[192,512]{1,0:T(8,128)(2,1)S(1)}, bf16[192,512]{1,0:T(8,128)(2,1)S(1)}, u32[]{:S(2)}, u32[]{:S(2)}) collective-permute-start(bf16[192,512]{1,0:T(8,128)(2,1)S(1)} %get-tuple-element.58), channel_id=1, source_target_pairs={{0,3},{1,2},{2,1},{3,0},{4,7},{5,6},{6,5},{7,4},{8,11},{9,10},{10,... | collective-permute-start | bytes 589832 | tf_op jit(solution)/shard_map/ppermute | solution.py:245
  22.6 8.7 %collective-permute-start.6 = (bf16[384,256]{1,0:T(8,128)(2,1)S(1)}, bf16[384,256]{1,0:T(8,128)(2,1)S(1)}, u32[]{:S(2)}, u32[]{:S(2)}) collective-permute-start(bf16[384,256]{1,0:T(8,128)(2,1)S(1)} %get-tuple-element.45), channel_id=1, source_target_pairs={{0,4},{4,0},{8,12},{12,8},{16,20},{20,16},{24,28},{28,24},{1,5},{5... | collective-permute-start | bytes 589832 | tf_op jit(solution)/shard_map/ppermute | solution.py:245
  25.2 18.9 %collective-permute-start.21 = (bf16[256,768]{1,0:T(8,128)(2,1)S(1)}, bf16[256,768]{1,0:T(8,128)(2,1)S(1)}, u32[]{:S(2)}, u32[]{:S(2)}) collective-permute-start(bf16[256,768]{1,0:T(8,128)(2,1)S(1)} %get-tuple-element.59._), channel_id=1, source_target_pairs={{0,16},{4,20},{8,24},{12,28},{16,0},{20,4},{24,8},{28,12},{1,17},{... | collective-permute-start | bytes 1179656 | tf_op jit(solution)/shard_map/ppermute | solution.py:245
  29.1 16.1 %collective-permute-start.22 = (bf16[256,768]{1,0:T(8,128)(2,1)S(1)}, bf16[256,768]{1,0:T(8,128)(2,1)S(1)}, u32[]{:S(2)}, u32[]{:S(2)}) collective-permute-start(bf16[256,768]{1,0:T(8,128)(2,1)S(1)} %get-tuple-element.72), channel_id=1, source_target_pairs={{0,8},{4,12},{8,0},{12,4},{16,24},{20,28},{24,16},{28,20},{1,9},{5... | collective-permute-start | bytes 1179656 | tf_op jit(solution)/shard_map/ppermute | solution.py:245
  30.8 1.4 %collective-permute-start.16 = (bf16[384,256]{1,0:T(8,128)(2,1)S(1)}, bf16[384,256]{1,0:T(8,128)(2,1)S(1)}, u32[]{:S(2)}, u32[]{:S(2)}) collective-permute-start(bf16[384,256]{1,0:T(8,128)(2,1)S(1)} %get-tuple-element.61), channel_id=1, source_target_pairs={{0,4},{4,0},{8,12},{12,8},{16,20},{20,16},{24,28},{28,24},{1,5},{5... | collective-permute-start | bytes 589832 | tf_op jit(solution)/shard_map/ppermute | solution.py:245
  30.8 1.7 %collective-permute-start.17 = (bf16[384,256]{1,0:T(8,128)(2,1)S(1)}, bf16[384,256]{1,0:T(8,128)(2,1)S(1)}, u32[]{:S(2)}, u32[]{:S(2)}) collective-permute-start(bf16[384,256]{1,0:T(8,128)(2,1)S(1)} %get-tuple-element.63), channel_id=1, source_target_pairs={{0,4},{4,0},{8,12},{12,8},{16,20},{20,16},{24,28},{28,24},{1,5},{5... | collective-permute-start | bytes 589832 | tf_op jit(solution)/shard_map/ppermute | solution.py:245
  31.3 1.5 %collective-permute-start.12 = (bf16[384,256]{1,0:T(8,128)(2,1)S(1)}, bf16[384,256]{1,0:T(8,128)(2,1)S(1)}, u32[]{:S(2)}, u32[]{:S(2)}) collective-permute-start(bf16[384,256]{1,0:T(8,128)(2,1)S(1)} %get-tuple-element.54), channel_id=1, source_target_pairs={{0,4},{4,0},{8,12},{12,8},{16,20},{20,16},{24,28},{28,24},{1,5},{5... | collective-permute-start | bytes 589832 | tf_op jit(solution)/shard_map/ppermute | solution.py:245
  35.2 3.6 %collective-permute-start.18 = (f32[8,128]{1,0:T(8,128)S(1)}, f32[8,128]{1,0:T(8,128)S(1)}, u32[]{:S(2)}, u32[]{:S(2)}) collective-permute-start(f32[8,128]{1,0:T(8,128)S(1)} %get-tuple-element.66), channel_id=1, source_target_pairs={{0,1},{1,0},{2,3},{3,2},{4,5},{5,4},{6,7},{7,6},{8,9},{9,8},{10,11... | collective-permute-start | bytes 12296 | tf_op jit(solution)/shard_map/ppermute | solution.py:245
  36.7 3.6 %collective-permute-start.19 = (f32[8,128]{1,0:T(8,128)S(1)}, f32[8,128]{1,0:T(8,128)S(1)}, u32[]{:S(2)}, u32[]{:S(2)}) collective-permute-start(f32[8,128]{1,0:T(8,128)S(1)} %get-tuple-element.67), channel_id=1, source_target_pairs={{0,2},{1,3},{2,0},{3,1},{4,6},{5,7},{6,4},{7,5},{8,10},{9,11},{10,... | collective-permute-start | bytes 12296 | tf_op jit(solution)/shard_map/ppermute | solution.py:245
  37.5 4.5 %collective-permute-start.20 = (f32[8,128]{1,0:T(8,128)S(1)}, f32[8,128]{1,0:T(8,128)S(1)}, u32[]{:S(2)}, u32[]{:S(2)}) collective-permute-start(f32[8,128]{1,0:T(8,128)S(1)} %get-tuple-element.68), channel_id=1, source_target_pairs={{0,3},{1,2},{2,1},{3,0},{4,7},{5,6},{6,5},{7,4},{8,11},{9,10},{10,... | collective-permute-start | bytes 12296 | tf_op jit(solution)/shard_map/ppermute | solution.py:245
  (3 other events, 17.1 us)

commit v6 on v5

--- a/solution.py
+++ b/solution.py
@@ -174,12 +174,10 @@
     sum_ref[half:, :] = (part[half:, :] + high_ref[...].astype(F32)).astype(BF16)
 
 
-def last_kernel(capacity, p0, p1, p2, p3, scaled_ref, _, part2_ref, part3_ref, own2, cross2, own3, cross3, all_ref):
-    for i, (part, own, cross) in enumerate(((part2_ref, own2, cross2), (part3_ref, own3, cross3))):
-        block = own.shape[1]
-        at = slice(i * block, (i + 1) * block)
-        split_rows((p0, p1, p2, p3), at, capacity, all_ref.at[i], own, cross)
-        part[...] = dot(all_ref[i], scaled_ref[...], ((0,), (0,))).astype(part.dtype)
+def part_kernel(capacity, column, p0, p1, p2, p3, scaled_ref, _, part_ref, own_ref, cross_ref, all_ref):
+    at = slice(column, column + own_ref.shape[1])
+    split_rows((p0, p1, p2, p3), at, capacity, all_ref, own_ref, cross_ref)
+    part_ref[...] = dot(all_ref[...], scaled_ref[...], ((0,), (0,))).astype(part_ref.dtype)
 
 
 def update_kernel(capacity, *refs):
@@ -296,12 +294,16 @@
         scratch=[pltpu.VMEM(stack, BF16)],
     )(*one, scaled, low, high)
     come1 = far(summed)
-    part2, part3, own2, cross2, own3, cross3 = call(
-        functools.partial(last_kernel, capacity),
-        [arr((block, units), BF16), arr((block, units), F32), mine, mine, mine, mine],
-        specs=[VMEM] * 5 + [ANY],
-        scratch=[pltpu.VMEM((2,) + stack, BF16)],
-    )(*rest, scaled, summed)
+    def product(column, dtype, after):
+        return call(
+            functools.partial(part_kernel, capacity, column),
+            [arr((block, units), dtype), mine, mine],
+            specs=[VMEM] * 5 + [ANY],
+            scratch=[pltpu.VMEM(stack, BF16)],
+        )(*rest, scaled, after)
+
+    part2, own2, cross2 = product(0, BF16, summed)
+    part3, own3, cross3 = product(block, F32, part2)
     come2 = near(part2)
     rows = []
     for own_k, cross_k in ((own0, cross0), (own1, cross1), (own2, cross2), (own3, cross3)):

time: 46.4 us -> 46.1 us (level)
  waiting for transfers between devices: 11.8 us -> 11.2 us
    ppermute x23, waiting for transfers between devices: 11.8 us -> 11.2 us  [over(): return lambda x: lax.ppermute(x, axis, pairs)]
    pallas_call x9 -> x10, Pallas kernels: 6.47 us -> 6.68 us  [run(): pl.pallas_call(kernel, out_shape=outs, in_specs=specs or [VMEM] * len(arg...]
  transfers between devices with their start and end apart: 23 -> 23, of which waited for: 12 -> 12; matrix products, arithmetic and copies ran while one was open for 2% -> 2% of each run, Pallas kernels for 14% -> 15%
where the time goes in v6:
time: 46.1 us; the launch traced here: 45.9 us
  starting transfers between devices  23.3 us (51%)
  waiting for transfers between devices  11.2 us (24%)
  Pallas kernels  6.68 us (14%)
  local copies, waits for them, and re-layouts  2.11 us (5%)
  other arithmetic  1.74 us (4%)
  between operations  0.76 us (2%)
    ppermute x23, starting transfers between devices, over(): return lambda x: lax.ppermute(x, axis, pairs)  23.3 us
    ppermute x23, waiting for transfers between devices, over(): return lambda x: lax.ppermute(x, axis, pairs)  11.2 us
    pallas_call x10, Pallas kernels, run(): pl.pallas_call(kernel, out_shape=outs, in_specs=specs or [VMEM] * len(arg...  6.68 us
    unnamed x8, local copies, waits for them, and re-layouts  2.11 us
    broadcast_in_dim x1, other arithmetic, per_device(): return (grad_hidden[None], gate_grad.T, weight_grad[None])  0.95 us
  transfers between devices with their start and end apart: 23, of which 12 were waited for; matrix products, arithmetic and copies ran while one was open for 2% of the time, Pallas kernels for 15%

profile of v6, /device:TPU:0, one launch (start us, length us, event | category | flops | bytes accessed | tf_op | source)
XLA Modules:
  0.0 45.9 jit_solution(15035778170638313026)
XLA Ops:
  1.2 0.8 %fusion.marks_ref = bf16[16,128]{1,0:T(8,128)(2,1)S(1)} fusion(s32[8,128]{1,0:T(8,128)} %bitcast.11, s32[16]{0:T(128)S(1)} %iota_multiply_fusion, bf16[8,128]{1,0:T(8,128)(2,1)} %bitcast.13), kind=kLoop, calls=%fused_computation.2 | loop fusion | flops 47104 | bytes 10304 | tf_op jit(solution)/shard_map/reduce_max | solution.py:259
  2.5 1.0 %copy-done.2 = bf16[128,2048]{1,0:T(8,128)(2,1)S(1)} copy-done((bf16[128,2048]{1,0:T(8,128)(2,1)S(1)}, bf16[128,2048]{1,0:T(8,128)(2,1)}, u32[]{:S(2)}) %copy-start.2) | copy-done | bytes 524312
  4.2 2.8 %collective-permute-start.2 = (bf16[208,256]{1,0:T(8,128)(2,1)S(1)}, bf16[208,256]{1,0:T(8,128)(2,1)S(1)}, u32[]{:S(2)}, u32[]{:S(2)}) collective-permute-start(bf16[208,256]{1,0:T(8,128)(2,1)S(1)} %get-tuple-element.39), channel_id=1, source_target_pairs={{0,1},{1,0},{2,3},{3,2},{4,5},{5,4},{6,7},{7,6},{8,9},{9,8},{10,11... | collective-permute-start | bytes 319496 | tf_op jit(solution)/shard_map/ppermute | solution.py:243
  7.0 1.5 %collective-permute-start.3 = (bf16[208,256]{1,0:T(8,128)(2,1)S(1)}, bf16[208,256]{1,0:T(8,128)(2,1)S(1)}, u32[]{:S(2)}, u32[]{:S(2)}) collective-permute-start(bf16[208,256]{1,0:T(8,128)(2,1)S(1)} %get-tuple-element.40), channel_id=1, source_target_pairs={{0,2},{1,3},{2,0},{3,1},{4,6},{5,7},{6,4},{7,5},{8,10},{9,11},{10,... | collective-permute-start | bytes 319496 | tf_op jit(solution)/shard_map/ppermute | solution.py:243
  8.6 1.1 %copy-done.1 = bf16[1,384,768]{2,1,0:T(8,128)(2,1)S(1)} copy-done((bf16[1,384,768]{2,1,0:T(8,128)(2,1)S(1)}, bf16[1,384,768]{2,1,0:T(8,128)(2,1)}, u32[]{:S(2)}) %copy-start.1) | copy-done | bytes 589848
  9.9 2.0 %collective-permute-start.7 = (bf16[192,256]{1,0:T(8,128)(2,1)S(1)}, bf16[192,256]{1,0:T(8,128)(2,1)S(1)}, u32[]{:S(2)}, u32[]{:S(2)}) collective-permute-start(bf16[192,256]{1,0:T(8,128)(2,1)S(1)} %get-tuple-element.47), channel_id=1, source_target_pairs={{0,1},{1,0},{2,3},{3,2},{4,5},{5,4},{6,7},{7,6},{8,9},{9,8},{10,11... | collective-permute-start | bytes 294920 | tf_op jit(solution)/shard_map/ppermute | solution.py:243
  12.0 1.5 %collective-permute-start.8 = (bf16[192,256]{1,0:T(8,128)(2,1)S(1)}, bf16[192,256]{1,0:T(8,128)(2,1)S(1)}, u32[]{:S(2)}, u32[]{:S(2)}) collective-permute-start(bf16[192,256]{1,0:T(8,128)(2,1)S(1)} %get-tuple-element.48), channel_id=1, source_target_pairs={{0,2},{1,3},{2,0},{3,1},{4,6},{5,7},{6,4},{7,5},{8,10},{9,11},{10,... | collective-permute-start | bytes 294920 | tf_op jit(solution)/shard_map/ppermute | solution.py:243
  13.8 1.2 %collective-permute-done.4.p3.refs_11_ = bf16[208,256]{1,0:T(8,128)(2,1)S(1)} collective-permute-done((bf16[208,256]{1,0:T(8,128)(2,1)S(1)}, bf16[208,256]{1,0:T(8,128)(2,1)S(1)}, u32[]{:S(2)}, u32[]{:S(2)}) %collective-permute-start.4) | collective-permute-done | bytes 106528 | tf_op jit(solution)/shard_map/ppermute | solution.py:243
  15.0 0.8 %shard_map.79 = (bf16[128,768]{1,0:T(8,128)(2,1)S(1)}, bf16[128,768]{1,0:T(8,128)(2,1)S(1)}, bf16[768,768]{1,0:T(8,128)(2,1)S(1)}, bf16[384,256]{1,0:T(8,128)(2,1)S(1)}, bf16[384,256]{1,0:T(8,128)(2,1)S(1)}) custom-call(bf16[208,256]{1,0:T(8,128)(2,1)S(1)} %get-tuple-element.38.p0.refs_8_, bf16[208,256]{1,0:T(8,128)(2,1)S(1)} %collective-permute-done.2.p1.refs_9_, ...), custom_call_target="tpu_custom_call" | custom-call | tf_op jit(solution)/shard_map/pallas_call | solution.py:224
  15.8 1.6 %collective-permute-start.10 = (bf16[128,768]{1,0:T(8,128)(2,1)S(1)}, bf16[128,768]{1,0:T(8,128)(2,1)S(1)}, u32[]{:S(2)}, u32[]{:S(2)}) collective-permute-start(bf16[128,768]{1,0:T(8,128)(2,1)S(1)} %get-tuple-element.51.outs_0_), channel_id=1, source_target_pairs={{0,8},{4,12},{8,0},{12,4},{16,24},{20,28},{24,16},{28,20},{1,9},{5... | collective-permute-start | bytes 589832 | tf_op jit(solution)/shard_map/ppermute | solution.py:243
  18.3 0.8 %collective-permute-start.13 = (bf16[192,512]{1,0:T(8,128)(2,1)S(1)}, bf16[192,512]{1,0:T(8,128)(2,1)S(1)}, u32[]{:S(2)}, u32[]{:S(2)}) collective-permute-start(bf16[192,512]{1,0:T(8,128)(2,1)S(1)} %get-tuple-element.56), channel_id=1, source_target_pairs={{0,1},{1,0},{2,3},{3,2},{4,5},{5,4},{6,7},{7,6},{8,9},{9,8},{10,11... | collective-permute-start | bytes 589832 | tf_op jit(solution)/shard_map/ppermute | solution.py:243
  19.1 1.2 %collective-permute-start.14 = (bf16[192,512]{1,0:T(8,128)(2,1)S(1)}, bf16[192,512]{1,0:T(8,128)(2,1)S(1)}, u32[]{:S(2)}, u32[]{:S(2)}) collective-permute-start(bf16[192,512]{1,0:T(8,128)(2,1)S(1)} %get-tuple-element.57), channel_id=1, source_target_pairs={{0,2},{1,3},{2,0},{3,1},{4,6},{5,7},{6,4},{7,5},{8,10},{9,11},{10,... | collective-permute-start | bytes 589832 | tf_op jit(solution)/shard_map/ppermute | solution.py:243
  20.3 1.5 %collective-permute-start.15 = (bf16[192,512]{1,0:T(8,128)(2,1)S(1)}, bf16[192,512]{1,0:T(8,128)(2,1)S(1)}, u32[]{:S(2)}, u32[]{:S(2)}) collective-permute-start(bf16[192,512]{1,0:T(8,128)(2,1)S(1)} %get-tuple-element.58), channel_id=1, source_target_pairs={{0,3},{1,2},{2,1},{3,0},{4,7},{5,6},{6,5},{7,4},{8,11},{9,10},{10,... | collective-permute-start | bytes 589832 | tf_op jit(solution)/shard_map/ppermute | solution.py:243
  22.6 2.1 %collective-permute-done.11.high_ref = bf16[128,768]{1,0:T(8,128)(2,1)S(1)} collective-permute-done((bf16[128,768]{1,0:T(8,128)(2,1)S(1)}, bf16[128,768]{1,0:T(8,128)(2,1)S(1)}, u32[]{:S(2)}, u32[]{:S(2)}) %collective-permute-start.11) | collective-permute-done | bytes 196640 | tf_op jit(solution)/shard_map/ppermute | solution.py:243
  25.2 2.6 %collective-permute-start.21 = (bf16[256,768]{1,0:T(8,128)(2,1)S(1)}, bf16[256,768]{1,0:T(8,128)(2,1)S(1)}, u32[]{:S(2)}, u32[]{:S(2)}) collective-permute-start(bf16[256,768]{1,0:T(8,128)(2,1)S(1)} %get-tuple-element.59._), channel_id=1, source_target_pairs={{0,16},{4,20},{8,24},{12,28},{16,0},{20,4},{24,8},{28,12},{1,17},{... | collective-permute-start | bytes 1179656 | tf_op jit(solution)/shard_map/ppermute | solution.py:243
  28.8 1.6 %collective-permute-start.22 = (bf16[256,768]{1,0:T(8,128)(2,1)S(1)}, bf16[256,768]{1,0:T(8,128)(2,1)S(1)}, u32[]{:S(2)}, u32[]{:S(2)}) collective-permute-start(bf16[256,768]{1,0:T(8,128)(2,1)S(1)} %get-tuple-element.62._), channel_id=1, source_target_pairs={{0,8},{4,12},{8,0},{12,4},{16,24},{20,28},{24,16},{28,20},{1,9},{5... | collective-permute-start | bytes 1179656 | tf_op jit(solution)/shard_map/ppermute | solution.py:243
  32.2 0.8 %collective-permute-done.17.refs_7_ = bf16[384,256]{1,0:T(8,128)(2,1)S(1)} collective-permute-done((bf16[384,256]{1,0:T(8,128)(2,1)S(1)}, bf16[384,256]{1,0:T(8,128)(2,1)S(1)}, u32[]{:S(2)}, u32[]{:S(2)}) %collective-permute-start.17) | collective-permute-done | bytes 196640 | tf_op jit(solution)/shard_map/ppermute | solution.py:243
  33.0 2.4 %shard_map.84 = (bf16[384,768]{1,0:T(8,128)(2,1)}, f32[8,128]{1,0:T(8,128)S(1)}, f32[8,128]{1,0:T(8,128)S(1)}, f32[8,128]{1,0:T(8,128)S(1)}, f32[8,128]{1,0:T(8,128)S(1)}) custom-call(bf16[384,256]{1,0:T(8,128)(2,1)S(1)} %get-tuple-element.44.refs_0_, bf16[384,256]{1,0:T(8,128)(2,1)S(1)} %collective-permute-done.6.refs_1_, ...), custom_call_target="tpu_custom_call" | custom-call | tf_op jit(solution)/shard_map/pallas_call | solution.py:224
  35.4 1.6 %collective-permute-start.18 = (f32[8,128]{1,0:T(8,128)S(1)}, f32[8,128]{1,0:T(8,128)S(1)}, u32[]{:S(2)}, u32[]{:S(2)}) collective-permute-start(f32[8,128]{1,0:T(8,128)S(1)} %get-tuple-element.67), channel_id=1, source_target_pairs={{0,1},{1,0},{2,3},{3,2},{4,5},{5,4},{6,7},{7,6},{8,9},{9,8},{10,11... | collective-permute-start | bytes 12296 | tf_op jit(solution)/shard_map/ppermute | solution.py:243
  37.7 1.2 %collective-permute-start.20 = (f32[8,128]{1,0:T(8,128)S(1)}, f32[8,128]{1,0:T(8,128)S(1)}, u32[]{:S(2)}, u32[]{:S(2)}) collective-permute-start(f32[8,128]{1,0:T(8,128)S(1)} %get-tuple-element.69), channel_id=1, source_target_pairs={{0,3},{1,2},{2,1},{3,0},{4,7},{5,6},{6,5},{7,4},{8,11},{9,10},{10,... | collective-permute-start | bytes 12296 | tf_op jit(solution)/shard_map/ppermute | solution.py:243
  39.0 1.6 %collective-permute-done.19.b2 = f32[8,128]{1,0:T(8,128)S(1)} collective-permute-done((f32[8,128]{1,0:T(8,128)S(1)}, f32[8,128]{1,0:T(8,128)S(1)}, u32[]{:S(2)}, u32[]{:S(2)}) %collective-permute-start.19) | collective-permute-done | bytes 4128 | tf_op jit(solution)/shard_map/ppermute | solution.py:243
  40.6 1.6 %collective-permute-done.20.b3 = f32[8,128]{1,0:T(8,128)S(1)} collective-permute-done((f32[8,128]{1,0:T(8,128)S(1)}, f32[8,128]{1,0:T(8,128)S(1)}, u32[]{:S(2)}, u32[]{:S(2)}) %collective-permute-start.20) | collective-permute-done | bytes 4128 | tf_op jit(solution)/shard_map/ppermute | solution.py:243
  42.2 1.9 %collective-permute-done.21.far_ref = bf16[256,768]{1,0:T(8,128)(2,1)S(1)} collective-permute-done((bf16[256,768]{1,0:T(8,128)(2,1)S(1)}, bf16[256,768]{1,0:T(8,128)(2,1)S(1)}, u32[]{:S(2)}, u32[]{:S(2)}) %collective-permute-start.21) | collective-permute-done | bytes 393248 | tf_op jit(solution)/shard_map/ppermute | solution.py:243
  44.9 0.9 %add_bitcast_fusion = f32[1,256,768]{2,1,0:T(8,128)} fusion(f32[256,768]{1,0:T(8,128)S(1)} %get-tuple-element.72, bf16[256,768]{1,0:T(8,128)(2,1)S(1)} %collective-permute-done.22), kind=kLoop, calls=%fused_computation | loop fusion | flops 393216 | bytes 1966080 | tf_op jit(solution)/shard_map/broadcast_in_dim | solution.py:320
  (43 shorter events, 8.7 us)
Async XLA Ops:
  0.6 3.0 %collective-permute-start = (bf16[128,2048]{1,0:T(8,128)(2,1)}, bf16[128,2048]{1,0:T(8,128)(2,1)S(1)}, u32[]{:S(2)}, u32[]{:S(2)}) collective-permute-start(bf16[128,2048]{1,0:T(8,128)(2,1)} %from_ref.1), channel_id=1, source_target_pairs={{0,4},{4,0},{8,12},{12,8},{16,20},{20,16},{24,28},{28,24},{1,5},{5... | collective-permute-start | bytes 1572872 | tf_op jit(solution)/shard_map/ppermute | solution.py:243
  1.1 10.8 %collective-permute-start.5 = (bf16[384,768]{1,0:T(8,128)(2,1)}, bf16[384,768]{1,0:T(8,128)(2,1)S(1)}, u32[]{:S(2)}, u32[]{:S(2)}) collective-permute-start(bf16[384,768]{1,0:T(8,128)(2,1)} %bitcast.9), channel_id=1, source_target_pairs={{0,4},{4,0},{8,12},{12,8},{16,20},{20,16},{24,28},{28,24},{1,5},{5... | collective-permute-start | bytes 1769480 | tf_op jit(solution)/shard_map/ppermute | solution.py:243
  2.0 1.6 %collective-permute-start.1 = (bf16[16,128]{1,0:T(8,128)(2,1)S(1)}, bf16[16,128]{1,0:T(8,128)(2,1)S(1)}, u32[]{:S(2)}, u32[]{:S(2)}) collective-permute-start(bf16[16,128]{1,0:T(8,128)(2,1)S(1)} %fusion.marks_ref), channel_id=1, source_target_pairs={{0,4},{4,0},{8,12},{12,8},{16,20},{20,16},{24,28},{28,24},{1,5},{5... | collective-permute-start | bytes 12296 | tf_op jit(solution)/shard_map/ppermute | solution.py:243
  4.2 9.3 %collective-permute-start.2 = (bf16[208,256]{1,0:T(8,128)(2,1)S(1)}, bf16[208,256]{1,0:T(8,128)(2,1)S(1)}, u32[]{:S(2)}, u32[]{:S(2)}) collective-permute-start(bf16[208,256]{1,0:T(8,128)(2,1)S(1)} %get-tuple-element.39), channel_id=1, source_target_pairs={{0,1},{1,0},{2,3},{3,2},{4,5},{5,4},{6,7},{7,6},{8,9},{9,8},{10,11... | collective-permute-start | bytes 319496 | tf_op jit(solution)/shard_map/ppermute | solution.py:243
  7.0 6.8 %collective-permute-start.3 = (bf16[208,256]{1,0:T(8,128)(2,1)S(1)}, bf16[208,256]{1,0:T(8,128)(2,1)S(1)}, u32[]{:S(2)}, u32[]{:S(2)}) collective-permute-start(bf16[208,256]{1,0:T(8,128)(2,1)S(1)} %get-tuple-element.40), channel_id=1, source_target_pairs={{0,2},{1,3},{2,0},{3,1},{4,6},{5,7},{6,4},{7,5},{8,10},{9,11},{10,... | collective-permute-start | bytes 319496 | tf_op jit(solution)/shard_map/ppermute | solution.py:243
  8.6 6.5 %collective-permute-start.4 = (bf16[208,256]{1,0:T(8,128)(2,1)S(1)}, bf16[208,256]{1,0:T(8,128)(2,1)S(1)}, u32[]{:S(2)}, u32[]{:S(2)}) collective-permute-start(bf16[208,256]{1,0:T(8,128)(2,1)S(1)} %get-tuple-element.41), channel_id=1, source_target_pairs={{0,3},{1,2},{2,1},{3,0},{4,7},{5,6},{6,5},{7,4},{8,11},{9,10},{10,... | collective-permute-start | bytes 319496 | tf_op jit(solution)/shard_map/ppermute | solution.py:243
  9.9 8.3 %collective-permute-start.7 = (bf16[192,256]{1,0:T(8,128)(2,1)S(1)}, bf16[192,256]{1,0:T(8,128)(2,1)S(1)}, u32[]{:S(2)}, u32[]{:S(2)}) collective-permute-start(bf16[192,256]{1,0:T(8,128)(2,1)S(1)} %get-tuple-element.47), channel_id=1, source_target_pairs={{0,1},{1,0},{2,3},{3,2},{4,5},{5,4},{6,7},{7,6},{8,9},{9,8},{10,11... | collective-permute-start | bytes 294920 | tf_op jit(solution)/shard_map/ppermute | solution.py:243
  12.0 7.2 %collective-permute-start.8 = (bf16[192,256]{1,0:T(8,128)(2,1)S(1)}, bf16[192,256]{1,0:T(8,128)(2,1)S(1)}, u32[]{:S(2)}, u32[]{:S(2)}) collective-permute-start(bf16[192,256]{1,0:T(8,128)(2,1)S(1)} %get-tuple-element.48), channel_id=1, source_target_pairs={{0,2},{1,3},{2,0},{3,1},{4,6},{5,7},{6,4},{7,5},{8,10},{9,11},{10,... | collective-permute-start | bytes 294920 | tf_op jit(solution)/shard_map/ppermute | solution.py:243
  13.5 6.8 %collective-permute-start.9 = (bf16[192,256]{1,0:T(8,128)(2,1)S(1)}, bf16[192,256]{1,0:T(8,128)(2,1)S(1)}, u32[]{:S(2)}, u32[]{:S(2)}) collective-permute-start(bf16[192,256]{1,0:T(8,128)(2,1)S(1)} %get-tuple-element.49), channel_id=1, source_target_pairs={{0,3},{1,2},{2,1},{3,0},{4,7},{5,6},{6,5},{7,4},{8,11},{9,10},{10,... | collective-permute-start | bytes 294920 | tf_op jit(solution)/shard_map/ppermute | solution.py:243
  15.8 6.8 %collective-permute-start.10 = (bf16[128,768]{1,0:T(8,128)(2,1)S(1)}, bf16[128,768]{1,0:T(8,128)(2,1)S(1)}, u32[]{:S(2)}, u32[]{:S(2)}) collective-permute-start(bf16[128,768]{1,0:T(8,128)(2,1)S(1)} %get-tuple-element.51.outs_0_), channel_id=1, source_target_pairs={{0,8},{4,12},{8,0},{12,4},{16,24},{20,28},{24,16},{28,20},{1,9},{5... | collective-permute-start | bytes 589832 | tf_op jit(solution)/shard_map/ppermute | solution.py:243
  17.4 7.2 %collective-permute-start.11 = (bf16[128,768]{1,0:T(8,128)(2,1)S(1)}, bf16[128,768]{1,0:T(8,128)(2,1)S(1)}, u32[]{:S(2)}, u32[]{:S(2)}) collective-permute-start(bf16[128,768]{1,0:T(8,128)(2,1)S(1)} %get-tuple-element.52), channel_id=1, source_target_pairs={{0,8},{4,12},{8,0},{12,4},{16,24},{20,28},{24,16},{28,20},{1,9},{5... | collective-permute-start | bytes 589832 | tf_op jit(solution)/shard_map/ppermute | solution.py:243
  18.3 9.6 %collective-permute-start.13 = (bf16[192,512]{1,0:T(8,128)(2,1)S(1)}, bf16[192,512]{1,0:T(8,128)(2,1)S(1)}, u32[]{:S(2)}, u32[]{:S(2)}) collective-permute-start(bf16[192,512]{1,0:T(8,128)(2,1)S(1)} %get-tuple-element.56), channel_id=1, source_target_pairs={{0,1},{1,0},{2,3},{3,2},{4,5},{5,4},{6,7},{7,6},{8,9},{9,8},{10,11... | collective-permute-start | bytes 589832 | tf_op jit(solution)/shard_map/ppermute | solution.py:243
  19.1 9.2 %collective-permute-start.14 = (bf16[192,512]{1,0:T(8,128)(2,1)S(1)}, bf16[192,512]{1,0:T(8,128)(2,1)S(1)}, u32[]{:S(2)}, u32[]{:S(2)}) collective-permute-start(bf16[192,512]{1,0:T(8,128)(2,1)S(1)} %get-tuple-element.57), channel_id=1, source_target_pairs={{0,2},{1,3},{2,0},{3,1},{4,6},{5,7},{6,4},{7,5},{8,10},{9,11},{10,... | collective-permute-start | bytes 589832 | tf_op jit(solution)/shard_map/ppermute | solution.py:243
  20.3 8.0 %collective-permute-start.15 = (bf16[192,512]{1,0:T(8,128)(2,1)S(1)}, bf16[192,512]{1,0:T(8,128)(2,1)S(1)}, u32[]{:S(2)}, u32[]{:S(2)}) collective-permute-start(bf16[192,512]{1,0:T(8,128)(2,1)S(1)} %get-tuple-element.58), channel_id=1, source_target_pairs={{0,3},{1,2},{2,1},{3,0},{4,7},{5,6},{6,5},{7,4},{8,11},{9,10},{10,... | collective-permute-start | bytes 589832 | tf_op jit(solution)/shard_map/ppermute | solution.py:243
  22.6 9.0 %collective-permute-start.6 = (bf16[384,256]{1,0:T(8,128)(2,1)S(1)}, bf16[384,256]{1,0:T(8,128)(2,1)S(1)}, u32[]{:S(2)}, u32[]{:S(2)}) collective-permute-start(bf16[384,256]{1,0:T(8,128)(2,1)S(1)} %get-tuple-element.45), channel_id=1, source_target_pairs={{0,4},{4,0},{8,12},{12,8},{16,20},{20,16},{24,28},{28,24},{1,5},{5... | collective-permute-start | bytes 589832 | tf_op jit(solution)/shard_map/ppermute | solution.py:243
  25.2 18.9 %collective-permute-start.21 = (bf16[256,768]{1,0:T(8,128)(2,1)S(1)}, bf16[256,768]{1,0:T(8,128)(2,1)S(1)}, u32[]{:S(2)}, u32[]{:S(2)}) collective-permute-start(bf16[256,768]{1,0:T(8,128)(2,1)S(1)} %get-tuple-element.59._), channel_id=1, source_target_pairs={{0,16},{4,20},{8,24},{12,28},{16,0},{20,4},{24,8},{28,12},{1,17},{... | collective-permute-start | bytes 1179656 | tf_op jit(solution)/shard_map/ppermute | solution.py:243
  28.8 16.1 %collective-permute-start.22 = (bf16[256,768]{1,0:T(8,128)(2,1)S(1)}, bf16[256,768]{1,0:T(8,128)(2,1)S(1)}, u32[]{:S(2)}, u32[]{:S(2)}) collective-permute-start(bf16[256,768]{1,0:T(8,128)(2,1)S(1)} %get-tuple-element.62._), channel_id=1, source_target_pairs={{0,8},{4,12},{8,0},{12,4},{16,24},{20,28},{24,16},{28,20},{1,9},{5... | collective-permute-start | bytes 1179656 | tf_op jit(solution)/shard_map/ppermute | solution.py:243
  30.5 1.4 %collective-permute-start.12 = (bf16[384,256]{1,0:T(8,128)(2,1)S(1)}, bf16[384,256]{1,0:T(8,128)(2,1)S(1)}, u32[]{:S(2)}, u32[]{:S(2)}) collective-permute-start(bf16[384,256]{1,0:T(8,128)(2,1)S(1)} %get-tuple-element.54), channel_id=1, source_target_pairs={{0,4},{4,0},{8,12},{12,8},{16,20},{20,16},{24,28},{28,24},{1,5},{5... | collective-permute-start | bytes 589832 | tf_op jit(solution)/shard_map/ppermute | solution.py:243
  30.5 1.7 %collective-permute-start.16 = (bf16[384,256]{1,0:T(8,128)(2,1)S(1)}, bf16[384,256]{1,0:T(8,128)(2,1)S(1)}, u32[]{:S(2)}, u32[]{:S(2)}) collective-permute-start(bf16[384,256]{1,0:T(8,128)(2,1)S(1)} %get-tuple-element.61), channel_id=1, source_target_pairs={{0,4},{4,0},{8,12},{12,8},{16,20},{20,16},{24,28},{28,24},{1,5},{5... | collective-permute-start | bytes 589832 | tf_op jit(solution)/shard_map/ppermute | solution.py:243
  31.5 12.6 %copy-start.3 = (s32[128,8]{0,1:T(8,128)S(1)}, s32[128,8]{0,1:T(8,128)}, u32[]{:S(2)}) copy-start(s32[128,8]{0,1:T(8,128)} %param.6) | copy-start | bytes 12292
  31.5 1.5 %collective-permute-start.17 = (bf16[384,256]{1,0:T(8,128)(2,1)S(1)}, bf16[384,256]{1,0:T(8,128)(2,1)S(1)}, u32[]{:S(2)}, u32[]{:S(2)}) collective-permute-start(bf16[384,256]{1,0:T(8,128)(2,1)S(1)} %get-tuple-element.64), channel_id=1, source_target_pairs={{0,4},{4,0},{8,12},{12,8},{16,20},{20,16},{24,28},{28,24},{1,5},{5... | collective-permute-start | bytes 589832 | tf_op jit(solution)/shard_map/ppermute | solution.py:243
  35.4 3.6 %collective-permute-start.18 = (f32[8,128]{1,0:T(8,128)S(1)}, f32[8,128]{1,0:T(8,128)S(1)}, u32[]{:S(2)}, u32[]{:S(2)}) collective-permute-start(f32[8,128]{1,0:T(8,128)S(1)} %get-tuple-element.67), channel_id=1, source_target_pairs={{0,1},{1,0},{2,3},{3,2},{4,5},{5,4},{6,7},{7,6},{8,9},{9,8},{10,11... | collective-permute-start | bytes 12296 | tf_op jit(solution)/shard_map/ppermute | solution.py:243
  37.0 3.6 %collective-permute-start.19 = (f32[8,128]{1,0:T(8,128)S(1)}, f32[8,128]{1,0:T(8,128)S(1)}, u32[]{:S(2)}, u32[]{:S(2)}) collective-permute-start(f32[8,128]{1,0:T(8,128)S(1)} %get-tuple-element.68), channel_id=1, source_target_pairs={{0,2},{1,3},{2,0},{3,1},{4,6},{5,7},{6,4},{7,5},{8,10},{9,11},{10,... | collective-permute-start | bytes 12296 | tf_op jit(solution)/shard_map/ppermute | solution.py:243
  37.7 4.5 %collective-permute-start.20 = (f32[8,128]{1,0:T(8,128)S(1)}, f32[8,128]{1,0:T(8,128)S(1)}, u32[]{:S(2)}, u32[]{:S(2)}) collective-permute-start(f32[8,128]{1,0:T(8,128)S(1)} %get-tuple-element.69), channel_id=1, source_target_pairs={{0,3},{1,2},{2,1},{3,0},{4,7},{5,6},{6,5},{7,4},{8,11},{9,10},{10,... | collective-permute-start | bytes 12296 | tf_op jit(solution)/shard_map/ppermute | solution.py:243
  (3 other events, 10.5 us)

commit v7 on v6

--- a/solution.py
+++ b/solution.py
@@ -278,7 +278,8 @@
         sent = [to_peer[r](pieces[r]) for r in range(peers)]
         return (sent, pieces[peers]) if take else sent
 
-    one, hidden = later((1,), hidden, take=True)
+    one = later((1,), matches)
+    hidden = call(copy_kernel, arr((slots, units), BF16))(hidden)
     stack = (2 * slots, block)
     mine = arr((slots, block), BF16)
     low, high, scaled, own0, cross0 = call(

time: 46.1 us -> 46.1 us (level)
  starting transfers between devices: 23.3 us -> 24.4 us
  local copies, waits for them, and re-layouts: 2.11 us -> 1.06 us
    ppermute x23, starting transfers between devices: 23.3 us -> 24.4 us  [over(): return lambda x: lax.ppermute(x, axis, pairs)]
    unnamed x8, local copies, waits for them, and re-layouts: 2.11 us -> 1.06 us
    pallas_call x10 -> x11, Pallas kernels: 6.68 us -> 6.71 us  [run(): pl.pallas_call(kernel, out_shape=outs, in_specs=specs or [VMEM] * len(arg...]
  transfers between devices with their start and end apart: 23 -> 23, of which waited for: 12 -> 13; matrix products, arithmetic and copies ran while one was open for 2% -> 2% of each run, Pallas kernels for 15% -> 15%
where the time goes in v7:
time: 46.1 us; the launch traced here: 45.9 us
  starting transfers between devices  24.4 us (53%)
  waiting for transfers between devices  11.2 us (24%)
  Pallas kernels  6.71 us (15%)
  other arithmetic  1.76 us (4%)
  local copies, waits for them, and re-layouts  1.06 us (2%)
  between operations  0.77 us (2%)
    ppermute x23, starting transfers between devices, over(): return lambda x: lax.ppermute(x, axis, pairs)  24.4 us
    ppermute x23, waiting for transfers between devices, over(): return lambda x: lax.ppermute(x, axis, pairs)  11.2 us
    pallas_call x11, Pallas kernels, run(): pl.pallas_call(kernel, out_shape=outs, in_specs=specs or [VMEM] * len(arg...  6.71 us
    unnamed x8, local copies, waits for them, and re-layouts  1.06 us
    broadcast_in_dim x1, other arithmetic, per_device(): return (grad_hidden[None], gate_grad.T, weight_grad[None])  0.96 us
  transfers between devices with their start and end apart: 23, of which 13 were waited for; matrix products, arithmetic and copies ran while one was open for 2% of the time, Pallas kernels for 15%

profile of v7, /device:TPU:0, one launch (start us, length us, event | category | flops | bytes accessed | tf_op | source)
XLA Modules:
  0.0 45.9 jit_solution(17419854957912041919)
XLA Ops:
  1.2 0.8 %fusion.marks_ref = bf16[16,128]{1,0:T(8,128)(2,1)S(1)} fusion(s32[8,128]{1,0:T(8,128)} %bitcast.11, s32[16]{0:T(128)S(1)} %iota_multiply_fusion, bf16[8,128]{1,0:T(8,128)(2,1)} %bitcast.13), kind=kLoop, calls=%fused_computation.2 | loop fusion | flops 47104 | bytes 10304 | tf_op jit(solution)/shard_map/reduce_max | solution.py:259
  2.5 1.0 %copy-done.2 = bf16[128,2048]{1,0:T(8,128)(2,1)S(1)} copy-done((bf16[128,2048]{1,0:T(8,128)(2,1)S(1)}, bf16[128,2048]{1,0:T(8,128)(2,1)}, u32[]{:S(2)}) %copy-start.2) | copy-done | bytes 524312
  4.2 2.8 %collective-permute-start.2 = (bf16[208,256]{1,0:T(8,128)(2,1)S(1)}, bf16[208,256]{1,0:T(8,128)(2,1)S(1)}, u32[]{:S(2)}, u32[]{:S(2)}) collective-permute-start(bf16[208,256]{1,0:T(8,128)(2,1)S(1)} %get-tuple-element.38), channel_id=1, source_target_pairs={{0,1},{1,0},{2,3},{3,2},{4,5},{5,4},{6,7},{7,6},{8,9},{9,8},{10,11... | collective-permute-start | bytes 319496 | tf_op jit(solution)/shard_map/ppermute | solution.py:243
  7.1 1.5 %collective-permute-start.3 = (bf16[208,256]{1,0:T(8,128)(2,1)S(1)}, bf16[208,256]{1,0:T(8,128)(2,1)S(1)}, u32[]{:S(2)}, u32[]{:S(2)}) collective-permute-start(bf16[208,256]{1,0:T(8,128)(2,1)S(1)} %get-tuple-element.39), channel_id=1, source_target_pairs={{0,2},{1,3},{2,0},{3,1},{4,6},{5,7},{6,4},{7,5},{8,10},{9,11},{10,... | collective-permute-start | bytes 319496 | tf_op jit(solution)/shard_map/ppermute | solution.py:243
  8.9 2.0 %collective-permute-start.7 = (bf16[192,256]{1,0:T(8,128)(2,1)S(1)}, bf16[192,256]{1,0:T(8,128)(2,1)S(1)}, u32[]{:S(2)}, u32[]{:S(2)}) collective-permute-start(bf16[192,256]{1,0:T(8,128)(2,1)S(1)} %get-tuple-element.45), channel_id=1, source_target_pairs={{0,1},{1,0},{2,3},{3,2},{4,5},{5,4},{6,7},{7,6},{8,9},{9,8},{10,11... | collective-permute-start | bytes 294920 | tf_op jit(solution)/shard_map/ppermute | solution.py:243
  10.9 1.5 %collective-permute-start.8 = (bf16[192,256]{1,0:T(8,128)(2,1)S(1)}, bf16[192,256]{1,0:T(8,128)(2,1)S(1)}, u32[]{:S(2)}, u32[]{:S(2)}) collective-permute-start(bf16[192,256]{1,0:T(8,128)(2,1)S(1)} %get-tuple-element.46), channel_id=1, source_target_pairs={{0,2},{1,3},{2,0},{3,1},{4,6},{5,7},{6,4},{7,5},{8,10},{9,11},{10,... | collective-permute-start | bytes 294920 | tf_op jit(solution)/shard_map/ppermute | solution.py:243
  12.4 1.4 %collective-permute-start.9 = (bf16[192,256]{1,0:T(8,128)(2,1)S(1)}, bf16[192,256]{1,0:T(8,128)(2,1)S(1)}, u32[]{:S(2)}, u32[]{:S(2)}) collective-permute-start(bf16[192,256]{1,0:T(8,128)(2,1)S(1)} %get-tuple-element.47), channel_id=1, source_target_pairs={{0,3},{1,2},{2,1},{3,0},{4,7},{5,6},{6,5},{7,4},{8,11},{9,10},{10,... | collective-permute-start | bytes 294920 | tf_op jit(solution)/shard_map/ppermute | solution.py:243
  14.3 1.1 %collective-permute-done.4.p3.refs_11_ = bf16[208,256]{1,0:T(8,128)(2,1)S(1)} collective-permute-done((bf16[208,256]{1,0:T(8,128)(2,1)S(1)}, bf16[208,256]{1,0:T(8,128)(2,1)S(1)}, u32[]{:S(2)}, u32[]{:S(2)}) %collective-permute-start.4) | collective-permute-done | bytes 106528 | tf_op jit(solution)/shard_map/ppermute | solution.py:243
  16.2 1.6 %collective-permute-start.10 = (bf16[128,768]{1,0:T(8,128)(2,1)S(1)}, bf16[128,768]{1,0:T(8,128)(2,1)S(1)}, u32[]{:S(2)}, u32[]{:S(2)}) collective-permute-start(bf16[128,768]{1,0:T(8,128)(2,1)S(1)} %get-tuple-element.49.outs_0_), channel_id=1, source_target_pairs={{0,8},{4,12},{8,0},{12,4},{16,24},{20,28},{24,16},{28,20},{1,9},{5... | collective-permute-start | bytes 589832 | tf_op jit(solution)/shard_map/ppermute | solution.py:243
  19.4 1.2 %collective-permute-start.14 = (bf16[192,512]{1,0:T(8,128)(2,1)S(1)}, bf16[192,512]{1,0:T(8,128)(2,1)S(1)}, u32[]{:S(2)}, u32[]{:S(2)}) collective-permute-start(bf16[192,512]{1,0:T(8,128)(2,1)S(1)} %get-tuple-element.55), channel_id=1, source_target_pairs={{0,2},{1,3},{2,0},{3,1},{4,6},{5,7},{6,4},{7,5},{8,10},{9,11},{10,... | collective-permute-start | bytes 589832 | tf_op jit(solution)/shard_map/ppermute | solution.py:243
  20.6 1.6 %collective-permute-start.15 = (bf16[192,512]{1,0:T(8,128)(2,1)S(1)}, bf16[192,512]{1,0:T(8,128)(2,1)S(1)}, u32[]{:S(2)}, u32[]{:S(2)}) collective-permute-start(bf16[192,512]{1,0:T(8,128)(2,1)S(1)} %get-tuple-element.56), channel_id=1, source_target_pairs={{0,3},{1,2},{2,1},{3,0},{4,7},{5,6},{6,5},{7,4},{8,11},{9,10},{10,... | collective-permute-start | bytes 589832 | tf_op jit(solution)/shard_map/ppermute | solution.py:243
  22.6 2.1 %collective-permute-done.11.high_ref = bf16[128,768]{1,0:T(8,128)(2,1)S(1)} collective-permute-done((bf16[128,768]{1,0:T(8,128)(2,1)S(1)}, bf16[128,768]{1,0:T(8,128)(2,1)S(1)}, u32[]{:S(2)}, u32[]{:S(2)}) %collective-permute-start.11) | collective-permute-done | bytes 196640 | tf_op jit(solution)/shard_map/ppermute | solution.py:243
  25.2 2.7 %collective-permute-start.21 = (bf16[256,768]{1,0:T(8,128)(2,1)S(1)}, bf16[256,768]{1,0:T(8,128)(2,1)S(1)}, u32[]{:S(2)}, u32[]{:S(2)}) collective-permute-start(bf16[256,768]{1,0:T(8,128)(2,1)S(1)} %get-tuple-element.57._), channel_id=1, source_target_pairs={{0,16},{4,20},{8,24},{12,28},{16,0},{20,4},{24,8},{28,12},{1,17},{... | collective-permute-start | bytes 1179656 | tf_op jit(solution)/shard_map/ppermute | solution.py:243
  27.9 1.0 %collective-permute-done.15.p3 = bf16[192,512]{1,0:T(8,128)(2,1)S(1)} collective-permute-done((bf16[192,512]{1,0:T(8,128)(2,1)S(1)}, bf16[192,512]{1,0:T(8,128)(2,1)S(1)}, u32[]{:S(2)}, u32[]{:S(2)}) %collective-permute-start.15) | collective-permute-done | bytes 196640 | tf_op jit(solution)/shard_map/ppermute | solution.py:243
  29.4 1.6 %collective-permute-start.22 = (bf16[256,768]{1,0:T(8,128)(2,1)S(1)}, bf16[256,768]{1,0:T(8,128)(2,1)S(1)}, u32[]{:S(2)}, u32[]{:S(2)}) collective-permute-start(bf16[256,768]{1,0:T(8,128)(2,1)S(1)} %get-tuple-element.60._), channel_id=1, source_target_pairs={{0,8},{4,12},{8,0},{12,4},{16,24},{20,28},{24,16},{28,20},{1,9},{5... | collective-permute-start | bytes 1179656 | tf_op jit(solution)/shard_map/ppermute | solution.py:243
  32.8 0.8 %collective-permute-done.17.refs_7_ = bf16[384,256]{1,0:T(8,128)(2,1)S(1)} collective-permute-done((bf16[384,256]{1,0:T(8,128)(2,1)S(1)}, bf16[384,256]{1,0:T(8,128)(2,1)S(1)}, u32[]{:S(2)}, u32[]{:S(2)}) %collective-permute-start.17) | collective-permute-done | bytes 196640 | tf_op jit(solution)/shard_map/ppermute | solution.py:243
  33.7 2.4 %shard_map.85 = (bf16[384,768]{1,0:T(8,128)(2,1)}, f32[8,128]{1,0:T(8,128)S(1)}, f32[8,128]{1,0:T(8,128)S(1)}, f32[8,128]{1,0:T(8,128)S(1)}, f32[8,128]{1,0:T(8,128)S(1)}) custom-call(bf16[384,256]{1,0:T(8,128)(2,1)S(1)} %get-tuple-element.41.refs_0_, bf16[384,256]{1,0:T(8,128)(2,1)S(1)} %collective-permute-done.6.refs_1_, ...), custom_call_target="tpu_custom_call" | custom-call | tf_op jit(solution)/shard_map/pallas_call | solution.py:224
  36.0 1.0 %collective-permute-start.18 = (f32[8,128]{1,0:T(8,128)S(1)}, f32[8,128]{1,0:T(8,128)S(1)}, u32[]{:S(2)}, u32[]{:S(2)}) collective-permute-start(f32[8,128]{1,0:T(8,128)S(1)} %get-tuple-element.65), channel_id=1, source_target_pairs={{0,1},{1,0},{2,3},{3,2},{4,5},{5,4},{6,7},{7,6},{8,9},{9,8},{10,11... | collective-permute-start | bytes 12296 | tf_op jit(solution)/shard_map/ppermute | solution.py:243
  37.0 1.0 %collective-permute-start.19 = (f32[8,128]{1,0:T(8,128)S(1)}, f32[8,128]{1,0:T(8,128)S(1)}, u32[]{:S(2)}, u32[]{:S(2)}) collective-permute-start(f32[8,128]{1,0:T(8,128)S(1)} %get-tuple-element.66), channel_id=1, source_target_pairs={{0,2},{1,3},{2,0},{3,1},{4,6},{5,7},{6,4},{7,5},{8,10},{9,11},{10,... | collective-permute-start | bytes 12296 | tf_op jit(solution)/shard_map/ppermute | solution.py:243
  38.0 1.5 %collective-permute-start.20 = (f32[8,128]{1,0:T(8,128)S(1)}, f32[8,128]{1,0:T(8,128)S(1)}, u32[]{:S(2)}, u32[]{:S(2)}) collective-permute-start(f32[8,128]{1,0:T(8,128)S(1)} %get-tuple-element.67), channel_id=1, source_target_pairs={{0,3},{1,2},{2,1},{3,0},{4,7},{5,6},{6,5},{7,4},{8,11},{9,10},{10,... | collective-permute-start | bytes 12296 | tf_op jit(solution)/shard_map/ppermute | solution.py:243
  39.6 1.0 %collective-permute-done.19.b2 = f32[8,128]{1,0:T(8,128)S(1)} collective-permute-done((f32[8,128]{1,0:T(8,128)S(1)}, f32[8,128]{1,0:T(8,128)S(1)}, u32[]{:S(2)}, u32[]{:S(2)}) %collective-permute-start.19) | collective-permute-done | bytes 4128 | tf_op jit(solution)/shard_map/ppermute | solution.py:243
  40.6 1.9 %collective-permute-done.20.b3 = f32[8,128]{1,0:T(8,128)S(1)} collective-permute-done((f32[8,128]{1,0:T(8,128)S(1)}, f32[8,128]{1,0:T(8,128)S(1)}, u32[]{:S(2)}, u32[]{:S(2)}) %collective-permute-start.20) | collective-permute-done | bytes 4128 | tf_op jit(solution)/shard_map/ppermute | solution.py:243
  42.5 1.6 %collective-permute-done.21.far_ref = bf16[256,768]{1,0:T(8,128)(2,1)S(1)} collective-permute-done((bf16[256,768]{1,0:T(8,128)(2,1)S(1)}, bf16[256,768]{1,0:T(8,128)(2,1)S(1)}, u32[]{:S(2)}, u32[]{:S(2)}) %collective-permute-start.21) | collective-permute-done | bytes 393248 | tf_op jit(solution)/shard_map/ppermute | solution.py:243
  44.9 1.0 %add_bitcast_fusion = f32[1,256,768]{2,1,0:T(8,128)} fusion(f32[256,768]{1,0:T(8,128)S(1)} %get-tuple-element.70, bf16[256,768]{1,0:T(8,128)(2,1)S(1)} %collective-permute-done.22), kind=kLoop, calls=%fused_computation | loop fusion | flops 393216 | bytes 1966080 | tf_op jit(solution)/shard_map/broadcast_in_dim | solution.py:321
  (44 shorter events, 8.8 us)
Async XLA Ops:
  0.6 13.2 %copy-start.1 = (bf16[1,384,768]{2,1,0:T(8,128)(2,1)S(1)}, bf16[1,384,768]{2,1,0:T(8,128)(2,1)}, u32[]{:S(2)}) copy-start(bf16[1,384,768]{2,1,0:T(8,128)(2,1)} %param.8) | copy-start | bytes 1769476
  0.6 3.0 %collective-permute-start = (bf16[128,2048]{1,0:T(8,128)(2,1)}, bf16[128,2048]{1,0:T(8,128)(2,1)S(1)}, u32[]{:S(2)}, u32[]{:S(2)}) collective-permute-start(bf16[128,2048]{1,0:T(8,128)(2,1)} %from_ref.1), channel_id=1, source_target_pairs={{0,4},{4,0},{8,12},{12,8},{16,20},{20,16},{24,28},{28,24},{1,5},{5... | collective-permute-start | bytes 1572872 | tf_op jit(solution)/shard_map/ppermute | solution.py:243
  1.2 9.7 %collective-permute-start.5 = (bf16[384,768]{1,0:T(8,128)(2,1)}, bf16[384,768]{1,0:T(8,128)(2,1)S(1)}, u32[]{:S(2)}, u32[]{:S(2)}) collective-permute-start(bf16[384,768]{1,0:T(8,128)(2,1)} %bitcast.9), channel_id=1, source_target_pairs={{0,4},{4,0},{8,12},{12,8},{16,20},{20,16},{24,28},{28,24},{1,5},{5... | collective-permute-start | bytes 1769480 | tf_op jit(solution)/shard_map/ppermute | solution.py:243
  2.0 1.6 %collective-permute-start.1 = (bf16[16,128]{1,0:T(8,128)(2,1)S(1)}, bf16[16,128]{1,0:T(8,128)(2,1)S(1)}, u32[]{:S(2)}, u32[]{:S(2)}) collective-permute-start(bf16[16,128]{1,0:T(8,128)(2,1)S(1)} %fusion.marks_ref), channel_id=1, source_target_pairs={{0,4},{4,0},{8,12},{12,8},{16,20},{20,16},{24,28},{28,24},{1,5},{5... | collective-permute-start | bytes 12296 | tf_op jit(solution)/shard_map/ppermute | solution.py:243
  4.2 8.2 %collective-permute-start.2 = (bf16[208,256]{1,0:T(8,128)(2,1)S(1)}, bf16[208,256]{1,0:T(8,128)(2,1)S(1)}, u32[]{:S(2)}, u32[]{:S(2)}) collective-permute-start(bf16[208,256]{1,0:T(8,128)(2,1)S(1)} %get-tuple-element.38), channel_id=1, source_target_pairs={{0,1},{1,0},{2,3},{3,2},{4,5},{5,4},{6,7},{7,6},{8,9},{9,8},{10,11... | collective-permute-start | bytes 319496 | tf_op jit(solution)/shard_map/ppermute | solution.py:243
  7.1 7.2 %collective-permute-start.3 = (bf16[208,256]{1,0:T(8,128)(2,1)S(1)}, bf16[208,256]{1,0:T(8,128)(2,1)S(1)}, u32[]{:S(2)}, u32[]{:S(2)}) collective-permute-start(bf16[208,256]{1,0:T(8,128)(2,1)S(1)} %get-tuple-element.39), channel_id=1, source_target_pairs={{0,2},{1,3},{2,0},{3,1},{4,6},{5,7},{6,4},{7,5},{8,10},{9,11},{10,... | collective-permute-start | bytes 319496 | tf_op jit(solution)/shard_map/ppermute | solution.py:243
  8.6 6.8 %collective-permute-start.4 = (bf16[208,256]{1,0:T(8,128)(2,1)S(1)}, bf16[208,256]{1,0:T(8,128)(2,1)S(1)}, u32[]{:S(2)}, u32[]{:S(2)}) collective-permute-start(bf16[208,256]{1,0:T(8,128)(2,1)S(1)} %get-tuple-element.40), channel_id=1, source_target_pairs={{0,3},{1,2},{2,1},{3,0},{4,7},{5,6},{6,5},{7,4},{8,11},{9,10},{10,... | collective-permute-start | bytes 319496 | tf_op jit(solution)/shard_map/ppermute | solution.py:243
  8.9 9.8 %collective-permute-start.7 = (bf16[192,256]{1,0:T(8,128)(2,1)S(1)}, bf16[192,256]{1,0:T(8,128)(2,1)S(1)}, u32[]{:S(2)}, u32[]{:S(2)}) collective-permute-start(bf16[192,256]{1,0:T(8,128)(2,1)S(1)} %get-tuple-element.45), channel_id=1, source_target_pairs={{0,1},{1,0},{2,3},{3,2},{4,5},{5,4},{6,7},{7,6},{8,9},{9,8},{10,11... | collective-permute-start | bytes 294920 | tf_op jit(solution)/shard_map/ppermute | solution.py:243
  10.9 8.5 %collective-permute-start.8 = (bf16[192,256]{1,0:T(8,128)(2,1)S(1)}, bf16[192,256]{1,0:T(8,128)(2,1)S(1)}, u32[]{:S(2)}, u32[]{:S(2)}) collective-permute-start(bf16[192,256]{1,0:T(8,128)(2,1)S(1)} %get-tuple-element.46), channel_id=1, source_target_pairs={{0,2},{1,3},{2,0},{3,1},{4,6},{5,7},{6,4},{7,5},{8,10},{9,11},{10,... | collective-permute-start | bytes 294920 | tf_op jit(solution)/shard_map/ppermute | solution.py:243
  12.4 8.2 %collective-permute-start.9 = (bf16[192,256]{1,0:T(8,128)(2,1)S(1)}, bf16[192,256]{1,0:T(8,128)(2,1)S(1)}, u32[]{:S(2)}, u32[]{:S(2)}) collective-permute-start(bf16[192,256]{1,0:T(8,128)(2,1)S(1)} %get-tuple-element.47), channel_id=1, source_target_pairs={{0,3},{1,2},{2,1},{3,0},{4,7},{5,6},{6,5},{7,4},{8,11},{9,10},{10,... | collective-permute-start | bytes 294920 | tf_op jit(solution)/shard_map/ppermute | solution.py:243
  16.2 6.4 %collective-permute-start.10 = (bf16[128,768]{1,0:T(8,128)(2,1)S(1)}, bf16[128,768]{1,0:T(8,128)(2,1)S(1)}, u32[]{:S(2)}, u32[]{:S(2)}) collective-permute-start(bf16[128,768]{1,0:T(8,128)(2,1)S(1)} %get-tuple-element.49.outs_0_), channel_id=1, source_target_pairs={{0,8},{4,12},{8,0},{12,4},{16,24},{20,28},{24,16},{28,20},{1,9},{5... | collective-permute-start | bytes 589832 | tf_op jit(solution)/shard_map/ppermute | solution.py:243
  17.8 6.8 %collective-permute-start.11 = (bf16[128,768]{1,0:T(8,128)(2,1)S(1)}, bf16[128,768]{1,0:T(8,128)(2,1)S(1)}, u32[]{:S(2)}, u32[]{:S(2)}) collective-permute-start(bf16[128,768]{1,0:T(8,128)(2,1)S(1)} %get-tuple-element.50), channel_id=1, source_target_pairs={{0,8},{4,12},{8,0},{12,4},{16,24},{20,28},{24,16},{28,20},{1,9},{5... | collective-permute-start | bytes 589832 | tf_op jit(solution)/shard_map/ppermute | solution.py:243
  18.7 9.2 %collective-permute-start.13 = (bf16[192,512]{1,0:T(8,128)(2,1)S(1)}, bf16[192,512]{1,0:T(8,128)(2,1)S(1)}, u32[]{:S(2)}, u32[]{:S(2)}) collective-permute-start(bf16[192,512]{1,0:T(8,128)(2,1)S(1)} %get-tuple-element.54), channel_id=1, source_target_pairs={{0,1},{1,0},{2,3},{3,2},{4,5},{5,4},{6,7},{7,6},{8,9},{9,8},{10,11... | collective-permute-start | bytes 589832 | tf_op jit(solution)/shard_map/ppermute | solution.py:243
  19.4 8.5 %collective-permute-start.14 = (bf16[192,512]{1,0:T(8,128)(2,1)S(1)}, bf16[192,512]{1,0:T(8,128)(2,1)S(1)}, u32[]{:S(2)}, u32[]{:S(2)}) collective-permute-start(bf16[192,512]{1,0:T(8,128)(2,1)S(1)} %get-tuple-element.55), channel_id=1, source_target_pairs={{0,2},{1,3},{2,0},{3,1},{4,6},{5,7},{6,4},{7,5},{8,10},{9,11},{10,... | collective-permute-start | bytes 589832 | tf_op jit(solution)/shard_map/ppermute | solution.py:243
  20.6 8.3 %collective-permute-start.15 = (bf16[192,512]{1,0:T(8,128)(2,1)S(1)}, bf16[192,512]{1,0:T(8,128)(2,1)S(1)}, u32[]{:S(2)}, u32[]{:S(2)}) collective-permute-start(bf16[192,512]{1,0:T(8,128)(2,1)S(1)} %get-tuple-element.56), channel_id=1, source_target_pairs={{0,3},{1,2},{2,1},{3,0},{4,7},{5,6},{6,5},{7,4},{8,11},{9,10},{10,... | collective-permute-start | bytes 589832 | tf_op jit(solution)/shard_map/ppermute | solution.py:243
  22.6 9.6 %collective-permute-start.6 = (bf16[384,256]{1,0:T(8,128)(2,1)S(1)}, bf16[384,256]{1,0:T(8,128)(2,1)S(1)}, u32[]{:S(2)}, u32[]{:S(2)}) collective-permute-start(bf16[384,256]{1,0:T(8,128)(2,1)S(1)} %get-tuple-element.42), channel_id=1, source_target_pairs={{0,4},{4,0},{8,12},{12,8},{16,20},{20,16},{24,28},{28,24},{1,5},{5... | collective-permute-start | bytes 589832 | tf_op jit(solution)/shard_map/ppermute | solution.py:243
  25.2 18.9 %collective-permute-start.21 = (bf16[256,768]{1,0:T(8,128)(2,1)S(1)}, bf16[256,768]{1,0:T(8,128)(2,1)S(1)}, u32[]{:S(2)}, u32[]{:S(2)}) collective-permute-start(bf16[256,768]{1,0:T(8,128)(2,1)S(1)} %get-tuple-element.57._), channel_id=1, source_target_pairs={{0,16},{4,20},{8,24},{12,28},{16,0},{20,4},{24,8},{28,12},{1,17},{... | collective-permute-start | bytes 1179656 | tf_op jit(solution)/shard_map/ppermute | solution.py:243
  29.4 15.5 %collective-permute-start.22 = (bf16[256,768]{1,0:T(8,128)(2,1)S(1)}, bf16[256,768]{1,0:T(8,128)(2,1)S(1)}, u32[]{:S(2)}, u32[]{:S(2)}) collective-permute-start(bf16[256,768]{1,0:T(8,128)(2,1)S(1)} %get-tuple-element.60._), channel_id=1, source_target_pairs={{0,8},{4,12},{8,0},{12,4},{16,24},{20,28},{24,16},{28,20},{1,9},{5... | collective-permute-start | bytes 1179656 | tf_op jit(solution)/shard_map/ppermute | solution.py:243
  31.1 1.4 %collective-permute-start.12 = (bf16[384,256]{1,0:T(8,128)(2,1)S(1)}, bf16[384,256]{1,0:T(8,128)(2,1)S(1)}, u32[]{:S(2)}, u32[]{:S(2)}) collective-permute-start(bf16[384,256]{1,0:T(8,128)(2,1)S(1)} %get-tuple-element.52), channel_id=1, source_target_pairs={{0,4},{4,0},{8,12},{12,8},{16,20},{20,16},{24,28},{28,24},{1,5},{5... | collective-permute-start | bytes 589832 | tf_op jit(solution)/shard_map/ppermute | solution.py:243
  31.1 1.7 %collective-permute-start.16 = (bf16[384,256]{1,0:T(8,128)(2,1)S(1)}, bf16[384,256]{1,0:T(8,128)(2,1)S(1)}, u32[]{:S(2)}, u32[]{:S(2)}) collective-permute-start(bf16[384,256]{1,0:T(8,128)(2,1)S(1)} %get-tuple-element.59), channel_id=1, source_target_pairs={{0,4},{4,0},{8,12},{12,8},{16,20},{20,16},{24,28},{28,24},{1,5},{5... | collective-permute-start | bytes 589832 | tf_op jit(solution)/shard_map/ppermute | solution.py:243
  32.1 1.5 %collective-permute-start.17 = (bf16[384,256]{1,0:T(8,128)(2,1)S(1)}, bf16[384,256]{1,0:T(8,128)(2,1)S(1)}, u32[]{:S(2)}, u32[]{:S(2)}) collective-permute-start(bf16[384,256]{1,0:T(8,128)(2,1)S(1)} %get-tuple-element.62), channel_id=1, source_target_pairs={{0,4},{4,0},{8,12},{12,8},{16,20},{20,16},{24,28},{28,24},{1,5},{5... | collective-permute-start | bytes 589832 | tf_op jit(solution)/shard_map/ppermute | solution.py:243
  36.0 3.6 %collective-permute-start.18 = (f32[8,128]{1,0:T(8,128)S(1)}, f32[8,128]{1,0:T(8,128)S(1)}, u32[]{:S(2)}, u32[]{:S(2)}) collective-permute-start(f32[8,128]{1,0:T(8,128)S(1)} %get-tuple-element.65), channel_id=1, source_target_pairs={{0,1},{1,0},{2,3},{3,2},{4,5},{5,4},{6,7},{7,6},{8,9},{9,8},{10,11... | collective-permute-start | bytes 12296 | tf_op jit(solution)/shard_map/ppermute | solution.py:243
  37.0 3.6 %collective-permute-start.19 = (f32[8,128]{1,0:T(8,128)S(1)}, f32[8,128]{1,0:T(8,128)S(1)}, u32[]{:S(2)}, u32[]{:S(2)}) collective-permute-start(f32[8,128]{1,0:T(8,128)S(1)} %get-tuple-element.66), channel_id=1, source_target_pairs={{0,2},{1,3},{2,0},{3,1},{4,6},{5,7},{6,4},{7,5},{8,10},{9,11},{10,... | collective-permute-start | bytes 12296 | tf_op jit(solution)/shard_map/ppermute | solution.py:243
  38.0 4.5 %collective-permute-start.20 = (f32[8,128]{1,0:T(8,128)S(1)}, f32[8,128]{1,0:T(8,128)S(1)}, u32[]{:S(2)}, u32[]{:S(2)}) collective-permute-start(f32[8,128]{1,0:T(8,128)S(1)} %get-tuple-element.67), channel_id=1, source_target_pairs={{0,3},{1,2},{2,1},{3,0},{4,7},{5,6},{6,5},{7,4},{8,11},{9,10},{10,... | collective-permute-start | bytes 12296 | tf_op jit(solution)/shard_map/ppermute | solution.py:243
  (3 other events, 22.0 us)

commit v8 on v7

--- a/solution.py
+++ b/solution.py
@@ -199,7 +199,7 @@
         pairs[r][...] = jnp.broadcast_to(line, (8, 128))
 
 
-def gate_kernel(ids_ref, matches_ref, b0, b1, b2, b3, part_ref, far_ref, out_ref, sum_ref):
+def gate_kernel(ids_ref, matches_ref, b0, b1, b2, b3, out_ref, done_ref):
     _, _, peer = coordinates()
     ids = ids_ref[...]
     total = jnp.zeros(ids.shape, F32)
@@ -211,7 +211,24 @@
         at_token = jnp.sum(jnp.where(match > 0.0, column, 0.0), axis=0, keepdims=True)
         total = jnp.where(ids == (peer ^ r) * EXP_DEV, at_token, total)
     out_ref[...] = total
+    done_ref[...] = total
+
+
+def far_kernel(part_ref, far_ref, _, sum_ref):
     sum_ref[...] = part_ref[...] + far_ref[...].astype(F32)
+
+
+def total_kernel(part_ref, near_ref, out_hbm, total_ref, sems):
+    size = total_ref.shape[0] // 4
+    copies = []
+    for i in range(4):
+        at = pl.ds(i * size, size)
+        total_ref[at, :] = part_ref[at, :] + near_ref[at, :].astype(F32)
+        copy = pltpu.make_async_copy(total_ref.at[at, :], out_hbm.at[at, :], sems.at[i])
+        copy.start()
+        copies.append(copy)
+    for copy in copies:
+        copy.wait()
 
 
 HBM = pl.BlockSpec(memory_space=pltpu.HBM)
@@ -219,13 +236,13 @@
 VMEM = pl.BlockSpec(memory_space=pltpu.VMEM)
 
 
-def call(kernel, outs, specs=None, scratch=(), cost=0, vmem=40 * 2**20):
+def call(kernel, outs, specs=None, scratch=(), cost=0, outs_at=None, vmem=40 * 2**20):
     def run(*args):
         return pl.pallas_call(
             kernel,
             out_shape=outs,
             in_specs=specs or [VMEM] * len(args),
-            out_specs=jax.tree.map(lambda _: VMEM, outs),
+            out_specs=outs_at or jax.tree.map(lambda _: VMEM, outs),
             scratch_shapes=list(scratch),
             compiler_params=pltpu.CompilerParams(vmem_limit_bytes=vmem),
             cost_estimate=pl.CostEstimate(flops=0, bytes_accessed=cost, transcendentals=0),
@@ -314,10 +331,16 @@
         [arr((slots, units), BF16)] + [arr((8, 128), F32)] * peers,
     )(*rows, *first, hidden, weight)
     back = [to_peer[r](pairs[r]) for r in range(peers)]
-    gate_grad, most = call(
-        gate_kernel, [arr((TOP, tokens), F32), arr((block, units), F32)], cost=4 * block * units
-    )(ids_t, matches, *back, part3, come1)
-    weight_grad = most + come2.astype(F32)
+    gate_grad, done = call(gate_kernel, [arr((TOP, tokens), F32)] * 2)(ids_t, matches, *back)
+    most = call(
+        far_kernel, arr((block, units), F32), specs=[VMEM] * 2 + [ANY], cost=4 * block * units
+    )(part3, come1, done)
+    weight_grad = call(
+        total_kernel,
+        arr((block, units), F32),
+        outs_at=HBM,
+        scratch=[pltpu.VMEM((block, units), F32), pltpu.SemaphoreType.DMA((4,))],
+    )(most, come2)
     return grad_hidden[None], gate_grad.T, weight_grad[None]
 
 

time: 46.1 us -> 46 us (level)
  Pallas kernels: 6.71 us -> 7.71 us
  other arithmetic: 1.76 us -> 0.8 us
    pallas_call x11 -> x13, Pallas kernels: 6.71 us -> 7.71 us  [run(): pl.pallas_call(kernel, out_shape=outs, in_specs=specs or [VMEM] * len(arg...]
    broadcast_in_dim x1 -> x0, other arithmetic: 0.96 us -> none  [per_device(): return (grad_hidden[None], gate_grad.T, weight_grad[None])]
where the time goes in v8:
time: 46 us; the launch traced here: 45.9 us
  starting transfers between devices  24.4 us (53%)
  waiting for transfers between devices  11.1 us (24%)
  Pallas kernels  7.71 us (17%)
  local copies, waits for them, and re-layouts  1.06 us (2%)
  other arithmetic  0.8 us (2%)
  between operations  0.78 us (2%)
    ppermute x23, starting transfers between devices, over(): return lambda x: lax.ppermute(x, axis, pairs)  24.4 us
    ppermute x23, waiting for transfers between devices, over(): return lambda x: lax.ppermute(x, axis, pairs)  11.1 us
    pallas_call x13, Pallas kernels, run(): pl.pallas_call(kernel, out_shape=outs, in_specs=specs or [VMEM] * len(arg...  7.71 us
    unnamed x8, local copies, waits for them, and re-layouts  1.06 us
  transfers between devices with their start and end apart: 23, of which 13 were waited for; matrix products, arithmetic and copies ran while one was open for 2% of the time, Pallas kernels for 15%

profile of v8, /device:TPU:0, one launch (start us, length us, event | category | flops | bytes accessed | tf_op | source)
XLA Modules:
  0.0 45.9 jit_solution(17528420815055518860)
XLA Ops:
  1.2 0.8 %fusion.marks_ref = bf16[16,128]{1,0:T(8,128)(2,1)S(1)} fusion(s32[8,128]{1,0:T(8,128)} %bitcast.10, s32[16]{0:T(128)S(1)} %iota_multiply_fusion, bf16[8,128]{1,0:T(8,128)(2,1)} %bitcast.13), kind=kLoop, calls=%fused_computation.1 | loop fusion | flops 47104 | bytes 10304 | tf_op jit(solution)/shard_map/reduce_max | solution.py:276
  2.5 1.0 %copy-done.2 = bf16[128,2048]{1,0:T(8,128)(2,1)S(1)} copy-done((bf16[128,2048]{1,0:T(8,128)(2,1)S(1)}, bf16[128,2048]{1,0:T(8,128)(2,1)}, u32[]{:S(2)}) %copy-start.2) | copy-done | bytes 524312
  4.2 2.8 %collective-permute-start.2 = (bf16[208,256]{1,0:T(8,128)(2,1)S(1)}, bf16[208,256]{1,0:T(8,128)(2,1)S(1)}, u32[]{:S(2)}, u32[]{:S(2)}) collective-permute-start(bf16[208,256]{1,0:T(8,128)(2,1)S(1)} %get-tuple-element.38), channel_id=1, source_target_pairs={{0,1},{1,0},{2,3},{3,2},{4,5},{5,4},{6,7},{7,6},{8,9},{9,8},{10,11... | collective-permute-start | bytes 319496 | tf_op jit(solution)/shard_map/ppermute | solution.py:260
  7.1 1.5 %collective-permute-start.3 = (bf16[208,256]{1,0:T(8,128)(2,1)S(1)}, bf16[208,256]{1,0:T(8,128)(2,1)S(1)}, u32[]{:S(2)}, u32[]{:S(2)}) collective-permute-start(bf16[208,256]{1,0:T(8,128)(2,1)S(1)} %get-tuple-element.39), channel_id=1, source_target_pairs={{0,2},{1,3},{2,0},{3,1},{4,6},{5,7},{6,4},{7,5},{8,10},{9,11},{10,... | collective-permute-start | bytes 319496 | tf_op jit(solution)/shard_map/ppermute | solution.py:260
  8.9 2.0 %collective-permute-start.7 = (bf16[192,256]{1,0:T(8,128)(2,1)S(1)}, bf16[192,256]{1,0:T(8,128)(2,1)S(1)}, u32[]{:S(2)}, u32[]{:S(2)}) collective-permute-start(bf16[192,256]{1,0:T(8,128)(2,1)S(1)} %get-tuple-element.45), channel_id=1, source_target_pairs={{0,1},{1,0},{2,3},{3,2},{4,5},{5,4},{6,7},{7,6},{8,9},{9,8},{10,11... | collective-permute-start | bytes 294920 | tf_op jit(solution)/shard_map/ppermute | solution.py:260
  10.9 1.5 %collective-permute-start.8 = (bf16[192,256]{1,0:T(8,128)(2,1)S(1)}, bf16[192,256]{1,0:T(8,128)(2,1)S(1)}, u32[]{:S(2)}, u32[]{:S(2)}) collective-permute-start(bf16[192,256]{1,0:T(8,128)(2,1)S(1)} %get-tuple-element.46), channel_id=1, source_target_pairs={{0,2},{1,3},{2,0},{3,1},{4,6},{5,7},{6,4},{7,5},{8,10},{9,11},{10,... | collective-permute-start | bytes 294920 | tf_op jit(solution)/shard_map/ppermute | solution.py:260
  12.4 1.4 %collective-permute-start.9 = (bf16[192,256]{1,0:T(8,128)(2,1)S(1)}, bf16[192,256]{1,0:T(8,128)(2,1)S(1)}, u32[]{:S(2)}, u32[]{:S(2)}) collective-permute-start(bf16[192,256]{1,0:T(8,128)(2,1)S(1)} %get-tuple-element.47), channel_id=1, source_target_pairs={{0,3},{1,2},{2,1},{3,0},{4,7},{5,6},{6,5},{7,4},{8,11},{9,10},{10,... | collective-permute-start | bytes 294920 | tf_op jit(solution)/shard_map/ppermute | solution.py:260
  14.3 1.1 %collective-permute-done.4.p3.refs_11_ = bf16[208,256]{1,0:T(8,128)(2,1)S(1)} collective-permute-done((bf16[208,256]{1,0:T(8,128)(2,1)S(1)}, bf16[208,256]{1,0:T(8,128)(2,1)S(1)}, u32[]{:S(2)}, u32[]{:S(2)}) %collective-permute-start.4) | collective-permute-done | bytes 106528 | tf_op jit(solution)/shard_map/ppermute | solution.py:260
  16.2 1.6 %collective-permute-start.10 = (bf16[128,768]{1,0:T(8,128)(2,1)S(1)}, bf16[128,768]{1,0:T(8,128)(2,1)S(1)}, u32[]{:S(2)}, u32[]{:S(2)}) collective-permute-start(bf16[128,768]{1,0:T(8,128)(2,1)S(1)} %get-tuple-element.49.outs_0_), channel_id=1, source_target_pairs={{0,8},{4,12},{8,0},{12,4},{16,24},{20,28},{24,16},{28,20},{1,9},{5... | collective-permute-start | bytes 589832 | tf_op jit(solution)/shard_map/ppermute | solution.py:260
  19.4 1.2 %collective-permute-start.14 = (bf16[192,512]{1,0:T(8,128)(2,1)S(1)}, bf16[192,512]{1,0:T(8,128)(2,1)S(1)}, u32[]{:S(2)}, u32[]{:S(2)}) collective-permute-start(bf16[192,512]{1,0:T(8,128)(2,1)S(1)} %get-tuple-element.55), channel_id=1, source_target_pairs={{0,2},{1,3},{2,0},{3,1},{4,6},{5,7},{6,4},{7,5},{8,10},{9,11},{10,... | collective-permute-start | bytes 589832 | tf_op jit(solution)/shard_map/ppermute | solution.py:260
  20.6 1.6 %collective-permute-start.15 = (bf16[192,512]{1,0:T(8,128)(2,1)S(1)}, bf16[192,512]{1,0:T(8,128)(2,1)S(1)}, u32[]{:S(2)}, u32[]{:S(2)}) collective-permute-start(bf16[192,512]{1,0:T(8,128)(2,1)S(1)} %get-tuple-element.56), channel_id=1, source_target_pairs={{0,3},{1,2},{2,1},{3,0},{4,7},{5,6},{6,5},{7,4},{8,11},{9,10},{10,... | collective-permute-start | bytes 589832 | tf_op jit(solution)/shard_map/ppermute | solution.py:260
  22.6 2.1 %collective-permute-done.11.high_ref = bf16[128,768]{1,0:T(8,128)(2,1)S(1)} collective-permute-done((bf16[128,768]{1,0:T(8,128)(2,1)S(1)}, bf16[128,768]{1,0:T(8,128)(2,1)S(1)}, u32[]{:S(2)}, u32[]{:S(2)}) %collective-permute-start.11) | collective-permute-done | bytes 196640 | tf_op jit(solution)/shard_map/ppermute | solution.py:260
  25.2 2.7 %collective-permute-start.21 = (bf16[256,768]{1,0:T(8,128)(2,1)S(1)}, bf16[256,768]{1,0:T(8,128)(2,1)S(1)}, u32[]{:S(2)}, u32[]{:S(2)}) collective-permute-start(bf16[256,768]{1,0:T(8,128)(2,1)S(1)} %get-tuple-element.57._), channel_id=1, source_target_pairs={{0,16},{4,20},{8,24},{12,28},{16,0},{20,4},{24,8},{28,12},{1,17},{... | collective-permute-start | bytes 1179656 | tf_op jit(solution)/shard_map/ppermute | solution.py:260
  27.9 1.0 %collective-permute-done.15.p3 = bf16[192,512]{1,0:T(8,128)(2,1)S(1)} collective-permute-done((bf16[192,512]{1,0:T(8,128)(2,1)S(1)}, bf16[192,512]{1,0:T(8,128)(2,1)S(1)}, u32[]{:S(2)}, u32[]{:S(2)}) %collective-permute-start.15) | collective-permute-done | bytes 196640 | tf_op jit(solution)/shard_map/ppermute | solution.py:260
  29.4 1.6 %collective-permute-start.22 = (bf16[256,768]{1,0:T(8,128)(2,1)S(1)}, bf16[256,768]{1,0:T(8,128)(2,1)S(1)}, u32[]{:S(2)}, u32[]{:S(2)}) collective-permute-start(bf16[256,768]{1,0:T(8,128)(2,1)S(1)} %get-tuple-element.60._), channel_id=1, source_target_pairs={{0,8},{4,12},{8,0},{12,4},{16,24},{20,28},{24,16},{28,20},{1,9},{5... | collective-permute-start | bytes 1179656 | tf_op jit(solution)/shard_map/ppermute | solution.py:260
  32.8 0.8 %collective-permute-done.17.refs_7_ = bf16[384,256]{1,0:T(8,128)(2,1)S(1)} collective-permute-done((bf16[384,256]{1,0:T(8,128)(2,1)S(1)}, bf16[384,256]{1,0:T(8,128)(2,1)S(1)}, u32[]{:S(2)}, u32[]{:S(2)}) %collective-permute-start.17) | collective-permute-done | bytes 196640 | tf_op jit(solution)/shard_map/ppermute | solution.py:260
  33.7 2.4 %shard_map.85 = (bf16[384,768]{1,0:T(8,128)(2,1)}, f32[8,128]{1,0:T(8,128)S(1)}, f32[8,128]{1,0:T(8,128)S(1)}, f32[8,128]{1,0:T(8,128)S(1)}, f32[8,128]{1,0:T(8,128)S(1)}) custom-call(bf16[384,256]{1,0:T(8,128)(2,1)S(1)} %get-tuple-element.41.refs_0_, bf16[384,256]{1,0:T(8,128)(2,1)S(1)} %collective-permute-done.6.refs_1_, ...), custom_call_target="tpu_custom_call" | custom-call | tf_op jit(solution)/shard_map/pallas_call | solution.py:241
  36.0 1.0 %collective-permute-start.18 = (f32[8,128]{1,0:T(8,128)S(1)}, f32[8,128]{1,0:T(8,128)S(1)}, u32[]{:S(2)}, u32[]{:S(2)}) collective-permute-start(f32[8,128]{1,0:T(8,128)S(1)} %get-tuple-element.65), channel_id=1, source_target_pairs={{0,1},{1,0},{2,3},{3,2},{4,5},{5,4},{6,7},{7,6},{8,9},{9,8},{10,11... | collective-permute-start | bytes 12296 | tf_op jit(solution)/shard_map/ppermute | solution.py:260
  37.0 1.0 %collective-permute-start.19 = (f32[8,128]{1,0:T(8,128)S(1)}, f32[8,128]{1,0:T(8,128)S(1)}, u32[]{:S(2)}, u32[]{:S(2)}) collective-permute-start(f32[8,128]{1,0:T(8,128)S(1)} %get-tuple-element.66), channel_id=1, source_target_pairs={{0,2},{1,3},{2,0},{3,1},{4,6},{5,7},{6,4},{7,5},{8,10},{9,11},{10,... | collective-permute-start | bytes 12296 | tf_op jit(solution)/shard_map/ppermute | solution.py:260
  38.0 1.5 %collective-permute-start.20 = (f32[8,128]{1,0:T(8,128)S(1)}, f32[8,128]{1,0:T(8,128)S(1)}, u32[]{:S(2)}, u32[]{:S(2)}) collective-permute-start(f32[8,128]{1,0:T(8,128)S(1)} %get-tuple-element.67), channel_id=1, source_target_pairs={{0,3},{1,2},{2,1},{3,0},{4,7},{5,6},{6,5},{7,4},{8,11},{9,10},{10,... | collective-permute-start | bytes 12296 | tf_op jit(solution)/shard_map/ppermute | solution.py:260
  39.6 1.0 %collective-permute-done.19.b2 = f32[8,128]{1,0:T(8,128)S(1)} collective-permute-done((f32[8,128]{1,0:T(8,128)S(1)}, f32[8,128]{1,0:T(8,128)S(1)}, u32[]{:S(2)}, u32[]{:S(2)}) %collective-permute-start.19) | collective-permute-done | bytes 4128 | tf_op jit(solution)/shard_map/ppermute | solution.py:260
  40.6 1.9 %collective-permute-done.20.b3 = f32[8,128]{1,0:T(8,128)S(1)} collective-permute-done((f32[8,128]{1,0:T(8,128)S(1)}, f32[8,128]{1,0:T(8,128)S(1)}, u32[]{:S(2)}, u32[]{:S(2)}) %collective-permute-start.20) | collective-permute-done | bytes 4128 | tf_op jit(solution)/shard_map/ppermute | solution.py:260
  43.2 0.9 %collective-permute-done.21.far_ref = bf16[256,768]{1,0:T(8,128)(2,1)S(1)} collective-permute-done((bf16[256,768]{1,0:T(8,128)(2,1)S(1)}, bf16[256,768]{1,0:T(8,128)(2,1)S(1)}, u32[]{:S(2)}, u32[]{:S(2)}) %collective-permute-start.21) | collective-permute-done | bytes 393248 | tf_op jit(solution)/shard_map/ppermute | solution.py:260
  44.9 0.9 %shard_map.88 = f32[256,768]{1,0:T(8,128)} custom-call(f32[256,768]{1,0:T(8,128)S(1)} %shard_map.87.part_ref, bf16[256,768]{1,0:T(8,128)(2,1)S(1)} %collective-permute-done.22.near_ref), custom_call_target="tpu_custom_call" | custom-call | tf_op jit(solution)/shard_map/pallas_call | solution.py:241
  (45 shorter events, 9.6 us)
Async XLA Ops:
  0.6 13.2 %copy-start.1 = (bf16[1,384,768]{2,1,0:T(8,128)(2,1)S(1)}, bf16[1,384,768]{2,1,0:T(8,128)(2,1)}, u32[]{:S(2)}) copy-start(bf16[1,384,768]{2,1,0:T(8,128)(2,1)} %param.8) | copy-start | bytes 1769476
  0.6 3.0 %collective-permute-start = (bf16[128,2048]{1,0:T(8,128)(2,1)}, bf16[128,2048]{1,0:T(8,128)(2,1)S(1)}, u32[]{:S(2)}, u32[]{:S(2)}) collective-permute-start(bf16[128,2048]{1,0:T(8,128)(2,1)} %from_ref.1), channel_id=1, source_target_pairs={{0,4},{4,0},{8,12},{12,8},{16,20},{20,16},{24,28},{28,24},{1,5},{5... | collective-permute-start | bytes 1572872 | tf_op jit(solution)/shard_map/ppermute | solution.py:260
  1.2 9.7 %collective-permute-start.5 = (bf16[384,768]{1,0:T(8,128)(2,1)}, bf16[384,768]{1,0:T(8,128)(2,1)S(1)}, u32[]{:S(2)}, u32[]{:S(2)}) collective-permute-start(bf16[384,768]{1,0:T(8,128)(2,1)} %bitcast.8), channel_id=1, source_target_pairs={{0,4},{4,0},{8,12},{12,8},{16,20},{20,16},{24,28},{28,24},{1,5},{5... | collective-permute-start | bytes 1769480 | tf_op jit(solution)/shard_map/ppermute | solution.py:260
  2.0 1.6 %collective-permute-start.1 = (bf16[16,128]{1,0:T(8,128)(2,1)S(1)}, bf16[16,128]{1,0:T(8,128)(2,1)S(1)}, u32[]{:S(2)}, u32[]{:S(2)}) collective-permute-start(bf16[16,128]{1,0:T(8,128)(2,1)S(1)} %fusion.marks_ref), channel_id=1, source_target_pairs={{0,4},{4,0},{8,12},{12,8},{16,20},{20,16},{24,28},{28,24},{1,5},{5... | collective-permute-start | bytes 12296 | tf_op jit(solution)/shard_map/ppermute | solution.py:260
  4.2 8.2 %collective-permute-start.2 = (bf16[208,256]{1,0:T(8,128)(2,1)S(1)}, bf16[208,256]{1,0:T(8,128)(2,1)S(1)}, u32[]{:S(2)}, u32[]{:S(2)}) collective-permute-start(bf16[208,256]{1,0:T(8,128)(2,1)S(1)} %get-tuple-element.38), channel_id=1, source_target_pairs={{0,1},{1,0},{2,3},{3,2},{4,5},{5,4},{6,7},{7,6},{8,9},{9,8},{10,11... | collective-permute-start | bytes 319496 | tf_op jit(solution)/shard_map/ppermute | solution.py:260
  7.1 7.2 %collective-permute-start.3 = (bf16[208,256]{1,0:T(8,128)(2,1)S(1)}, bf16[208,256]{1,0:T(8,128)(2,1)S(1)}, u32[]{:S(2)}, u32[]{:S(2)}) collective-permute-start(bf16[208,256]{1,0:T(8,128)(2,1)S(1)} %get-tuple-element.39), channel_id=1, source_target_pairs={{0,2},{1,3},{2,0},{3,1},{4,6},{5,7},{6,4},{7,5},{8,10},{9,11},{10,... | collective-permute-start | bytes 319496 | tf_op jit(solution)/shard_map/ppermute | solution.py:260
  8.6 6.8 %collective-permute-start.4 = (bf16[208,256]{1,0:T(8,128)(2,1)S(1)}, bf16[208,256]{1,0:T(8,128)(2,1)S(1)}, u32[]{:S(2)}, u32[]{:S(2)}) collective-permute-start(bf16[208,256]{1,0:T(8,128)(2,1)S(1)} %get-tuple-element.40), channel_id=1, source_target_pairs={{0,3},{1,2},{2,1},{3,0},{4,7},{5,6},{6,5},{7,4},{8,11},{9,10},{10,... | collective-permute-start | bytes 319496 | tf_op jit(solution)/shard_map/ppermute | solution.py:260
  8.9 9.8 %collective-permute-start.7 = (bf16[192,256]{1,0:T(8,128)(2,1)S(1)}, bf16[192,256]{1,0:T(8,128)(2,1)S(1)}, u32[]{:S(2)}, u32[]{:S(2)}) collective-permute-start(bf16[192,256]{1,0:T(8,128)(2,1)S(1)} %get-tuple-element.45), channel_id=1, source_target_pairs={{0,1},{1,0},{2,3},{3,2},{4,5},{5,4},{6,7},{7,6},{8,9},{9,8},{10,11... | collective-permute-start | bytes 294920 | tf_op jit(solution)/shard_map/ppermute | solution.py:260
  10.9 8.5 %collective-permute-start.8 = (bf16[192,256]{1,0:T(8,128)(2,1)S(1)}, bf16[192,256]{1,0:T(8,128)(2,1)S(1)}, u32[]{:S(2)}, u32[]{:S(2)}) collective-permute-start(bf16[192,256]{1,0:T(8,128)(2,1)S(1)} %get-tuple-element.46), channel_id=1, source_target_pairs={{0,2},{1,3},{2,0},{3,1},{4,6},{5,7},{6,4},{7,5},{8,10},{9,11},{10,... | collective-permute-start | bytes 294920 | tf_op jit(solution)/shard_map/ppermute | solution.py:260
  12.4 8.2 %collective-permute-start.9 = (bf16[192,256]{1,0:T(8,128)(2,1)S(1)}, bf16[192,256]{1,0:T(8,128)(2,1)S(1)}, u32[]{:S(2)}, u32[]{:S(2)}) collective-permute-start(bf16[192,256]{1,0:T(8,128)(2,1)S(1)} %get-tuple-element.47), channel_id=1, source_target_pairs={{0,3},{1,2},{2,1},{3,0},{4,7},{5,6},{6,5},{7,4},{8,11},{9,10},{10,... | collective-permute-start | bytes 294920 | tf_op jit(solution)/shard_map/ppermute | solution.py:260
  16.2 6.4 %collective-permute-start.10 = (bf16[128,768]{1,0:T(8,128)(2,1)S(1)}, bf16[128,768]{1,0:T(8,128)(2,1)S(1)}, u32[]{:S(2)}, u32[]{:S(2)}) collective-permute-start(bf16[128,768]{1,0:T(8,128)(2,1)S(1)} %get-tuple-element.49.outs_0_), channel_id=1, source_target_pairs={{0,8},{4,12},{8,0},{12,4},{16,24},{20,28},{24,16},{28,20},{1,9},{5... | collective-permute-start | bytes 589832 | tf_op jit(solution)/shard_map/ppermute | solution.py:260
  17.8 6.8 %collective-permute-start.11 = (bf16[128,768]{1,0:T(8,128)(2,1)S(1)}, bf16[128,768]{1,0:T(8,128)(2,1)S(1)}, u32[]{:S(2)}, u32[]{:S(2)}) collective-permute-start(bf16[128,768]{1,0:T(8,128)(2,1)S(1)} %get-tuple-element.50), channel_id=1, source_target_pairs={{0,8},{4,12},{8,0},{12,4},{16,24},{20,28},{24,16},{28,20},{1,9},{5... | collective-permute-start | bytes 589832 | tf_op jit(solution)/shard_map/ppermute | solution.py:260
  18.7 9.2 %collective-permute-start.13 = (bf16[192,512]{1,0:T(8,128)(2,1)S(1)}, bf16[192,512]{1,0:T(8,128)(2,1)S(1)}, u32[]{:S(2)}, u32[]{:S(2)}) collective-permute-start(bf16[192,512]{1,0:T(8,128)(2,1)S(1)} %get-tuple-element.54), channel_id=1, source_target_pairs={{0,1},{1,0},{2,3},{3,2},{4,5},{5,4},{6,7},{7,6},{8,9},{9,8},{10,11... | collective-permute-start | bytes 589832 | tf_op jit(solution)/shard_map/ppermute | solution.py:260
  19.4 8.5 %collective-permute-start.14 = (bf16[192,512]{1,0:T(8,128)(2,1)S(1)}, bf16[192,512]{1,0:T(8,128)(2,1)S(1)}, u32[]{:S(2)}, u32[]{:S(2)}) collective-permute-start(bf16[192,512]{1,0:T(8,128)(2,1)S(1)} %get-tuple-element.55), channel_id=1, source_target_pairs={{0,2},{1,3},{2,0},{3,1},{4,6},{5,7},{6,4},{7,5},{8,10},{9,11},{10,... | collective-permute-start | bytes 589832 | tf_op jit(solution)/shard_map/ppermute | solution.py:260
  20.6 8.3 %collective-permute-start.15 = (bf16[192,512]{1,0:T(8,128)(2,1)S(1)}, bf16[192,512]{1,0:T(8,128)(2,1)S(1)}, u32[]{:S(2)}, u32[]{:S(2)}) collective-permute-start(bf16[192,512]{1,0:T(8,128)(2,1)S(1)} %get-tuple-element.56), channel_id=1, source_target_pairs={{0,3},{1,2},{2,1},{3,0},{4,7},{5,6},{6,5},{7,4},{8,11},{9,10},{10,... | collective-permute-start | bytes 589832 | tf_op jit(solution)/shard_map/ppermute | solution.py:260
  22.6 9.6 %collective-permute-start.6 = (bf16[384,256]{1,0:T(8,128)(2,1)S(1)}, bf16[384,256]{1,0:T(8,128)(2,1)S(1)}, u32[]{:S(2)}, u32[]{:S(2)}) collective-permute-start(bf16[384,256]{1,0:T(8,128)(2,1)S(1)} %get-tuple-element.42), channel_id=1, source_target_pairs={{0,4},{4,0},{8,12},{12,8},{16,20},{20,16},{24,28},{28,24},{1,5},{5... | collective-permute-start | bytes 589832 | tf_op jit(solution)/shard_map/ppermute | solution.py:260
  25.2 18.9 %collective-permute-start.21 = (bf16[256,768]{1,0:T(8,128)(2,1)S(1)}, bf16[256,768]{1,0:T(8,128)(2,1)S(1)}, u32[]{:S(2)}, u32[]{:S(2)}) collective-permute-start(bf16[256,768]{1,0:T(8,128)(2,1)S(1)} %get-tuple-element.57._), channel_id=1, source_target_pairs={{0,16},{4,20},{8,24},{12,28},{16,0},{20,4},{24,8},{28,12},{1,17},{... | collective-permute-start | bytes 1179656 | tf_op jit(solution)/shard_map/ppermute | solution.py:260
  29.4 15.5 %collective-permute-start.22 = (bf16[256,768]{1,0:T(8,128)(2,1)S(1)}, bf16[256,768]{1,0:T(8,128)(2,1)S(1)}, u32[]{:S(2)}, u32[]{:S(2)}) collective-permute-start(bf16[256,768]{1,0:T(8,128)(2,1)S(1)} %get-tuple-element.60._), channel_id=1, source_target_pairs={{0,8},{4,12},{8,0},{12,4},{16,24},{20,28},{24,16},{28,20},{1,9},{5... | collective-permute-start | bytes 1179656 | tf_op jit(solution)/shard_map/ppermute | solution.py:260
  31.1 1.4 %collective-permute-start.12 = (bf16[384,256]{1,0:T(8,128)(2,1)S(1)}, bf16[384,256]{1,0:T(8,128)(2,1)S(1)}, u32[]{:S(2)}, u32[]{:S(2)}) collective-permute-start(bf16[384,256]{1,0:T(8,128)(2,1)S(1)} %get-tuple-element.52), channel_id=1, source_target_pairs={{0,4},{4,0},{8,12},{12,8},{16,20},{20,16},{24,28},{28,24},{1,5},{5... | collective-permute-start | bytes 589832 | tf_op jit(solution)/shard_map/ppermute | solution.py:260
  31.1 1.7 %collective-permute-start.16 = (bf16[384,256]{1,0:T(8,128)(2,1)S(1)}, bf16[384,256]{1,0:T(8,128)(2,1)S(1)}, u32[]{:S(2)}, u32[]{:S(2)}) collective-permute-start(bf16[384,256]{1,0:T(8,128)(2,1)S(1)} %get-tuple-element.59), channel_id=1, source_target_pairs={{0,4},{4,0},{8,12},{12,8},{16,20},{20,16},{24,28},{28,24},{1,5},{5... | collective-permute-start | bytes 589832 | tf_op jit(solution)/shard_map/ppermute | solution.py:260
  32.1 1.5 %collective-permute-start.17 = (bf16[384,256]{1,0:T(8,128)(2,1)S(1)}, bf16[384,256]{1,0:T(8,128)(2,1)S(1)}, u32[]{:S(2)}, u32[]{:S(2)}) collective-permute-start(bf16[384,256]{1,0:T(8,128)(2,1)S(1)} %get-tuple-element.62), channel_id=1, source_target_pairs={{0,4},{4,0},{8,12},{12,8},{16,20},{20,16},{24,28},{28,24},{1,5},{5... | collective-permute-start | bytes 589832 | tf_op jit(solution)/shard_map/ppermute | solution.py:260
  36.0 3.6 %collective-permute-start.18 = (f32[8,128]{1,0:T(8,128)S(1)}, f32[8,128]{1,0:T(8,128)S(1)}, u32[]{:S(2)}, u32[]{:S(2)}) collective-permute-start(f32[8,128]{1,0:T(8,128)S(1)} %get-tuple-element.65), channel_id=1, source_target_pairs={{0,1},{1,0},{2,3},{3,2},{4,5},{5,4},{6,7},{7,6},{8,9},{9,8},{10,11... | collective-permute-start | bytes 12296 | tf_op jit(solution)/shard_map/ppermute | solution.py:260
  37.0 3.6 %collective-permute-start.19 = (f32[8,128]{1,0:T(8,128)S(1)}, f32[8,128]{1,0:T(8,128)S(1)}, u32[]{:S(2)}, u32[]{:S(2)}) collective-permute-start(f32[8,128]{1,0:T(8,128)S(1)} %get-tuple-element.66), channel_id=1, source_target_pairs={{0,2},{1,3},{2,0},{3,1},{4,6},{5,7},{6,4},{7,5},{8,10},{9,11},{10,... | collective-permute-start | bytes 12296 | tf_op jit(solution)/shard_map/ppermute | solution.py:260
  38.0 4.5 %collective-permute-start.20 = (f32[8,128]{1,0:T(8,128)S(1)}, f32[8,128]{1,0:T(8,128)S(1)}, u32[]{:S(2)}, u32[]{:S(2)}) collective-permute-start(f32[8,128]{1,0:T(8,128)S(1)} %get-tuple-element.67), channel_id=1, source_target_pairs={{0,3},{1,2},{2,1},{3,0},{4,7},{5,6},{6,5},{7,4},{8,11},{9,10},{10,... | collective-permute-start | bytes 12296 | tf_op jit(solution)/shard_map/ppermute | solution.py:260
  (3 other events, 20.4 us)
